TPU v7x, 32 devices: a whole 2x2x4 slice. The times are simulated.
32 devices in a mesh: req: 8 (over y, x, core), wgt: 4 (over z).
Axes of the slice: x: 2, y: 2, z: 4, core: 2. Of those that a mesh axis runs over, the one named last changes fastest.
Arguments:
- arrivals: bfloat16 [32, 48, 6144], P('req', None, 'wgt'), may hold values from -6 to 6
- group_of: int32 [32], replicated, may hold values from 0 to 7, as said below
- lengths: int32 [32], P('req'), may hold values from 1 to 2048, as said below
- page_table: int32 [32, 16], P('req'), may hold values from 0 to 39, as said below
- ln_gain: bfloat16 [6144], replicated, may hold values from 0.25 to 1.75
- ln_bias: bfloat16 [6144], replicated, may hold values from -1.5 to 1.5
- w_qkv: bfloat16 [6144, 9216], P('req', 'wgt'), may hold values from -0.078125 to 0.078125
- qkv_bias: bfloat16 [9216], P('wgt'), may hold values from -4.5 to 4.5
- key_pool: bfloat16 [320, 128, 3072], P('req', None, 'wgt'), may hold values from -8 to 8
- value_pool: bfloat16 [320, 128, 3072], P('req', None, 'wgt'), may hold values from -6 to 6
Outputs:
- attended: bfloat16 [32, 48, 3072], P('req', None, 'wgt')
- new_keys: bfloat16 [32, 48, 3072], P('req', None, 'wgt')
- new_values: bfloat16 [32, 48, 3072], P('req', None, 'wgt')
Inputs may be any that keep to these rules, and one draw needn't show every extreme that they name: `group_of`: every group number is named by exactly 4 requests; the requests that arrive at one group (consecutive blocks of 4 in arrival order) name different groups. `lengths`: in each group at most one request has more than 1024 cached tokens; some request has exactly 2048. `page_table`: entries name pages of the request's group's own pool of 40; the pages that hold cached tokens of one group's requests are all different.
All inputs are finite; a program needn't handle non-finite values.
Results may differ from a plain program's by a relative error of at most 0.0066.
Values may be sent and summed in bfloat16 or wider, within the bound.
No kernel may reach another device: no remote copies, remote signals or barrier semaphores. Data moves between devices by JAX's collectives and lax.ppermute only.
A program may use at most 128 MiB of HBM per device.

v0:
```python
import math

import jax
import jax.numpy as jnp
from jax import lax
from jax.sharding import PartitionSpec as P

HEAD = 96
ROT = 24


EPS = 1e-05


def rotary(block, positions):
    half_rot = ROT // 2
    inverse = jnp.power(10000.0, -jnp.arange(half_rot, dtype=jnp.float32) * 2.0 / ROT)
    angles = positions[:, :, None] * inverse[None, None, :]
    cosine = jnp.cos(angles)[:, :, None, :]
    sine = jnp.sin(angles)[:, :, None, :]
    first = block[..., :half_rot]
    second = block[..., half_rot:ROT]
    return jnp.concatenate(
        [first * cosine - second * sine, second * cosine + first * sine, block[..., ROT:]], axis=-1
    )


def per_device(
    arrivals, group_of, lengths, page_table, ln_gain, ln_bias, w_qkv, qkv_bias, key_pool, value_pool
):
    req_count = lengths.shape[0]
    fresh_len = arrivals.shape[1]
    model_width = ln_gain.shape[0]
    local_cols = w_qkv.shape[1]
    local_heads = local_cols // (3 * HEAD)
    everyone = group_of.shape[0]
    my_group = lax.axis_index("req")
    same_group = group_of[:, None] == group_of[None, :]
    earlier = jnp.arange(everyone)[None, :] < jnp.arange(everyone)[:, None]
    rank_in = jnp.sum((same_group & earlier).astype(jnp.int32), axis=1)
    wanted = (group_of[None, :] == my_group) & (rank_in[None, :] == jnp.arange(req_count)[:, None])
    chooser = wanted.astype(jnp.bfloat16)
    all_lengths = lax.all_gather(lengths, "req", axis=0, tiled=True)
    arrival_ids = my_group * req_count + jnp.arange(req_count, dtype=jnp.int32)
    assigned = group_of[arrival_ids] * req_count + rank_in[arrival_ids]
    gathered = lax.all_gather(arrivals, "wgt", axis=2, tiled=True)
    widened = gathered.astype(jnp.float32)
    center = jnp.mean(widened, axis=-1, keepdims=True)
    spread = jnp.mean(jnp.square(widened - center), axis=-1, keepdims=True)
    normed = (widened - center) * lax.rsqrt(spread + EPS) * ln_gain.astype(
        jnp.float32
    ) + ln_bias.astype(jnp.float32)
    project_normed = normed.astype(jnp.bfloat16).reshape(req_count * fresh_len, model_width)
    summed = jnp.dot(
        project_normed,
        lax.all_gather(w_qkv, "req", axis=0, tiled=True),
        preferred_element_type=jnp.float32,
    )
    summed = summed + qkv_bias.astype(jnp.float32)
    projected = summed.reshape(req_count, fresh_len, local_heads, 3, HEAD)
    positions = (
        all_lengths[assigned][:, None] + jnp.arange(fresh_len, dtype=jnp.int32)[None, :]
    ).astype(jnp.float32)
    queries = rotary(projected[:, :, :, 0], positions)
    turned = rotary(projected[:, :, :, 1], positions)
    stacked = jnp.stack([queries, turned, projected[:, :, :, 2]], axis=3)
    local_packed = stacked.astype(jnp.bfloat16).reshape(req_count, fresh_len, local_cols)
    packed = jnp.einsum(
        "jr,rcd->jcd",
        chooser,
        lax.all_gather(local_packed, "req", axis=0, tiled=True),
        preferred_element_type=jnp.float32,
    ).astype(jnp.bfloat16)
    triple = packed.reshape(req_count, fresh_len, local_heads, 3, HEAD)
    queries = triple[:, :, :, 0]
    fresh_keys = triple[:, :, :, 1]
    fresh_values = triple[:, :, :, 2]
    span = page_table.shape[1] * key_pool.shape[1]
    cached_keys = key_pool[page_table].reshape(req_count, span, local_heads, HEAD)
    cached_values = value_pool[page_table].reshape(req_count, span, local_heads, HEAD)
    scale = 1.0 / math.sqrt(HEAD)
    scores_old = (
        jnp.einsum("rqhd,rkhd->rhqk", queries, cached_keys, preferred_element_type=jnp.float32)
        * scale
    )
    visible = jnp.arange(span, dtype=jnp.int32)[None, None, None, :] < lengths[:, None, None, None]
    scores_old = jnp.where(visible, scores_old, -1e30)
    scores_new = (
        jnp.einsum("rqhd,rkhd->rhqk", queries, fresh_keys, preferred_element_type=jnp.float32)
        * scale
    )
    causal = jnp.arange(fresh_len)[:, None] >= jnp.arange(fresh_len)[None, :]
    scores_new = jnp.where(causal[None, None, :, :], scores_new, -1e30)
    peak = jnp.maximum(
        jnp.max(scores_old, axis=-1, keepdims=True), jnp.max(scores_new, axis=-1, keepdims=True)
    )
    exp_old = jnp.exp(scores_old - peak)
    exp_new = jnp.exp(scores_new - peak)
    denom = jnp.sum(exp_old, axis=-1, keepdims=True) + jnp.sum(exp_new, axis=-1, keepdims=True)
    weight_old = (exp_old / denom).astype(jnp.bfloat16)
    weight_new = (exp_new / denom).astype(jnp.bfloat16)
    mixed = jnp.einsum(
        "rhqk,rkhd->rqhd", weight_old, cached_values, preferred_element_type=jnp.float32
    )
    mixed = mixed + jnp.einsum(
        "rhqk,rkhd->rqhd", weight_new, fresh_values, preferred_element_type=jnp.float32
    )
    attended = mixed.astype(jnp.bfloat16).reshape(req_count, fresh_len, local_heads * HEAD)
    return (
        attended,
        fresh_keys.reshape(req_count, fresh_len, local_heads * HEAD),
        fresh_values.reshape(req_count, fresh_len, local_heads * HEAD),
    )


def solution(mesh):
    in_specs = (
        P("req", None, "wgt"),
        P(),
        P("req"),
        P("req", None),
        P(),
        P(),
        P("req", "wgt"),
        P("wgt"),
        P("req", None, "wgt"),
        P("req", None, "wgt"),
    )
    out_specs = (P("req", None, "wgt"), P("req", None, "wgt"), P("req", None, "wgt"))
    return jax.shard_map(
        per_device, mesh=mesh, in_specs=in_specs, out_specs=out_specs, check_vma=False
    )
```

profile of v0, /device:TPU:0, one launch (start us, length us, event | category | flops | bytes accessed | tf_op | source)
XLA Modules:
  0.0 376.0 jit_solution(12219935112345486848)
XLA Ops:
  7.2 0.0 all-gather.4.cloned.1.call-start
  7.2 0.7 all-gather.4.cloned.1.call-update
  7.9 0.0 all-gather.6.cloned.1.call-start
  7.9 0.7 all-gather.6.cloned.1.call-update
  8.7 0.0 all-gather.8.cloned.1.call-start
  8.7 0.7 convert_element_type.48
  9.4 0.7 convert_element_type.49
  10.1 0.7 convert_element_type.51
  10.8 1.3 gather_fusion.1
  12.1 0.9 convert_reduce_fusion.1
  13.0 0.6 gather_fusion.2
  13.7 1.2 dynamic-slice
  15.6 0.9 dynamic-update-slice
  16.4 9.5 %all-reduce = s32[32]{0:T(128)S(1)} all-reduce(s32[32]{0:T(128)S(1)} %dynamic-update-slice), channel_id=1, replica_groups=mesh['req'=8,'wgt'=4] {'req'}, use_global_device_ids=true, to_apply=%add | all-reduce | flops 32 | bytes 256
  25.9 0.6 gather_fusion.3
  26.6 0.1 add_convert_fusion.2
  26.6 0.4 multiply_cosine_fusion
  27.1 35.7 %all-gather.4.cloned.1.call-done = bf16[4,48,6144]{2,1,0:T(8,128)(2,1)} async-done(((bf16[4,48,1536]{2,1,0:T(8,128)(2,1)}), bf16[4,48,6144]{2,1,0:T(8,128)(2,1)}) %all-gather.4.cloned.1.call-update) | async-done | bytes 2359312 | tf_op jit(solution)/shard_map/all_gather | solution.py:46
  62.8 2.1 convert_reduce_fusion
  64.8 2.4 fusion.15
  67.3 2.7 fusion.18
  70.0 132.2 %all-gather.6.cloned.1.call-done = bf16[6144,2304]{1,0:T(8,128)(2,1)} async-done(((bf16[768,2304]{1,0:T(8,128)(2,1)}), bf16[6144,2304]{1,0:T(8,128)(2,1)}) %all-gather.6.cloned.1.call-update) | async-done | bytes 28311568 | tf_op jit(solution)/shard_map/all_gather | solution.py:56
  202.2 13.9 %convolution_add_fusion = f32[192,2304]{1,0:T(8,128)} fusion(bf16[192,6144]{1,0:T(8,128)(2,1)S(1)} %bitcast.55, bf16[6144,2304]{1,0:T(8,128)(2,1)} %all-gather.6.cloned.1.call-done, f32[2304]{0:T(1024)S(1)} %convert_element_type.51), kind=kOutput, calls=%fused_computation.29 | convolution fusion | flops 5436260352 | bytes 32449536 | tf_op jit(solution)/shard_map/dot_general | solution.py:54
  216.0 4.1 %reshape.167 = f32[4,48,8,3,96]{4,3,2,1,0:T(4,128)S(1)} reshape(f32[192,2304]{1,0:T(8,128)} %convolution_add_fusion) | data formatting | bytes 3538944 | tf_op jit(solution)/shard_map/reshape | solution.py:60
  220.1 1.2 fusion.45
  221.3 0.8 slice.86
  222.1 0.2 slice.87
  222.3 0.2 slice.88
  222.5 0.7 subtract_convert_fusion.1
  223.2 0.0 copy-start.3
  223.2 0.7 maximum_bitcast_fusion
  223.9 0.8 copy.73
  224.8 0.8 copy.74
  225.6 3.3 pad_maximum_fusion
  228.9 2.5 convert_element_type.53
  231.4 0.0 all-gather.8.cloned.1.call-update
  231.4 0.0 copy-done.3
  231.4 0.1 reshape.173
  231.5 10.9 %gather_fusion.4 = bf16[64,128,768]{2,1,0:T(8,128)(2,1)} fusion(bf16[40,128,768]{2,1,0:T(8,128)(2,1)} %param.18, s32[1024]{0:T(1024)S(1)} %pad_clamp_fusion), kind=kCustom, calls=%fused_computation.4 | custom fusion | bytes 25166080 | tf_op jit(solution)/shard_map/gather | solution.py:79
  242.4 28.4 %reshape.224 = bf16[4,2048,8,96]{3,2,1,0:T(8,128)(2,1)} reshape(bf16[64,128,768]{2,1,0:T(8,128)(2,1)} %gather_fusion.4) | data formatting | bytes 25165824 | tf_op jit(solution)/shard_map/reshape | solution.py:79
  270.8 10.6 %gather_fusion = bf16[64,128,768]{2,1,0:T(8,128)(2,1)} fusion(bf16[40,128,768]{2,1,0:T(8,128)(2,1)} %param.19, s32[1024]{0:T(1024)S(1)} %pad_clamp_fusion), kind=kCustom, calls=%fused_computation | custom fusion | bytes 25166080 | tf_op jit(solution)/shard_map/gather | solution.py:80
  281.4 28.4 %reshape.223 = bf16[4,2048,8,96]{3,2,1,0:T(8,128)(2,1)} reshape(bf16[64,128,768]{2,1,0:T(8,128)(2,1)} %gather_fusion) | data formatting | bytes 25165824 | tf_op jit(solution)/shard_map/reshape | solution.py:80
  309.8 0.0 copy-done
  309.8 0.0 copy-done.4
  309.9 0.1 iota_compare_fusion
  309.9 0.0 all-gather.8.cloned.1.call-done
  310.0 7.1 %fusion.19 = bf16[4,48,2304]{2,0,1:T(4,128)(2,1)S(1)} fusion(bf16[32,48,2304]{2,1,0:T(8,128)(2,1)} %all-gather.8.cloned.1.call-done, s32[32]{0:T(128)S(1)} %convert_reduce_fusion.1, pred[32]{0:T(512)(128)(4,1)S(1)} %broadcast_compare_fusion), kind=kOutput, calls=%fused_computation.30 | convolution fusion | flops 28754176 | bytes 7962784 | tf_op jit(solution)/shard_map/jr,rcd->jcd/dot_general | solution.py:68
  317.0 1.9 reshape.225
  318.9 6.9 %slice_reduce_fusion = (bf16[4,48,8,96]{3,2,0,1:T(8,128)(2,1)}, bf16[4,48,8,96]{3,2,0,1:T(8,128)(2,1)S(1)}, bf16[4,48,8,1,96]{4,3,2,0,1:T(2,128)(2,1)S(1)}, bf16...) fusion(bf16[4,48,8,3,96]{4,3,2,0,1:T(4,128)(2,1)S(1)} %reshape.225), kind=kLoop, calls=%fused_computation.81 | loop fusion | bytes 2359296 | tf_op jit(solution)/shard_map/slice | solution.py:77
  325.8 15.5 %fusion.4 = (f32[4,8,48]{2,1,0:T(8,128)S(1)}, f32[4,8,48,2048]{3,2,1,0:T(8,128)}) fusion(pred[4,2048]{1,0:T(4,128)(4,1)S(1)} %iota_compare_fusion, bf16[4,2048,8,96]{3,2,1,0:T(8,128)(2,1)} %reshape.224, bf16[4,48,8,1,96]{4,3,2,0,1:T(2,128)(2,1)S(1)} %get-tuple-element.8), kind=kOutput, calls=%fused_computation.12 | convolution fusion | flops 613415424 | bytes 25475072 | tf_op jit(solution)/shard_map/rqhd,rkhd->rhqk/dot_general | solution.py:83
  341.3 1.0 fusion.46
  342.3 0.0 copy-start.2
  342.3 0.2 fusion.32
  342.5 0.0 copy-start.1
  342.5 7.5 %fusion.5 = f32[4,8,48]{2,1,0:T(8,128)S(1)} fusion(f32[4,8,48,2048]{3,2,1,0:T(8,128)} %get-tuple-element.19, f32[4,8,48]{2,1,0:T(8,128)S(1)} %max.8, pred[4,2048]{1,0:T(4,128)(4,1)S(1)} %iota_compare_fusion), kind=kLoop, calls=%fused_computation.13 | loop fusion | flops 12581376 | bytes 12603392 | tf_op jit(solution)/shard_map/reduce_sum | solution.py:99
  350.0 0.0 copy-done.2
  350.0 1.5 fusion.33
  351.6 12.2 %fusion.29 = bf16[4,48,8,96]{3,1,2,0:T(8,128)(2,1)} fusion(f32[4,8,96,48]{2,3,1,0:T(8,128)} %fusion.33, bf16[4,2048,8,96]{3,2,1,0:T(8,128)(2,1)} %reshape.223, f32[4,8,48,2048]{3,2,1,0:T(8,128)S(1)} %copy-done.1, f32[4,8,48]{2,1,0:T(8,128)S(1)} %add.131, f32[4,8,48]{2,1,0:T(8,128)S(1)} %max.8, pred[4,2048]{1,0:T(4,128)(4,1)S(1)} %iota_compare_fusion), kind=kOutput, calls=%fused_computation.36 | convolution fusion | flops 620003328 | bytes 26071040 | tf_op jit(solution)/shard_map/rhqk,rkhd->rqhd/dot_general | solution.py:102
  363.7 1.1 copy.84
  364.8 1.0 reshape.170
  365.9 1.4 reshape.227
  367.3 0.7 copy.101
  368.0 0.4 reshape.226
  368.4 0.7 copy.99
  (17 shorter events, 0.1 us)
Async XLA Ops:
  7.2 55.6 %all-gather.4.cloned.1.call-start = ((), (), s32[]{:S(2)}) async-start(), calls=%async_computation | async-start | bytes 2949120 | tf_op jit(solution)/shard_map/all_gather | solution.py:46
  7.9 194.3 %all-gather.6.cloned.1.call-start = ((), (), s32[]{:S(2)}) async-start(), calls=%async_computation.1 | async-start | bytes 31850496 | tf_op jit(solution)/shard_map/all_gather | solution.py:56
  8.7 301.3 %all-gather.8.cloned.1.call-start = ((), (), s32[]{:S(2)}) async-start(), calls=%async_computation.2 | async-start | bytes 7962624 | tf_op jit(solution)/shard_map/all_gather | solution.py:71
  223.2 8.2 %copy-start.3 = (s32[4,16]{1,0:T(4,128)S(1)}, s32[4,16]{1,0:T(4,128)}, u32[]{:S(2)}) copy-start(s32[4,16]{1,0:T(4,128)} %param.13) | copy-start | bytes 772
  281.4 28.4 %copy-start = (s32[32]{0:T(128)S(1)}, s32[32]{0:T(128)}, u32[]{:S(2)}) copy-start(s32[32]{0:T(128)} %param.11) | copy-start | bytes 388
  281.4 28.4 %copy-start.4 = (s32[4]{0:T(128)S(1)}, s32[4]{0:T(128)}, u32[]{:S(2)}) copy-start(s32[4]{0:T(128)} %param.12) | copy-start | bytes 52
  342.3 7.7 %copy-start.2 = (bf16[4,48,8,1,96]{4,3,2,0,1:T(2,128)(2,1)S(1)}, bf16[4,48,8,1,96]{4,3,2,0,1:T(2,128)(2,1)}, u32[]{:S(2)}) copy-start(bf16[4,48,8,1,96]{4,3,2,0,1:T(2,128)(2,1)} %get-tuple-element.9) | copy-start | bytes 884740
  342.5 9.1 %copy-start.1 = (f32[4,8,48,2048]{3,2,1,0:T(8,128)S(1)}, f32[4,8,48,2048]{3,2,1,0:T(8,128)}, u32[]{:S(2)}) copy-start(f32[4,8,48,2048]{3,2,1,0:T(8,128)} %get-tuple-element.19) | copy-start | bytes 37748740
Sparse Core Ops, SparseCore 0:
  9.6 53.1 all-gather.3
  64.6 137.4 all-gather.5
  231.5 48.8 all-gather.7
where the time goes:
time: 381 us; the launch traced here: 376 us
  waiting for transfers between devices  169 us (44%)
  local copies, waits for them, and re-layouts  108 us (28%)
  matrix products  51.1 us (13%)
  other arithmetic  23.3 us (6%)
  between operations  14.9 us (4%)
  blocking collectives  9.46 us (2%)
    all_gather x1, waiting for transfers between devices, per_device(): lax.all_gather(w_qkv, 'req', axis=0, tiled=True)  132 us
    all_gather x1, waiting for transfers between devices, per_device(): gathered = lax.all_gather(arrivals, 'wgt', axis=2, tiled=True)  35.7 us
    reshape x1, local copies, waits for them, and re-layouts, per_device(): key_pool[page_table].reshape(req_count, span, local_heads, HEAD)  28.4 us
    reshape x1, local copies, waits for them, and re-layouts, per_device(): value_pool[page_table].reshape(req_count, span, local_heads, HEAD)  28.4 us
    dot_general x1, matrix products, per_device(): jnp.einsum('rqhd,rkhd->rhqk', queries, cached_keys, preferred_element_typ...  15.5 us
    dot_general x1, matrix products, per_device(): jnp.dot(project_normed, lax.all_gather(w_qkv, 'req', axis=0, tiled=True),...  13.9 us
    dot_general x1, matrix products, per_device(): jnp.einsum('rhqk,rkhd->rqhd', weight_old, cached_values, preferred_elemen...  12.2 us
    gather x1, local copies, waits for them, and re-layouts, per_device(): key_pool[page_table].reshape(req_count, span, local_heads, HEAD)  10.9 us
  transfers between devices with their start and end apart: 3, of which 2 were waited for; matrix products, arithmetic and copies ran while one was open for 25% of the time, Pallas kernels for 0%

commit v1 on v0

v1 whole, which is shorter than its diff:
```python
import functools
import math

import jax
import jax.numpy as jnp
import numpy as np
from jax import lax
from jax.experimental import pallas as pl
from jax.experimental.pallas import tpu as pltpu
from jax.sharding import PartitionSpec as P

HEAD = 96
ROT = 24
EPS = 1e-05
LANES = 128
WINDOW = 2 * LANES
CHUNK_PAGES = 4
VMEM_LIMIT = 56 * 1024 * 1024

ANY = pl.BlockSpec(memory_space=pl.ANY)
SMEM = pl.BlockSpec(memory_space=pltpu.SMEM)
VMEM = pl.BlockSpec(memory_space=pltpu.VMEM)


def norm_kernel(depth, chips, place, *refs):
    pieces = refs[: 2 * depth - 1]
    gain, bias = refs[2 * depth - 1 : 2 * depth + 1]
    outs = refs[2 * depth + 1 : 2 * depth + 1 + chips]
    held, sems = refs[2 * depth + 1 + chips :]
    me, chip = place[0], place[1]
    copies = []
    for index, piece in enumerate(pieces):
        if index == 0:
            offset = 0
        elif index < depth:
            offset = -index
        else:
            offset = index - depth + 1
        copies.append((offset, pltpu.make_async_copy(piece, held.at[me + offset], sems.at[index])))

    def inside(offset):
        return (me + offset >= 0) & (me + offset < depth)

    for offset, copy in copies:

        @pl.when(inside(offset))
        def _():
            copy.start()

    for offset, copy in copies:

        @pl.when(inside(offset))
        def _():
            copy.wait()

    rows, width = held.shape[1], held.shape[2]
    step = 16
    total_width = depth * width
    block = total_width // chips
    per = chips // depth

    def body(index, carry):
        at = pl.ds(pl.multiple_of(index * step, step), step)
        values = [held[part, at, :].astype(jnp.float32) for part in range(depth)]
        total = sum(jnp.sum(value, axis=-1, keepdims=True) for value in values)
        center = total / total_width
        square = sum(
            jnp.sum(jnp.square(value - center), axis=-1, keepdims=True) for value in values
        )
        scale = lax.rsqrt(square / total_width + EPS)
        for offset in range(chips):
            target = chip ^ offset
            part = target // per
            lane = pl.ds(pl.multiple_of((target % per) * block, LANES), block)
            value = held[part, at, lane].astype(jnp.float32)
            value = (value - center) * scale * gain[target] + bias[target]
            outs[offset][at, :] = value.astype(jnp.bfloat16)
        return carry

    lax.fori_loop(0, rows // step, body, 0)


def project_kernel(fresh_len, req_count, place, source, *refs):
    groups = (len(refs) - 7) // 2
    tokens = refs[:groups]
    own_rows, other_rows = refs[groups : groups + 2]
    outs = refs[groups + 2 : 2 * groups + 2]
    held, weights, picked, sems, weight_sems = refs[2 * groups + 2 :]
    core = place[0]
    depth = own_rows.shape[0]
    copies = [
        pltpu.make_async_copy(
            token, held.at[pl.ds(index * req_count, req_count)], sems.at[index]
        )
        for index, token in enumerate(tokens)
    ]
    copies.append(
        pltpu.make_async_copy(
            own_rows,
            weights.at[pl.ds(pl.multiple_of(core * depth, 16), depth)],
            weight_sems.at[0],
        )
    )
    copies.append(
        pltpu.make_async_copy(
            other_rows,
            weights.at[pl.ds(pl.multiple_of((1 - core) * depth, 16), depth)],
            weight_sems.at[1],
        )
    )
    for copy in copies:
        copy.start()
    for copy in copies:
        copy.wait()
    rows = req_count * fresh_len
    for pair in range(groups // 2):
        for item in range(2 * req_count):
            picked[item * fresh_len : (item + 1) * fresh_len, :] = held[
                source[pair * 2 * req_count + item]
            ]
        result = jnp.dot(picked[...], weights[...], preferred_element_type=jnp.float32).astype(
            jnp.bfloat16
        )
        outs[2 * pair][...] = result[:rows]
        outs[2 * pair + 1][...] = result[rows:]


def attend_kernel(shape, place, lengths, table, *refs):
    groups, req_count, fresh_len, page, heads = shape
    parts = refs[:groups]
    bias, cosine, sine_up, sine_down, key_pool, value_pool = refs[groups : groups + 6]
    attended, new_keys, new_values = refs[groups + 6 : groups + 9]
    keys, values, sems = refs[groups + 9 :]
    core = place[0]
    chunk = CHUNK_PAGES * page
    pairs = heads // 2

    counts = [pl.cdiv(lengths[index], chunk) for index in range(req_count)]
    bases = [jnp.int32(0)]
    for count in counts[:-1]:
        bases.append(bases[-1] + count * CHUNK_PAGES)

    def copies(index, entry):
        number = table[index, entry]
        slot = bases[index] + entry
        return (
            pltpu.make_async_copy(key_pool.at[number], keys.at[slot], sems.at[index]),
            pltpu.make_async_copy(value_pool.at[number], values.at[slot], sems.at[index]),
        )

    for index in range(req_count):

        def start(entry, carry, index=index):
            for copy in copies(index, entry):
                copy.start()
            return carry

        lax.fori_loop(0, counts[index] * CHUNK_PAGES, start, 0)

    even = sum(parts[index][...].astype(jnp.float32) for index in range(0, groups, 2))
    odd = sum(parts[index][...].astype(jnp.float32) for index in range(1, groups, 2))
    halves = (jnp.where(core == 0, even, odd), jnp.where(core == 0, odd, even))
    halves = [
        half + bias[:, side * half.shape[1] : (side + 1) * half.shape[1]]
        for side, half in enumerate(halves)
    ]

    def kind(which):
        pieces = []
        for head in range(heads):
            half = halves[head // pairs]
            begin = (head % pairs) * 3 * HEAD + which * HEAD
            pieces.append(half[:, begin : begin + HEAD])
        return jnp.concatenate(pieces, axis=1)

    width = heads * HEAD

    def turn(block):
        half_rot = ROT // 2
        return (
            block * cosine[...]
            + pltpu.roll(block, width - half_rot, 1) * sine_up[...]
            + pltpu.roll(block, half_rot, 1) * sine_down[...]
        )

    queries = turn(kind(0)).astype(jnp.bfloat16)
    turned = turn(kind(1)).astype(jnp.bfloat16)
    plain = kind(2).astype(jnp.bfloat16)
    for index in range(req_count):
        rows = slice(index * fresh_len, (index + 1) * fresh_len)
        new_keys[index] = turned[rows]
        new_values[index] = plain[rows]

    factor = 1.0 / math.sqrt(HEAD) / math.log(2.0)
    starts = [(2 * HEAD * pair) // LANES * LANES for pair in range(pairs)]
    lane = lax.broadcasted_iota(jnp.int32, (fresh_len, WINDOW), 1)

    def owned(pair, member):
        begin = (2 * pair + member) * HEAD - starts[pair]
        return (lane >= begin) & (lane < begin + HEAD)

    def contract(left, right):
        return lax.dot_general(
            left, right, (((1,), (1,)), ((), ())), preferred_element_type=jnp.float32
        )

    zero = jnp.zeros((fresh_len, WINDOW), jnp.bfloat16)
    spread_rows = heads * fresh_len
    row = lax.broadcasted_iota(jnp.int32, (2 * fresh_len, fresh_len), 0)
    causal_pair = lax.rem(row, fresh_len) >= lax.broadcasted_iota(
        jnp.int32, (2 * fresh_len, fresh_len), 1
    )
    for index in range(req_count):
        rows = slice(index * fresh_len, (index + 1) * fresh_len)
        spread = []
        for pair in range(pairs):
            window = queries[rows, starts[pair] : starts[pair] + WINDOW]
            spread.append(
                jnp.concatenate(
                    [jnp.where(owned(pair, member), window, zero) for member in range(2)], axis=0
                )
            )
        scores = jnp.concatenate(
            [
                jnp.where(
                    causal_pair,
                    contract(spread[pair], turned[rows, starts[pair] : starts[pair] + WINDOW]),
                    -1e30,
                )
                for pair in range(pairs)
            ],
            axis=0,
        )
        peak = jnp.max(scores, axis=1, keepdims=True)
        weight = jnp.exp2((scores - peak) * factor)
        denom = jnp.sum(weight, axis=1, keepdims=True)
        weight = weight.astype(jnp.bfloat16)
        mixed = jnp.concatenate(
            [
                jnp.dot(
                    weight[pair * 2 * fresh_len : (pair + 1) * 2 * fresh_len],
                    plain[rows, starts[pair] : starts[pair] + WINDOW],
                    preferred_element_type=jnp.float32,
                )
                for pair in range(pairs)
            ],
            axis=0,
        )

        def finish(entry, carry, index=index):
            for copy in copies(index, entry):
                copy.wait()
            return carry

        lax.fori_loop(0, counts[index] * CHUNK_PAGES, finish, 0)

        def step(part, carry, index=index, spread=spread):
            peak, denom, mixed = carry
            first = bases[index] + part * CHUNK_PAGES
            key_block = keys[pl.ds(first, CHUNK_PAGES)].reshape(chunk, width)
            scores = jnp.concatenate(
                [
                    contract(spread[pair], key_block[:, starts[pair] : starts[pair] + WINDOW])
                    for pair in range(pairs)
                ],
                axis=0,
            )
            position = part * chunk + lax.broadcasted_iota(jnp.int32, (spread_rows, chunk), 1)
            scores = jnp.where(position < lengths[index], scores, -1e30)
            higher = jnp.maximum(peak, jnp.max(scores, axis=1, keepdims=True))
            shrink = jnp.exp2((peak - higher) * factor)
            weight = jnp.exp2((scores - higher) * factor)
            denom = denom * shrink + jnp.sum(weight, axis=1, keepdims=True)
            weight = weight.astype(jnp.bfloat16)
            value_block = values[pl.ds(first, CHUNK_PAGES)].reshape(chunk, width)
            added = jnp.concatenate(
                [
                    jnp.dot(
                        weight[pair * 2 * fresh_len : (pair + 1) * 2 * fresh_len],
                        value_block[:, starts[pair] : starts[pair] + WINDOW],
                        preferred_element_type=jnp.float32,
                    )
                    for pair in range(pairs)
                ],
                axis=0,
            )
            return higher, denom, mixed * shrink + added

        peak, denom, mixed = lax.fori_loop(0, counts[index], step, (peak, denom, mixed))
        mixed = mixed / denom
        tiles = [None] * (width // LANES)
        for pair in range(pairs):
            for member in range(2):
                begin = (2 * pair + member) * fresh_len
                part = jnp.where(owned(pair, member), mixed[begin : begin + fresh_len], 0.0)
                for side in range(2):
                    place_at = starts[pair] // LANES + side
                    tile = part[:, side * LANES : (side + 1) * LANES]
                    tiles[place_at] = tile if tiles[place_at] is None else tiles[place_at] + tile
        attended[index] = jnp.concatenate(tiles, axis=1).astype(jnp.bfloat16)


def per_device(
    req_size,
    wgt_size,
    arrivals,
    group_of,
    lengths,
    page_table,
    ln_gain,
    ln_bias,
    w_qkv,
    qkv_bias,
    key_pool,
    value_pool,
):
    req_count, fresh_len, width = arrivals.shape
    rows = req_count * fresh_len
    depth, local_cols = w_qkv.shape
    half_cols = local_cols // 2
    heads = local_cols // (3 * HEAD)
    page = key_pool.shape[1]
    chips = req_size // 2
    block = 2 * depth
    everyone = group_of.shape[0]
    me = lax.axis_index("req")
    layer = lax.axis_index("wgt")
    core = me & 1
    chip = me >> 1

    def swap(value, distance):
        return lax.ppermute(
            value, "req", [(device, device ^ distance) for device in range(req_size)]
        )

    own = arrivals.reshape(rows, width)
    upward, downward = [], []
    up = down = own
    for hop in range(1, wgt_size):
        up = lax.ppermute(up, "wgt", [(at, at + 1) for at in range(hop - 1, wgt_size - 1)])
        down = lax.ppermute(down, "wgt", [(at + 1, at) for at in range(wgt_size - hop)])
        upward.append(up)
        downward.append(down)

    own_rows = lax.dynamic_slice_in_dim(w_qkv, core * half_cols, half_cols, 1)
    other_rows = swap(lax.dynamic_slice_in_dim(w_qkv, (1 - core) * half_cols, half_cols, 1), 1)

    ids = jnp.arange(everyone, dtype=jnp.int32)
    same_group = group_of[:, None] == group_of[None, :]
    earlier = ids[None, :] < ids[:, None]
    rank = jnp.sum((same_group & earlier).astype(jnp.int32), axis=1)
    slot_of = group_of * req_count + rank
    target = (me ^ (ids // req_count)) * req_count + ids % req_count
    order = jnp.sum(jnp.where(slot_of[None, :] == target[:, None], ids[None, :], 0), axis=1)
    source = ((order // req_count) ^ me) * req_count + order % req_count

    lane = np.arange(heads * HEAD) % HEAD
    half_rot = ROT // 2
    inverse = jnp.power(10000.0, -jnp.asarray(lane % half_rot, jnp.float32) * 2.0 / ROT)
    positions = (
        lengths[:, None] + jnp.arange(fresh_len, dtype=jnp.int32)[None, :]
    ).astype(jnp.float32)
    angles = positions.reshape(rows, 1) * inverse[None, :]
    turns = jnp.asarray(lane < ROT)[None, :]
    cosine = jnp.where(turns, jnp.cos(angles), 1.0)
    sine = jnp.sin(angles)
    sine_up = jnp.where(jnp.asarray(lane < half_rot)[None, :], -sine, 0.0)
    sine_down = jnp.where(turns & jnp.asarray(lane >= half_rot)[None, :], sine, 0.0)

    normed = pl.pallas_call(
        functools.partial(norm_kernel, wgt_size, chips),
        out_shape=[jax.ShapeDtypeStruct((rows, block), jnp.bfloat16)] * chips,
        in_specs=[SMEM] + [ANY] * (2 * wgt_size - 1) + [VMEM] * 2,
        out_specs=[VMEM] * chips,
        scratch_shapes=[
            pltpu.VMEM((wgt_size, rows, width), jnp.bfloat16),
            pltpu.SemaphoreType.DMA((2 * wgt_size - 1,)),
        ],
        compiler_params=pltpu.CompilerParams(vmem_limit_bytes=VMEM_LIMIT),
        name="norm",
    )(
        jnp.stack([layer, chip]).astype(jnp.int32),
        own,
        *upward,
        *downward,
        ln_gain.astype(jnp.float32).reshape(chips, 1, block),
        ln_bias.astype(jnp.float32).reshape(chips, 1, block),
    )

    tokens = []
    for distance in range(chips):
        mine = normed[distance] if distance == 0 else swap(normed[distance], 2 * distance)
        tokens += [mine, swap(mine, 1)]

    place = jnp.stack([core]).astype(jnp.int32)
    partial = pl.pallas_call(
        functools.partial(project_kernel, fresh_len, req_count),
        out_shape=[jax.ShapeDtypeStruct((rows, half_cols), jnp.bfloat16)] * req_size,
        in_specs=[SMEM] * 2 + [ANY] * (req_size + 2),
        out_specs=[VMEM] * req_size,
        scratch_shapes=[
            pltpu.VMEM((everyone, fresh_len, block), jnp.bfloat16),
            pltpu.VMEM((block, half_cols), jnp.bfloat16),
            pltpu.VMEM((2 * rows, block), jnp.bfloat16),
            pltpu.SemaphoreType.DMA((req_size,)),
            pltpu.SemaphoreType.DMA((2,)),
        ],
        compiler_params=pltpu.CompilerParams(vmem_limit_bytes=VMEM_LIMIT),
        name="project",
    )(
        place,
        source,
        *[token.reshape(req_count, fresh_len, block) for token in tokens],
        own_rows,
        other_rows,
    )

    parts = [partial[0]] + [swap(partial[distance], distance) for distance in range(1, req_size)]

    slots = page_table.shape[1] * (req_count + 1) // 2
    out = jax.ShapeDtypeStruct((req_count, fresh_len, heads * HEAD), jnp.bfloat16)
    return pl.pallas_call(
        functools.partial(attend_kernel, (req_size, req_count, fresh_len, page, heads)),
        out_shape=[out] * 3,
        in_specs=[SMEM] * 3 + [VMEM] * (req_size + 4) + [ANY] * 2,
        out_specs=[VMEM] * 3,
        scratch_shapes=[
            pltpu.VMEM((slots, page, heads * HEAD), jnp.bfloat16),
            pltpu.VMEM((slots, page, heads * HEAD), jnp.bfloat16),
            pltpu.SemaphoreType.DMA((req_count,)),
        ],
        compiler_params=pltpu.CompilerParams(vmem_limit_bytes=VMEM_LIMIT),
        name="attend",
    )(
        place,
        lengths,
        page_table,
        *parts,
        qkv_bias.astype(jnp.float32).reshape(1, local_cols),
        cosine,
        sine_up,
        sine_down,
        key_pool,
        value_pool,
    )


def solution(mesh):
    in_specs = (
        P("req", None, "wgt"),
        P(),
        P("req"),
        P("req", None),
        P(),
        P(),
        P("req", "wgt"),
        P("wgt"),
        P("req", None, "wgt"),
        P("req", None, "wgt"),
    )
    out_specs = (P("req", None, "wgt"), P("req", None, "wgt"), P("req", None, "wgt"))
    return jax.shard_map(
        functools.partial(per_device, mesh.shape["req"], mesh.shape["wgt"]),
        mesh=mesh,
        in_specs=in_specs,
        out_specs=out_specs,
        check_vma=False,
    )
```

time: 381 us -> 162 us (0.43); the launches traced: 376 us -> 161 us
  local copies, waits for them, and re-layouts: 108 us -> 6.08 us
  waiting for transfers between devices: 169 us -> 91.4 us
  matrix products: 51.1 us -> 0 us
  Pallas kernels: 0 us -> 32.8 us
  starting transfers between devices: 0.11 us -> 23.1 us
  other arithmetic: 23.3 us -> 6.91 us
  between operations: 14.9 us -> 0.89 us
  blocking collectives: 9.46 us -> 0 us
    all_gather x3 -> x0, waiting for transfers between devices: 168 us -> none  [the longest x1 132 us: per_device(): lax.all_gather(w_qkv, 'req', axis=0, tiled=True)]
    ppermute x0 -> x21, waiting for transfers between devices: none -> 91.4 us  [the longest x15 55.2 us: swap(): lax.ppermute(value, 'req', [(device, device ^ distance) for device in ran...]
    reshape x5 -> x1, local copies, waits for them, and re-layouts: 63.8 us -> 0.6 us  [per_device(): qkv_bias.astype(jnp.float32).reshape(1, local_cols)]
    dot_general x6 -> x0, matrix products: 51.1 us -> none  [the longest x1 15.5 us: per_device(): jnp.einsum('rqhd,rkhd->rhqk', queries, cached_keys, preferred_element_typ...]
    pallas_call x0 -> x3, Pallas kernels: none -> 32.8 us  [the longest x1 14 us: per_device(): pl.pallas_call(functools.partial(attend_kernel, (req_size, req_count, fre...]
    gather x5 -> x0, local copies, waits for them, and re-layouts: 24.1 us -> none  [the longest x1 10.9 us: per_device(): key_pool[page_table].reshape(req_count, span, local_heads, HEAD)]
    ppermute x0 -> x21, starting transfers between devices: none -> 23.1 us  [the longest x15 11.3 us: swap(): lax.ppermute(value, 'req', [(device, device ^ distance) for device in ran...]
    reduce_sum x5 -> x2, other arithmetic: 13.1 us -> 0.36 us  [the longest x1 0.18 us: per_device(): jnp.sum(jnp.where(slot_of[None, :] == target[:, None], ids[None, :], 0),...]
  transfers between devices with their start and end apart: 3 -> 21, of which waited for: 2 -> 11; matrix products, arithmetic and copies ran while one was open for 25% -> 7% of each run, Pallas kernels for 0% -> 5%
where the time goes in v1:
time: 162 us; the launch traced here: 161 us
  waiting for transfers between devices  91.4 us (56%)
  Pallas kernels  32.8 us (20%)
  starting transfers between devices  23.1 us (14%)
  other arithmetic  6.91 us (4%)
  local copies, waits for them, and re-layouts  6.08 us (4%)
    ppermute x15, waiting for transfers between devices, swap(): lax.ppermute(value, 'req', [(device, device ^ distance) for device in ran...  55.2 us
    ppermute x3, waiting for transfers between devices, per_device(): lax.ppermute(down, 'wgt', [(at + 1, at) for at in range(wgt_size - hop)])  24.6 us
    pallas_call x1, Pallas kernels, per_device(): pl.pallas_call(functools.partial(attend_kernel, (req_size, req_count, fre...  14 us
    ppermute x3, waiting for transfers between devices, per_device(): lax.ppermute(up, 'wgt', [(at, at + 1) for at in range(hop - 1, wgt_size -...  11.6 us
    pallas_call x1, Pallas kernels, per_device(): pl.pallas_call(functools.partial(project_kernel, fresh_len, req_count), o...  11.5 us
    ppermute x15, starting transfers between devices, swap(): lax.ppermute(value, 'req', [(device, device ^ distance) for device in ran...  11.3 us
    ppermute x3, starting transfers between devices, per_device(): lax.ppermute(up, 'wgt', [(at, at + 1) for at in range(hop - 1, wgt_size -...  7.96 us
    pallas_call x1, Pallas kernels, per_device(): pl.pallas_call(functools.partial(norm_kernel, wgt_size, chips), out_shape...  7.34 us
  transfers between devices with their start and end apart: 21, of which 11 were waited for; matrix products, arithmetic and copies ran while one was open for 7% of the time, Pallas kernels for 5%

profile of v1, /device:TPU:0, one launch (start us, length us, event | category | flops | bytes accessed | tf_op | source)
XLA Modules:
  0.0 161.1 jit_solution(12407866662110384214)
XLA Ops:
  0.6 5.0 %collective-permute-start = (bf16[192,1536]{1,0:T(8,128)(2,1)}, bf16[192,1536]{1,0:T(8,128)(2,1)S(1)}, u32[]{:S(2)}, u32[]{:S(2)}) collective-permute-start(bf16[192,1536]{1,0:T(8,128)(2,1)} %bitcast.14), channel_id=1, source_target_pairs={{0,1},{1,2},{2,3},{4,5},{5,6},{6,7},{8,9},{9,10},{10,11},{12,13},{... | collective-permute-start | bytes 1769480 | tf_op jit(solution)/shard_map/ppermute | solution.py:340
  5.6 1.3 collective-permute-start.3
  6.9 11.5 %collective-permute-done.refs_1_ = bf16[192,1536]{1,0:T(8,128)(2,1)S(1)} collective-permute-done((bf16[192,1536]{1,0:T(8,128)(2,1)}, bf16[192,1536]{1,0:T(8,128)(2,1)S(1)}, u32[]{:S(2)}, u32[]{:S(2)}) %collective-permute-start) | collective-permute-done | bytes 589856 | tf_op jit(solution)/shard_map/ppermute | solution.py:340
  18.5 1.5 collective-permute-start.1
  19.9 2.6 %collective-permute-done.3.refs_4_ = bf16[192,1536]{1,0:T(8,128)(2,1)S(1)} collective-permute-done((bf16[192,1536]{1,0:T(8,128)(2,1)}, bf16[192,1536]{1,0:T(8,128)(2,1)S(1)}, u32[]{:S(2)}, u32[]{:S(2)}) %collective-permute-start.3) | collective-permute-done | bytes 589856 | tf_op jit(solution)/shard_map/ppermute | solution.py:341
  22.5 1.3 collective-permute-start.4
  23.8 0.0 collective-permute-done.1.refs_2_
  23.8 1.5 collective-permute-start.2
  25.3 13.9 %collective-permute-done.4.refs_5_ = bf16[192,1536]{1,0:T(8,128)(2,1)} collective-permute-done((bf16[192,1536]{1,0:T(8,128)(2,1)S(1)}, bf16[192,1536]{1,0:T(8,128)(2,1)}, u32[]{:S(2)}, u32[]{:S(2)}) %collective-permute-start.4) | collective-permute-done | bytes 589856 | tf_op jit(solution)/shard_map/ppermute | solution.py:341
  39.3 1.3 collective-permute-start.5
  40.6 3.5 %constant_dynamic-slice_fusion = (bf16[768,1152]{1,0:T(8,128)(2,1)S(1)}, bf16[768,1152]{1,0:T(8,128)(2,1)}) fusion(bf16[768,2304]{1,0:T(8,128)(2,1)} %param.20, s32[]{:T(128)S(6)} %select_n.53, s32[]{:T(128)S(6)} %select_n.52), kind=kLoop, calls=%fused_computation.26 | loop fusion | bytes 7077896 | tf_op jit(solution)/shard_map/dynamic_slice | solution.py:346
  44.1 0.0 collective-permute-start.13
  44.1 0.6 reshape.112
  44.7 1.3 reshape.114
  46.1 0.6 pad_add_fusion.place
  46.7 0.0 collective-permute-done.2.refs_3_
  46.7 8.1 %collective-permute-done.5.refs_6_ = bf16[192,1536]{1,0:T(8,128)(2,1)} collective-permute-done((bf16[192,1536]{1,0:T(8,128)(2,1)}, bf16[192,1536]{1,0:T(8,128)(2,1)}, u32[]{:S(2)}, u32[]{:S(2)}) %collective-permute-start.5) | collective-permute-done | bytes 589856 | tf_op jit(solution)/shard_map/ppermute | solution.py:341
  54.8 7.3 %norm.1 = (bf16[192,1536]{1,0:T(8,128)(2,1)}, bf16[192,1536]{1,0:T(8,128)(2,1)}, bf16[192,1536]{1,0:T(8,128)(2,1)}, bf16[192,1536]{1,0:T(8,128)(2,1)}) custom-call(s32[2]{0:T(128)} %pad_add_fusion.place, bf16[192,1536]{1,0:T(8,128)(2,1)} %bitcast.16, bf16[192,1536]{1,0:T(8,128)(2,1)} %copy-done.1, bf16[192,1536]{1,0:T(8,128)(2,1)} %collective-permute-done.1.refs_2_, ...), custom_call_target="tpu_custom_call" | custom-call | tf_op jit(solution)/shard_map/norm/pallas_call | solution.py:370
  62.1 1.6 collective-permute-start.9
  63.7 1.4 collective-permute-start.11
  65.1 0.5 collective-permute-start.7
  65.7 0.0 collective-permute-start.6
  65.7 21.7 %collective-permute-done.9 = bf16[192,1536]{1,0:T(8,128)(2,1)S(1)} collective-permute-done((bf16[192,1536]{1,0:T(8,128)(2,1)}, bf16[192,1536]{1,0:T(8,128)(2,1)S(1)}, u32[]{:S(2)}, u32[]{:S(2)}) %collective-permute-start.9) | collective-permute-done | bytes 589856 | tf_op jit(solution)/shard_map/ppermute | solution.py:332
  87.4 0.0 collective-permute-start.10
  87.4 0.0 collective-permute-done.11
  87.4 0.5 collective-permute-start.12
  87.9 0.7 collective-permute-done.7
  88.6 0.0 collective-permute-start.8
  88.6 0.2 convert_reduce_fusion
  88.8 0.2 select_reduce_fusion
  89.0 0.5 fusion.6.source
  89.5 0.0 collective-permute-done.13.refs_9_
  89.5 0.0 collective-permute-done.6
  89.6 0.0 collective-permute-done.10
  89.6 0.7 collective-permute-done.12
  90.2 0.8 collective-permute-done.8
  91.1 0.0 copy-done.3
  91.1 0.3 copy-done.8
  91.4 0.5 copy-done.9
  91.9 0.0 copy-start.22
  91.9 0.0 copy-start.23
  91.9 11.5 %project.1 = (bf16[192,1152]{1,0:T(8,128)(2,1)}, bf16[192,1152]{1,0:T(8,128)(2,1)}, bf16[192,1152]{1,0:T(8,128)(2,1)}, bf16[192,1152]{1,0:T(8,128)(2,1)}, bf16[1...) custom-call(s32[1]{0:T(128)} %bitcast.place, ...), custom_call_target="tpu_custom_call" | custom-call | tf_op jit(solution)/shard_map/project/pallas_call | solution.py:396
  103.4 0.2 collective-permute-start.14
  103.6 1.5 collective-permute-start.15
  105.2 0.2 collective-permute-start.16
  105.4 1.5 collective-permute-start.17
  106.9 0.3 collective-permute-start.18
  107.2 0.0 collective-permute-done.14.refs_1_
  107.2 2.4 %collective-permute-start.19 = (bf16[192,1152]{1,0:T(8,128)(2,1)}, bf16[192,1152]{1,0:T(8,128)(2,1)S(1)}, u32[]{:S(2)}, u32[]{:S(2)}) collective-permute-start(bf16[192,1152]{1,0:T(8,128)(2,1)} %get-tuple-element.25), channel_id=1, source_target_pairs={{0,24},{4,28},{8,16},{12,20},{16,8},{20,12},{24,0},{28,4},{1,25},{... | collective-permute-start | bytes 1327112 | tf_op jit(solution)/shard_map/ppermute | solution.py:332
  109.6 7.2 %collective-permute-done.15.refs_2_ = bf16[192,1152]{1,0:T(8,128)(2,1)S(1)} collective-permute-done((bf16[192,1152]{1,0:T(8,128)(2,1)}, bf16[192,1152]{1,0:T(8,128)(2,1)S(1)}, u32[]{:S(2)}, u32[]{:S(2)}) %collective-permute-start.15) | collective-permute-done | bytes 442400 | tf_op jit(solution)/shard_map/ppermute | solution.py:332
  116.9 1.0 collective-permute-start.20
  117.9 0.1 add_convert_fusion
  118.0 0.1 convert_element_type.18
  118.1 0.6 reshape.117.refs_8_
  118.7 3.4 %fusion = (f32[192,768]{1,0:T(8,128)}, f32[192,768]{1,0:T(8,128)}, f32[192,768]{1,0:T(8,128)}) fusion(f32[768]{0:T(1024)S(1)} %copy-done.19, f32[192]{0:T(256)S(1)} %convert_element_type.18, pred[768]{0:T(1024)(128)(4,1)S(1)} %copy-done.23, pred[768]{0:T(1024)(128)(4,1)S(1)} %copy-done.22, pred[768]{0:T(1024)(128)(4,1)S(1)} %copy-done.21), kind=kLoop, calls=%fused_computation.2 | loop fusion | flops 737280 | bytes 1775616 | tf_op jit(solution)/shard_map/jit(_where)/select_n | solution.py:368
  122.1 3.4 %collective-permute-done.16.refs_3_ = bf16[192,1152]{1,0:T(8,128)(2,1)S(1)} collective-permute-done((bf16[192,1152]{1,0:T(8,128)(2,1)}, bf16[192,1152]{1,0:T(8,128)(2,1)S(1)}, u32[]{:S(2)}, u32[]{:S(2)}) %collective-permute-start.16) | collective-permute-done | bytes 442400 | tf_op jit(solution)/shard_map/ppermute | solution.py:332
  125.5 0.0 collective-permute-done.17.refs_4_
  125.5 20.6 %collective-permute-done.18.refs_5_ = bf16[192,1152]{1,0:T(8,128)(2,1)S(1)} collective-permute-done((bf16[192,1152]{1,0:T(8,128)(2,1)}, bf16[192,1152]{1,0:T(8,128)(2,1)S(1)}, u32[]{:S(2)}, u32[]{:S(2)}) %collective-permute-start.18) | collective-permute-done | bytes 442400 | tf_op jit(solution)/shard_map/ppermute | solution.py:332
  146.1 0.0 collective-permute-done.19.refs_6_
  146.1 0.0 collective-permute-done.20.refs_7_
  146.1 0.7 copy-done.14
  146.8 0.1 copy-done.15
  147.0 0.2 copy-done.16
  147.2 14.0 %attend.1 = (bf16[4,48,768]{2,1,0:T(8,128)(2,1)}, bf16[4,48,768]{2,1,0:T(8,128)(2,1)}, bf16[4,48,768]{2,1,0:T(8,128)(2,1)}) custom-call(s32[1]{0:T(128)} %bitcast.place, s32[4]{0:T(128)} %lengths.1, s32[4,16]{1,0:T(4,128)} %table.1, bf16[192,1152]{1,0:T(8,128)(2,1)} %get-tuple-element.19.refs_0_, bf16[192,1152]{1,0:T(8,128)(2,1)} %copy-done.10, ...), custom_call_target="tpu_custom_call" | custom-call | tf_op jit(solution)/shard_map/attend/pallas_call | solution.py:422
  (43 shorter events, 0.1 us)
Async XLA Ops:
  0.6 17.8 %collective-permute-start = (bf16[192,1536]{1,0:T(8,128)(2,1)}, bf16[192,1536]{1,0:T(8,128)(2,1)S(1)}, u32[]{:S(2)}, u32[]{:S(2)}) collective-permute-start(bf16[192,1536]{1,0:T(8,128)(2,1)} %bitcast.14), channel_id=1, source_target_pairs={{0,1},{1,2},{2,3},{4,5},{5,6},{6,7},{8,9},{9,10},{10,11},{12,13},{... | collective-permute-start | bytes 1769480 | tf_op jit(solution)/shard_map/ppermute | solution.py:340
  5.6 16.9 %collective-permute-start.3 = (bf16[192,1536]{1,0:T(8,128)(2,1)}, bf16[192,1536]{1,0:T(8,128)(2,1)S(1)}, u32[]{:S(2)}, u32[]{:S(2)}) collective-permute-start(bf16[192,1536]{1,0:T(8,128)(2,1)} %bitcast.15), channel_id=1, source_target_pairs={{1,0},{2,1},{3,2},{5,4},{6,5},{7,6},{9,8},{10,9},{11,10},{13,12},{... | collective-permute-start | bytes 1769480 | tf_op jit(solution)/shard_map/ppermute | solution.py:341
  18.5 25.7 %copy-start.1 = (bf16[192,1536]{1,0:T(8,128)(2,1)}, bf16[192,1536]{1,0:T(8,128)(2,1)S(1)}, u32[]{:S(2)}) copy-start(bf16[192,1536]{1,0:T(8,128)(2,1)S(1)} %collective-permute-done.refs_1_) | copy-start | bytes 1769476
  18.5 5.4 %collective-permute-start.1 = (bf16[192,1536]{1,0:T(8,128)(2,1)S(1)}, bf16[192,1536]{1,0:T(8,128)(2,1)}, u32[]{:S(2)}, u32[]{:S(2)}) collective-permute-start(bf16[192,1536]{1,0:T(8,128)(2,1)S(1)} %collective-permute-done.refs_1_), channel_id=1, source_target_pairs={{1,2},{2,3},{5,6},{6,7},{9,10},{10,11},{13,14},{14,15},{17,18},{18... | collective-permute-start | bytes 1769480 | tf_op jit(solution)/shard_map/ppermute | solution.py:340
  22.5 21.6 %copy-start.2 = (bf16[192,1536]{1,0:T(8,128)(2,1)}, bf16[192,1536]{1,0:T(8,128)(2,1)S(1)}, u32[]{:S(2)}) copy-start(bf16[192,1536]{1,0:T(8,128)(2,1)S(1)} %collective-permute-done.3.refs_4_) | copy-start | bytes 1769476
  22.5 16.8 %collective-permute-start.4 = (bf16[192,1536]{1,0:T(8,128)(2,1)S(1)}, bf16[192,1536]{1,0:T(8,128)(2,1)}, u32[]{:S(2)}, u32[]{:S(2)}) collective-permute-start(bf16[192,1536]{1,0:T(8,128)(2,1)S(1)} %collective-permute-done.3.refs_4_), channel_id=1, source_target_pairs={{1,0},{2,1},{5,4},{6,5},{9,8},{10,9},{13,12},{14,13},{17,16},{18,1... | collective-permute-start | bytes 1769480 | tf_op jit(solution)/shard_map/ppermute | solution.py:341
  23.8 20.3 %copy-start.17 = (bf16[6144]{0:T(1024)(128)(2,1)S(1)}, bf16[6144]{0:T(1024)(128)(2,1)}, u32[]{:S(2)}) copy-start(bf16[6144]{0:T(1024)(128)(2,1)} %param.18) | copy-start | bytes 36868
  23.8 22.8 %collective-permute-start.2 = (bf16[192,1536]{1,0:T(8,128)(2,1)}, bf16[192,1536]{1,0:T(8,128)(2,1)}, u32[]{:S(2)}, u32[]{:S(2)}) collective-permute-start(bf16[192,1536]{1,0:T(8,128)(2,1)} %collective-permute-done.1.refs_2_), channel_id=1, source_target_pairs={{2,3},{6,7},{10,11},{14,15},{18,19},{22,23},{26,27},{30,31}} | collective-permute-start | bytes 1769480 | tf_op jit(solution)/shard_map/ppermute | solution.py:340
  39.3 15.5 %collective-permute-start.5 = (bf16[192,1536]{1,0:T(8,128)(2,1)}, bf16[192,1536]{1,0:T(8,128)(2,1)}, u32[]{:S(2)}, u32[]{:S(2)}) collective-permute-start(bf16[192,1536]{1,0:T(8,128)(2,1)} %collective-permute-done.4.refs_5_), channel_id=1, source_target_pairs={{1,0},{5,4},{9,8},{13,12},{17,16},{21,20},{25,24},{29,28}} | collective-permute-start | bytes 1769480 | tf_op jit(solution)/shard_map/ppermute | solution.py:341
  44.1 45.4 %collective-permute-start.13 = (bf16[768,1152]{1,0:T(8,128)(2,1)S(1)}, bf16[768,1152]{1,0:T(8,128)(2,1)S(1)}, u32[]{:S(2)}, u32[]{:S(2)}) collective-permute-start(bf16[768,1152]{1,0:T(8,128)(2,1)S(1)} %get-tuple-element.27), channel_id=1, source_target_pairs={{0,4},{4,0},{8,12},{12,8},{16,20},{20,16},{24,28},{28,24},{1,5},{5... | collective-permute-start | bytes 5308424 | tf_op jit(solution)/shard_map/ppermute | solution.py:332
  54.8 33.9 %copy-start.24 = (s32[32]{0:T(128)S(1)}, s32[32]{0:T(128)}, u32[]{:S(2)}) copy-start(s32[32]{0:T(128)} %param.15) | copy-start | bytes 388
  62.1 25.3 %collective-permute-start.9 = (bf16[192,1536]{1,0:T(8,128)(2,1)}, bf16[192,1536]{1,0:T(8,128)(2,1)S(1)}, u32[]{:S(2)}, u32[]{:S(2)}) collective-permute-start(bf16[192,1536]{1,0:T(8,128)(2,1)} %get-tuple-element.17), channel_id=1, source_target_pairs={{0,16},{4,20},{8,24},{12,28},{16,0},{20,4},{24,8},{28,12},{1,17},{... | collective-permute-start | bytes 1769480 | tf_op jit(solution)/shard_map/ppermute | solution.py:332
  63.7 23.7 %collective-permute-start.11 = (bf16[192,1536]{1,0:T(8,128)(2,1)}, bf16[192,1536]{1,0:T(8,128)(2,1)S(1)}, u32[]{:S(2)}, u32[]{:S(2)}) collective-permute-start(bf16[192,1536]{1,0:T(8,128)(2,1)} %get-tuple-element.18), channel_id=1, source_target_pairs={{0,24},{4,28},{8,16},{12,20},{16,8},{20,12},{24,0},{28,4},{1,25},{... | collective-permute-start | bytes 1769480 | tf_op jit(solution)/shard_map/ppermute | solution.py:332
  65.1 23.5 %collective-permute-start.7 = (bf16[192,1536]{1,0:T(8,128)(2,1)}, bf16[192,1536]{1,0:T(8,128)(2,1)S(1)}, u32[]{:S(2)}, u32[]{:S(2)}) collective-permute-start(bf16[192,1536]{1,0:T(8,128)(2,1)} %get-tuple-element.16), channel_id=1, source_target_pairs={{0,8},{4,12},{8,0},{12,4},{16,24},{20,28},{24,16},{28,20},{1,9},{5... | collective-permute-start | bytes 1769480 | tf_op jit(solution)/shard_map/ppermute | solution.py:332
  65.7 23.9 %collective-permute-start.6 = (bf16[192,1536]{1,0:T(8,128)(2,1)}, bf16[192,1536]{1,0:T(8,128)(2,1)S(1)}, u32[]{:S(2)}, u32[]{:S(2)}) collective-permute-start(bf16[192,1536]{1,0:T(8,128)(2,1)} %get-tuple-element.15), channel_id=1, source_target_pairs={{0,4},{4,0},{8,12},{12,8},{16,20},{20,16},{24,28},{28,24},{1,5},{5... | collective-permute-start | bytes 1769480 | tf_op jit(solution)/shard_map/ppermute | solution.py:332
  87.4 3.7 %copy-start.3 = (bf16[192,1536]{1,0:T(8,128)(2,1)}, bf16[192,1536]{1,0:T(8,128)(2,1)S(1)}, u32[]{:S(2)}) copy-start(bf16[192,1536]{1,0:T(8,128)(2,1)S(1)} %collective-permute-done.9) | copy-start | bytes 1769476
  87.4 2.2 %collective-permute-start.10 = (bf16[192,1536]{1,0:T(8,128)(2,1)S(1)}, bf16[192,1536]{1,0:T(8,128)(2,1)S(1)}, u32[]{:S(2)}, u32[]{:S(2)}) collective-permute-start(bf16[192,1536]{1,0:T(8,128)(2,1)S(1)} %collective-permute-done.9), channel_id=1, source_target_pairs={{0,4},{4,0},{8,12},{12,8},{16,20},{20,16},{24,28},{28,24},{1,5},{5... | collective-permute-start | bytes 1769480 | tf_op jit(solution)/shard_map/ppermute | solution.py:332
  87.4 3.7 %copy-start.4 = (bf16[192,1536]{1,0:T(8,128)(2,1)}, bf16[192,1536]{1,0:T(8,128)(2,1)S(1)}, u32[]{:S(2)}) copy-start(bf16[192,1536]{1,0:T(8,128)(2,1)S(1)} %collective-permute-done.11) | copy-start | bytes 1769476
  87.4 2.8 %collective-permute-start.12 = (bf16[192,1536]{1,0:T(8,128)(2,1)S(1)}, bf16[192,1536]{1,0:T(8,128)(2,1)S(1)}, u32[]{:S(2)}, u32[]{:S(2)}) collective-permute-start(bf16[192,1536]{1,0:T(8,128)(2,1)S(1)} %collective-permute-done.11), channel_id=1, source_target_pairs={{0,4},{4,0},{8,12},{12,8},{16,20},{20,16},{24,28},{28,24},{1,5},{5... | collective-permute-start | bytes 1769480 | tf_op jit(solution)/shard_map/ppermute | solution.py:332
  88.6 2.5 %copy-start.5 = (bf16[192,1536]{1,0:T(8,128)(2,1)}, bf16[192,1536]{1,0:T(8,128)(2,1)S(1)}, u32[]{:S(2)}) copy-start(bf16[192,1536]{1,0:T(8,128)(2,1)S(1)} %collective-permute-done.7) | copy-start | bytes 1769476
  88.6 2.5 %collective-permute-start.8 = (bf16[192,1536]{1,0:T(8,128)(2,1)S(1)}, bf16[192,1536]{1,0:T(8,128)(2,1)S(1)}, u32[]{:S(2)}, u32[]{:S(2)}) collective-permute-start(bf16[192,1536]{1,0:T(8,128)(2,1)S(1)} %collective-permute-done.7), channel_id=1, source_target_pairs={{0,4},{4,0},{8,12},{12,8},{16,20},{20,16},{24,28},{28,24},{1,5},{5... | collective-permute-start | bytes 1769480 | tf_op jit(solution)/shard_map/ppermute | solution.py:332
  89.5 1.6 copy-start
  89.5 1.6 copy-start.6
  89.6 1.5 copy-start.7
  90.2 1.1 copy-start.8
  91.1 0.8 copy-start.9
  91.9 26.0 %copy-start.20 = (s32[4]{0:T(128)S(1)}, s32[4]{0:T(128)}, u32[]{:S(2)}) copy-start(s32[4]{0:T(128)} %lengths.1) | copy-start | bytes 52
  91.9 26.2 %copy-start.18 = (bf16[2304]{0:T(1024)(128)(2,1)S(1)}, bf16[2304]{0:T(1024)(128)(2,1)}, u32[]{:S(2)}) copy-start(bf16[2304]{0:T(1024)(128)(2,1)} %param.21) | copy-start | bytes 13828
  91.9 26.8 %copy-start.19 = (f32[768]{0:T(1024)S(1)}, f32[768]{0:T(1024)}, u32[]{:S(2)}) copy-start(f32[768]{0:T(1024)} %constant.87) | copy-start | bytes 9220
  91.9 26.8 %copy-start.21 = (pred[768]{0:T(1024)(128)(4,1)S(1)}, pred[768]{0:T(1024)(128)(4,1)}, u32[]{:S(2)}) copy-start(pred[768]{0:T(1024)(128)(4,1)} %constant.79.clone) | copy-start | bytes 2308
  91.9 26.8 %copy-start.22 = (pred[768]{0:T(1024)(128)(4,1)S(1)}, pred[768]{0:T(1024)(128)(4,1)}, u32[]{:S(2)}) copy-start(pred[768]{0:T(1024)(128)(4,1)} %constant.80.clone) | copy-start | bytes 2308
  91.9 26.8 %copy-start.23 = (pred[768]{0:T(1024)(128)(4,1)S(1)}, pred[768]{0:T(1024)(128)(4,1)}, u32[]{:S(2)}) copy-start(pred[768]{0:T(1024)(128)(4,1)} %constant.88) | copy-start | bytes 2308
  103.4 3.7 %collective-permute-start.14 = (bf16[192,1152]{1,0:T(8,128)(2,1)}, bf16[192,1152]{1,0:T(8,128)(2,1)S(1)}, u32[]{:S(2)}, u32[]{:S(2)}) collective-permute-start(bf16[192,1152]{1,0:T(8,128)(2,1)} %get-tuple-element.20), channel_id=1, source_target_pairs={{0,4},{4,0},{8,12},{12,8},{16,20},{20,16},{24,28},{28,24},{1,5},{5... | collective-permute-start | bytes 1327112 | tf_op jit(solution)/shard_map/ppermute | solution.py:332
  103.6 13.2 %collective-permute-start.15 = (bf16[192,1152]{1,0:T(8,128)(2,1)}, bf16[192,1152]{1,0:T(8,128)(2,1)S(1)}, u32[]{:S(2)}, u32[]{:S(2)}) collective-permute-start(bf16[192,1152]{1,0:T(8,128)(2,1)} %get-tuple-element.21), channel_id=1, source_target_pairs={{0,8},{4,12},{8,0},{12,4},{16,24},{20,28},{24,16},{28,20},{1,9},{5... | collective-permute-start | bytes 1327112 | tf_op jit(solution)/shard_map/ppermute | solution.py:332
  105.2 20.3 %collective-permute-start.16 = (bf16[192,1152]{1,0:T(8,128)(2,1)}, bf16[192,1152]{1,0:T(8,128)(2,1)S(1)}, u32[]{:S(2)}, u32[]{:S(2)}) collective-permute-start(bf16[192,1152]{1,0:T(8,128)(2,1)} %get-tuple-element.22), channel_id=1, source_target_pairs={{0,12},{4,8},{8,4},{12,0},{16,28},{20,24},{24,20},{28,16},{1,13},{... | collective-permute-start | bytes 1327112 | tf_op jit(solution)/shard_map/ppermute | solution.py:332
  105.4 20.1 %collective-permute-start.17 = (bf16[192,1152]{1,0:T(8,128)(2,1)}, bf16[192,1152]{1,0:T(8,128)(2,1)S(1)}, u32[]{:S(2)}, u32[]{:S(2)}) collective-permute-start(bf16[192,1152]{1,0:T(8,128)(2,1)} %get-tuple-element.23), channel_id=1, source_target_pairs={{0,16},{4,20},{8,24},{12,28},{16,0},{20,4},{24,8},{28,12},{1,17},{... | collective-permute-start | bytes 1327112 | tf_op jit(solution)/shard_map/ppermute | solution.py:332
  106.9 39.2 %collective-permute-start.18 = (bf16[192,1152]{1,0:T(8,128)(2,1)}, bf16[192,1152]{1,0:T(8,128)(2,1)S(1)}, u32[]{:S(2)}, u32[]{:S(2)}) collective-permute-start(bf16[192,1152]{1,0:T(8,128)(2,1)} %get-tuple-element.24), channel_id=1, source_target_pairs={{0,20},{4,16},{8,28},{12,24},{16,4},{20,0},{24,12},{28,8},{1,21},{... | collective-permute-start | bytes 1327112 | tf_op jit(solution)/shard_map/ppermute | solution.py:332
  107.2 38.9 %copy-start.10 = (bf16[192,1152]{1,0:T(8,128)(2,1)}, bf16[192,1152]{1,0:T(8,128)(2,1)S(1)}, u32[]{:S(2)}) copy-start(bf16[192,1152]{1,0:T(8,128)(2,1)S(1)} %collective-permute-done.14.refs_1_) | copy-start | bytes 1327108
  107.2 38.9 %collective-permute-start.19 = (bf16[192,1152]{1,0:T(8,128)(2,1)}, bf16[192,1152]{1,0:T(8,128)(2,1)S(1)}, u32[]{:S(2)}, u32[]{:S(2)}) collective-permute-start(bf16[192,1152]{1,0:T(8,128)(2,1)} %get-tuple-element.25), channel_id=1, source_target_pairs={{0,24},{4,28},{8,16},{12,20},{16,8},{20,12},{24,0},{28,4},{1,25},{... | collective-permute-start | bytes 1327112 | tf_op jit(solution)/shard_map/ppermute | solution.py:332
  116.9 29.3 %copy-start.11 = (bf16[192,1152]{1,0:T(8,128)(2,1)}, bf16[192,1152]{1,0:T(8,128)(2,1)S(1)}, u32[]{:S(2)}) copy-start(bf16[192,1152]{1,0:T(8,128)(2,1)S(1)} %collective-permute-done.15.refs_2_) | copy-start | bytes 1327108
  116.9 29.2 %collective-permute-start.20 = (bf16[192,1152]{1,0:T(8,128)(2,1)}, bf16[192,1152]{1,0:T(8,128)(2,1)S(1)}, u32[]{:S(2)}, u32[]{:S(2)}) collective-permute-start(bf16[192,1152]{1,0:T(8,128)(2,1)} %get-tuple-element.26), channel_id=1, source_target_pairs={{0,28},{4,24},{8,20},{12,16},{16,12},{20,8},{24,4},{28,0},{1,29},{... | collective-permute-start | bytes 1327112 | tf_op jit(solution)/shard_map/ppermute | solution.py:332
  125.5 20.7 %copy-start.12 = (bf16[192,1152]{1,0:T(8,128)(2,1)}, bf16[192,1152]{1,0:T(8,128)(2,1)S(1)}, u32[]{:S(2)}) copy-start(bf16[192,1152]{1,0:T(8,128)(2,1)S(1)} %collective-permute-done.16.refs_3_) | copy-start | bytes 1327108
  125.5 20.7 %copy-start.13 = (bf16[192,1152]{1,0:T(8,128)(2,1)}, bf16[192,1152]{1,0:T(8,128)(2,1)S(1)}, u32[]{:S(2)}) copy-start(bf16[192,1152]{1,0:T(8,128)(2,1)S(1)} %collective-permute-done.17.refs_4_) | copy-start | bytes 1327108
  146.1 0.8 copy-start.14
  146.1 0.9 copy-start.15
  146.1 1.1 copy-start.16

commit v2 on v1

--- a/solution.py
+++ b/solution.py
@@ -15,11 +15,86 @@
 LANES = 128
 WINDOW = 2 * LANES
 CHUNK_PAGES = 4
-VMEM_LIMIT = 56 * 1024 * 1024
+MIB = 1024 * 1024
 
 ANY = pl.BlockSpec(memory_space=pl.ANY)
 SMEM = pl.BlockSpec(memory_space=pltpu.SMEM)
 VMEM = pl.BlockSpec(memory_space=pltpu.VMEM)
+
+
+def plan_kernel(req_count, place, group_of, arrivals, slots, sources, *refs):
+    chunks = refs[:2]
+    order, slot_of, color, filled, sems = refs[2:]
+    everyone = group_of.shape[0]
+    groups = everyone // req_count
+    half = req_count // 2
+    me = place[0]
+
+    def clear(group, carry):
+        filled[group] = 0
+        return carry
+
+    lax.fori_loop(0, groups, clear, 0)
+
+    def rank(item, carry):
+        group = group_of[item]
+        slot = group * req_count + filled[group]
+        filled[group] = filled[group] + 1
+        slot_of[item] = slot
+        order[slot] = item
+        color[item] = -1
+        return carry
+
+    lax.fori_loop(0, everyone, rank, 0)
+
+    def walk(pair, carry):
+        def body(state):
+            item = state[0]
+            color[item] = 0
+            color[item ^ 1] = 1
+            following = order[slot_of[item ^ 1] ^ 1]
+            return following, color[following]
+
+        lax.while_loop(lambda state: state[1] < 0, body, (2 * pair, color[2 * pair]))
+        return carry
+
+    lax.fori_loop(0, everyone // 2, walk, 0)
+
+    copies = []
+    for pair in range(half):
+        first = color[me * req_count + 2 * pair]
+        for part in range(2):
+            copies.append(
+                pltpu.make_async_copy(
+                    arrivals.at[2 * pair + (first ^ part)],
+                    chunks[part].at[pair],
+                    sems.at[part * half + pair],
+                )
+            )
+    for copy in copies:
+        copy.start()
+
+    def pick(group, pair, part):
+        begin = group * req_count + 2 * pair
+        return 2 * pair + (color[order[begin]] ^ part)
+
+    for pair in range(half):
+        for part in range(2):
+            slots[part * half + pair] = pick(me, pair, part)
+
+    def trace(distance, carry):
+        group = me ^ distance
+        for pair in range(half):
+            for part in range(2):
+                item = order[group * req_count + pick(group, pair, part)]
+                origin = lax.div(item, req_count) ^ me
+                within = lax.div(lax.rem(item, req_count), 2)
+                sources[(part * groups + distance) * half + pair] = origin * half + within
+        return carry
+
+    lax.fori_loop(0, groups, trace, 0)
+    for copy in copies:
+        copy.wait()
 
 
 def norm_kernel(depth, chips, place, *refs):
@@ -80,7 +155,7 @@
     lax.fori_loop(0, rows // step, body, 0)
 
 
-def project_kernel(fresh_len, req_count, place, source, *refs):
+def project_kernel(fresh_len, held_count, part, place, source, *refs):
     groups = (len(refs) - 7) // 2
     tokens = refs[:groups]
     own_rows, other_rows = refs[groups : groups + 2]
@@ -90,65 +165,66 @@
     depth = own_rows.shape[0]
     copies = [
         pltpu.make_async_copy(
-            token, held.at[pl.ds(index * req_count, req_count)], sems.at[index]
-        )
-        for index, token in enumerate(tokens)
-    ]
-    copies.append(
-        pltpu.make_async_copy(
             own_rows,
             weights.at[pl.ds(pl.multiple_of(core * depth, 16), depth)],
             weight_sems.at[0],
-        )
-    )
-    copies.append(
+        ),
         pltpu.make_async_copy(
             other_rows,
             weights.at[pl.ds(pl.multiple_of((1 - core) * depth, 16), depth)],
             weight_sems.at[1],
-        )
-    )
+        ),
+    ]
+    copies += [
+        pltpu.make_async_copy(
+            token, held.at[pl.ds(index * held_count, held_count)], sems.at[index]
+        )
+        for index, token in enumerate(tokens)
+    ]
     for copy in copies:
         copy.start()
     for copy in copies:
         copy.wait()
-    rows = req_count * fresh_len
-    for pair in range(groups // 2):
-        for item in range(2 * req_count):
+    rows = held_count * fresh_len
+    together = min(groups, 4)
+    for first in range(0, groups, together):
+        for item in range(together * held_count):
             picked[item * fresh_len : (item + 1) * fresh_len, :] = held[
-                source[pair * 2 * req_count + item]
+                source[(part * groups + first) * held_count + item]
             ]
         result = jnp.dot(picked[...], weights[...], preferred_element_type=jnp.float32).astype(
             jnp.bfloat16
         )
-        outs[2 * pair][...] = result[:rows]
-        outs[2 * pair + 1][...] = result[rows:]
-
-
-def attend_kernel(shape, place, lengths, table, *refs):
-    groups, req_count, fresh_len, page, heads = shape
+        for index in range(together):
+            outs[first + index][...] = result[index * rows : (index + 1) * rows]
+
+
+def attend_kernel(shape, place, slots, all_lengths, table, *refs):
+    groups, held_count, fresh_len, page, heads, part = shape
     parts = refs[:groups]
     bias, cosine, sine_up, sine_down, key_pool, value_pool = refs[groups : groups + 6]
-    attended, new_keys, new_values = refs[groups + 6 : groups + 9]
-    keys, values, sems = refs[groups + 9 :]
+    outs = refs[-9:-6]
+    keys, values, ready, sems, out_sems, new_sems = refs[-6:]
     core = place[0]
     chunk = CHUNK_PAGES * page
     pairs = heads // 2
 
-    counts = [pl.cdiv(lengths[index], chunk) for index in range(req_count)]
+    slot = [slots[part * held_count + index] for index in range(held_count)]
+    lengths = [all_lengths[slot[index]] for index in range(held_count)]
+    counts = [pl.cdiv(lengths[index], chunk) for index in range(held_count)]
     bases = [jnp.int32(0)]
     for count in counts[:-1]:
         bases.append(bases[-1] + count * CHUNK_PAGES)
 
     def copies(index, entry):
-        number = table[index, entry]
-        slot = bases[index] + entry
+        number = table[slot[index], entry]
+        to = bases[index] + entry
         return (
-            pltpu.make_async_copy(key_pool.at[number], keys.at[slot], sems.at[index]),
-            pltpu.make_async_copy(value_pool.at[number], values.at[slot], sems.at[index]),
-        )
-
-    for index in range(req_count):
+            pltpu.make_async_copy(key_pool.at[number], keys.at[to], sems.at[index]),
+            pltpu.make_async_copy(value_pool.at[number], values.at[to], sems.at[index]),
+        )
+
+    for index in range(held_count):
 
         def start(entry, carry, index=index):
             for copy in copies(index, entry):
@@ -175,21 +251,35 @@
 
     width = heads * HEAD
 
+    def rows_of(ref):
+        return jnp.concatenate([ref[slot[index]] for index in range(held_count)], axis=0)
+
+    cosine, sine_up, sine_down = rows_of(cosine), rows_of(sine_up), rows_of(sine_down)
+
     def turn(block):
         half_rot = ROT // 2
         return (
-            block * cosine[...]
-            + pltpu.roll(block, width - half_rot, 1) * sine_up[...]
-            + pltpu.roll(block, half_rot, 1) * sine_down[...]
+            block * cosine
+            + pltpu.roll(block, width - half_rot, 1) * sine_up
+            + pltpu.roll(block, half_rot, 1) * sine_down
         )
 
     queries = turn(kind(0)).astype(jnp.bfloat16)
     turned = turn(kind(1)).astype(jnp.bfloat16)
     plain = kind(2).astype(jnp.bfloat16)
-    for index in range(req_count):
+    for index in range(held_count):
         rows = slice(index * fresh_len, (index + 1) * fresh_len)
-        new_keys[index] = turned[rows]
-        new_values[index] = plain[rows]
+        ready[1, index] = turned[rows]
+        ready[2, index] = plain[rows]
+    new_copies = [
+        pltpu.make_async_copy(
+            ready.at[which, index], outs[which].at[slot[index]], new_sems.at[which - 1, index]
+        )
+        for which in (1, 2)
+        for index in range(held_count)
+    ]
+    for copy in new_copies:
+        copy.start()
 
     factor = 1.0 / math.sqrt(HEAD) / math.log(2.0)
     starts = [(2 * HEAD * pair) // LANES * LANES for pair in range(pairs)]
@@ -210,7 +300,7 @@
     causal_pair = lax.rem(row, fresh_len) >= lax.broadcasted_iota(
         jnp.int32, (2 * fresh_len, fresh_len), 1
     )
-    for index in range(req_count):
+    for index in range(held_count):
         rows = slice(index * fresh_len, (index + 1) * fresh_len)
         spread = []
         for pair in range(pairs):
@@ -297,7 +387,15 @@
                     place_at = starts[pair] // LANES + side
                     tile = part[:, side * LANES : (side + 1) * LANES]
                     tiles[place_at] = tile if tiles[place_at] is None else tiles[place_at] + tile
-        attended[index] = jnp.concatenate(tiles, axis=1).astype(jnp.bfloat16)
+        ready[0, index] = jnp.concatenate(tiles, axis=1).astype(jnp.bfloat16)
+        new_copies.append(
+            pltpu.make_async_copy(
+                ready.at[0, index], outs[0].at[slot[index]], out_sems.at[index]
+            )
+        )
+        new_copies[-1].start()
+    for copy in new_copies:
+        copy.wait()
 
 
 def per_device(
@@ -333,26 +431,30 @@
             value, "req", [(device, device ^ distance) for device in range(req_size)]
         )
 
-    own = arrivals.reshape(rows, width)
-    upward, downward = [], []
-    up = down = own
-    for hop in range(1, wgt_size):
-        up = lax.ppermute(up, "wgt", [(at, at + 1) for at in range(hop - 1, wgt_size - 1)])
-        down = lax.ppermute(down, "wgt", [(at + 1, at) for at in range(wgt_size - hop)])
-        upward.append(up)
-        downward.append(down)
-
     own_rows = lax.dynamic_slice_in_dim(w_qkv, core * half_cols, half_cols, 1)
     other_rows = swap(lax.dynamic_slice_in_dim(w_qkv, (1 - core) * half_cols, half_cols, 1), 1)
 
-    ids = jnp.arange(everyone, dtype=jnp.int32)
-    same_group = group_of[:, None] == group_of[None, :]
-    earlier = ids[None, :] < ids[:, None]
-    rank = jnp.sum((same_group & earlier).astype(jnp.int32), axis=1)
-    slot_of = group_of * req_count + rank
-    target = (me ^ (ids // req_count)) * req_count + ids % req_count
-    order = jnp.sum(jnp.where(slot_of[None, :] == target[:, None], ids[None, :], 0), axis=1)
-    source = ((order // req_count) ^ me) * req_count + order % req_count
+    half = req_count // 2
+    piece = jax.ShapeDtypeStruct((half, fresh_len, width), jnp.bfloat16)
+    slots, sources, *chunks = pl.pallas_call(
+        functools.partial(plan_kernel, req_count),
+        out_shape=[
+            jax.ShapeDtypeStruct((2 * half,), jnp.int32),
+            jax.ShapeDtypeStruct((2 * req_size * half,), jnp.int32),
+            piece,
+            piece,
+        ],
+        in_specs=[SMEM, SMEM, ANY],
+        out_specs=[SMEM, SMEM, ANY, ANY],
+        scratch_shapes=[
+            pltpu.SMEM((everyone,), jnp.int32),
+            pltpu.SMEM((everyone,), jnp.int32),
+            pltpu.SMEM((everyone,), jnp.int32),
+            pltpu.SMEM((req_size,), jnp.int32),
+            pltpu.SemaphoreType.DMA((2 * half,)),
+        ],
+        name="plan",
+    )(jnp.stack([me]).astype(jnp.int32), group_of, arrivals)
 
     lane = np.arange(heads * HEAD) % HEAD
     half_rot = ROT // 2
@@ -367,82 +469,101 @@
     sine_up = jnp.where(jnp.asarray(lane < half_rot)[None, :], -sine, 0.0)
     sine_down = jnp.where(turns & jnp.asarray(lane >= half_rot)[None, :], sine, 0.0)
 
-    normed = pl.pallas_call(
-        functools.partial(norm_kernel, wgt_size, chips),
-        out_shape=[jax.ShapeDtypeStruct((rows, block), jnp.bfloat16)] * chips,
-        in_specs=[SMEM] + [ANY] * (2 * wgt_size - 1) + [VMEM] * 2,
-        out_specs=[VMEM] * chips,
-        scratch_shapes=[
-            pltpu.VMEM((wgt_size, rows, width), jnp.bfloat16),
-            pltpu.SemaphoreType.DMA((2 * wgt_size - 1,)),
-        ],
-        compiler_params=pltpu.CompilerParams(vmem_limit_bytes=VMEM_LIMIT),
-        name="norm",
-    )(
-        jnp.stack([layer, chip]).astype(jnp.int32),
-        own,
-        *upward,
-        *downward,
-        ln_gain.astype(jnp.float32).reshape(chips, 1, block),
-        ln_bias.astype(jnp.float32).reshape(chips, 1, block),
-    )
-
-    tokens = []
-    for distance in range(chips):
-        mine = normed[distance] if distance == 0 else swap(normed[distance], 2 * distance)
-        tokens += [mine, swap(mine, 1)]
-
+    tables = [
+        value.reshape(req_count, fresh_len, heads * HEAD)
+        for value in (cosine, sine_up, sine_down)
+    ]
+    gain = ln_gain.astype(jnp.float32).reshape(chips, 1, block)
+    shift = ln_bias.astype(jnp.float32).reshape(chips, 1, block)
+    bias = qkv_bias.astype(jnp.float32).reshape(1, local_cols)
     place = jnp.stack([core]).astype(jnp.int32)
-    partial = pl.pallas_call(
-        functools.partial(project_kernel, fresh_len, req_count),
-        out_shape=[jax.ShapeDtypeStruct((rows, half_cols), jnp.bfloat16)] * req_size,
-        in_specs=[SMEM] * 2 + [ANY] * (req_size + 2),
-        out_specs=[VMEM] * req_size,
-        scratch_shapes=[
-            pltpu.VMEM((everyone, fresh_len, block), jnp.bfloat16),
-            pltpu.VMEM((block, half_cols), jnp.bfloat16),
-            pltpu.VMEM((2 * rows, block), jnp.bfloat16),
-            pltpu.SemaphoreType.DMA((req_size,)),
-            pltpu.SemaphoreType.DMA((2,)),
-        ],
-        compiler_params=pltpu.CompilerParams(vmem_limit_bytes=VMEM_LIMIT),
-        name="project",
-    )(
-        place,
-        source,
-        *[token.reshape(req_count, fresh_len, block) for token in tokens],
-        own_rows,
-        other_rows,
-    )
-
-    parts = [partial[0]] + [swap(partial[distance], distance) for distance in range(1, req_size)]
-
-    slots = page_table.shape[1] * (req_count + 1) // 2
+    where = jnp.stack([layer, chip]).astype(jnp.int32)
+    chunk_rows = half * fresh_len
+    span = page_table.shape[1]
+    pages = span + (half - 1) * (span // 2)
     out = jax.ShapeDtypeStruct((req_count, fresh_len, heads * HEAD), jnp.bfloat16)
-    return pl.pallas_call(
-        functools.partial(attend_kernel, (req_size, req_count, fresh_len, page, heads)),
-        out_shape=[out] * 3,
-        in_specs=[SMEM] * 3 + [VMEM] * (req_size + 4) + [ANY] * 2,
-        out_specs=[VMEM] * 3,
-        scratch_shapes=[
-            pltpu.VMEM((slots, page, heads * HEAD), jnp.bfloat16),
-            pltpu.VMEM((slots, page, heads * HEAD), jnp.bfloat16),
-            pltpu.SemaphoreType.DMA((req_count,)),
-        ],
-        compiler_params=pltpu.CompilerParams(vmem_limit_bytes=VMEM_LIMIT),
-        name="attend",
-    )(
-        place,
-        lengths,
-        page_table,
-        *parts,
-        qkv_bias.astype(jnp.float32).reshape(1, local_cols),
-        cosine,
-        sine_up,
-        sine_down,
-        key_pool,
-        value_pool,
-    )
+
+    pieces = [[chunk.reshape(chunk_rows, width)] for chunk in chunks]
+    ends = [(own[0], own[0]) for own in pieces]
+    downs = [[], []]
+    for hop in range(1, wgt_size):
+        for part in range(2):
+            up, down = ends[part]
+            up = lax.ppermute(up, "wgt", [(at, at + 1) for at in range(hop - 1, wgt_size - 1)])
+            down = lax.ppermute(down, "wgt", [(at + 1, at) for at in range(wgt_size - hop)])
+            ends[part] = (up, down)
+            pieces[part].append(up)
+            downs[part].append(down)
+
+    results = []
+    for part in range(2):
+        normed = pl.pallas_call(
+            functools.partial(norm_kernel, wgt_size, chips),
+            out_shape=[jax.ShapeDtypeStruct((chunk_rows, block), jnp.bfloat16)] * chips,
+            in_specs=[SMEM] + [ANY] * (2 * wgt_size - 1) + [VMEM] * 2,
+            out_specs=[VMEM] * chips,
+            scratch_shapes=[
+                pltpu.VMEM((wgt_size, chunk_rows, width), jnp.bfloat16),
+                pltpu.SemaphoreType.DMA((2 * wgt_size - 1,)),
+            ],
+            compiler_params=pltpu.CompilerParams(vmem_limit_bytes=12 * MIB),
+            name="norm",
+        )(where, *pieces[part], *downs[part], gain, shift)
+
+        tokens = []
+        for distance in range(chips):
+            mine = normed[distance] if distance == 0 else swap(normed[distance], 2 * distance)
+            tokens += [mine, swap(mine, 1)]
+
+        partial = pl.pallas_call(
+            functools.partial(project_kernel, fresh_len, half, part),
+            out_shape=[jax.ShapeDtypeStruct((chunk_rows, half_cols), jnp.bfloat16)] * req_size,
+            in_specs=[SMEM] * 2 + [ANY] * (req_size + 2),
+            out_specs=[VMEM] * req_size,
+            scratch_shapes=[
+                pltpu.VMEM((req_size * half, fresh_len, block), jnp.bfloat16),
+                pltpu.VMEM((block, half_cols), jnp.bfloat16),
+                pltpu.VMEM((min(req_size, 4) * chunk_rows, block), jnp.bfloat16),
+                pltpu.SemaphoreType.DMA((req_size,)),
+                pltpu.SemaphoreType.DMA((2,)),
+            ],
+            compiler_params=pltpu.CompilerParams(vmem_limit_bytes=20 * MIB),
+            name="project",
+        )(
+            place,
+            sources,
+            *[token.reshape(half, fresh_len, block) for token in tokens],
+            own_rows,
+            other_rows,
+        )
+
+        parts = [partial[0]]
+        parts += [swap(partial[distance], distance) for distance in range(1, req_size)]
+
+        operands = [
+            place, slots, lengths, page_table, *parts, bias, *tables, key_pool, value_pool
+        ]
+        specs = [SMEM] * 4 + [VMEM] * (req_size + 4) + [ANY] * 2
+        results = pl.pallas_call(
+            functools.partial(
+                attend_kernel, (req_size, half, fresh_len, page, heads, part)
+            ),
+            out_shape=[out] * 3,
+            in_specs=specs + [ANY] * len(results),
+            out_specs=[ANY] * 3,
+            scratch_shapes=[
+                pltpu.VMEM((pages, page, heads * HEAD), jnp.bfloat16),
+                pltpu.VMEM((pages, page, heads * HEAD), jnp.bfloat16),
+                pltpu.VMEM((3, half, fresh_len, heads * HEAD), jnp.bfloat16),
+                pltpu.SemaphoreType.DMA((half,)),
+                pltpu.SemaphoreType.DMA((half,)),
+                pltpu.SemaphoreType.DMA((2, half)),
+            ],
+            input_output_aliases={len(specs) + index: index for index in range(len(results))},
+            compiler_params=pltpu.CompilerParams(vmem_limit_bytes=24 * MIB),
+            name="attend",
+        )(*operands, *results)
+    return results
 
 
 def solution(mesh):

time: 162 us -> 176 us (1.086)
  the two profiles are of different devices: /device:TPU:0 before, /device:TPU:5 now
where the time goes in v2:
time: 176 us; the launch traced here: 174 us
  Pallas kernels  71.2 us (40%)
  starting transfers between devices  58.5 us (33%)
  waiting for transfers between devices  32 us (18%)
  local copies, waits for them, and re-layouts  7.82 us (4%)
  other arithmetic  3.1 us (2%)
    ppermute x29, starting transfers between devices, swap(): lax.ppermute(value, 'req', [(device, device ^ distance) for device in ran...  37 us
    pallas_call x2, Pallas kernels, per_device(): pl.pallas_call(functools.partial(attend_kernel, (req_size, half, fresh_le...  32.6 us
    pallas_call x1, Pallas kernels, per_device(): pl.pallas_call(functools.partial(plan_kernel, req_count), out_shape=[jax....  21.1 us
    ppermute x6, waiting for transfers between devices, per_device(): lax.ppermute(down, 'wgt', [(at + 1, at) for at in range(wgt_size - hop)])  15.4 us
    ppermute x29, waiting for transfers between devices, swap(): lax.ppermute(value, 'req', [(device, device ^ distance) for device in ran...  14.9 us
    ppermute x6, starting transfers between devices, per_device(): lax.ppermute(up, 'wgt', [(at, at + 1) for at in range(hop - 1, wgt_size -...  13.8 us
    pallas_call x2, Pallas kernels, per_device(): pl.pallas_call(functools.partial(project_kernel, fresh_len, half, part),...  10.2 us
    ppermute x6, starting transfers between devices, per_device(): lax.ppermute(down, 'wgt', [(at + 1, at) for at in range(wgt_size - hop)])  7.68 us
  transfers between devices with their start and end apart: 41, of which 9 were waited for; matrix products, arithmetic and copies ran while one was open for 4% of the time, Pallas kernels for 20%

profile of v2, /device:TPU:5, one launch (start us, length us, event | category | flops | bytes accessed | tf_op | source)
XLA Modules:
  0.0 173.8 jit_solution(6750682410796956615)
XLA Ops:
  0.6 21.1 %plan.1 = (s32[4]{0:T(128)}, s32[32]{0:T(128)}, bf16[2,48,1536]{2,1,0:T(8,128)(2,1)}, bf16[2,48,1536]{2,1,0:T(8,128)(2,1)}) custom-call(s32[1]{0:T(128)} %bitcast.1.place, s32[32]{0:T(128)} %group_of.1, bf16[4,48,1536]{2,1,0:T(8,128)(2,1)} %arrivals.1), custom_call_target="tpu_custom_call" | custom-call | tf_op jit(solution)/shard_map/plan/pallas_call | solution.py:439
  21.8 3.9 %collective-permute-start.21 = (bf16[96,1536]{1,0:T(8,128)(2,1)}, bf16[96,1536]{1,0:T(8,128)(2,1)}, u32[]{:S(2)}, u32[]{:S(2)}) collective-permute-start(bf16[96,1536]{1,0:T(8,128)(2,1)} %bitcast.33), channel_id=1, source_target_pairs={{0,1},{1,2},{2,3},{4,5},{5,6},{6,7},{8,9},{9,10},{10,11},{12,13},{... | collective-permute-start | bytes 884744 | tf_op jit(solution)/shard_map/ppermute | solution.py:492
  25.7 1.3 collective-permute-start.24
  27.0 0.0 copy-start.1
  27.0 3.6 %constant_dynamic-slice_fusion = (bf16[768,1152]{1,0:T(8,128)(2,1)}, bf16[768,1152]{1,0:T(8,128)(2,1)S(1)}) fusion(bf16[768,2304]{1,0:T(8,128)(2,1)} %param.20, s32[]{:T(128)S(6)} %select_n.20, s32[]{:T(128)S(6)} %select_n.19), kind=kLoop, calls=%fused_computation.8 | loop fusion | bytes 7077896 | tf_op jit(solution)/shard_map/dynamic_slice | solution.py:435
  30.6 1.0 collective-permute-start.13
  31.5 5.0 %collective-permute-start = (bf16[96,1536]{1,0:T(8,128)(2,1)S(1)}, bf16[96,1536]{1,0:T(8,128)(2,1)}, u32[]{:S(2)}, u32[]{:S(2)}) collective-permute-start(bf16[96,1536]{1,0:T(8,128)(2,1)S(1)} %bitcast.26), channel_id=1, source_target_pairs={{0,1},{1,2},{2,3},{4,5},{5,6},{6,7},{8,9},{9,10},{10,11},{12,13},{... | collective-permute-start | bytes 884744 | tf_op jit(solution)/shard_map/ppermute | solution.py:492
  36.5 1.3 collective-permute-start.3
  37.8 1.4 collective-permute-start.22
  39.2 1.3 collective-permute-start.25
  40.5 1.7 collective-permute-done.refs_1_
  42.2 1.4 collective-permute-start.1
  43.6 3.3 %collective-permute-done.3.refs_4_ = bf16[96,1536]{1,0:T(8,128)(2,1)} collective-permute-done((bf16[96,1536]{1,0:T(8,128)(2,1)S(1)}, bf16[96,1536]{1,0:T(8,128)(2,1)}, u32[]{:S(2)}, u32[]{:S(2)}) %collective-permute-start.3) | collective-permute-done | bytes 294944 | tf_op jit(solution)/shard_map/ppermute | solution.py:493
  46.9 1.3 collective-permute-start.4
  48.2 1.4 collective-permute-start.23
  49.6 3.6 %collective-permute-done.25.refs_5_ = bf16[96,1536]{1,0:T(8,128)(2,1)} collective-permute-done((bf16[96,1536]{1,0:T(8,128)(2,1)}, bf16[96,1536]{1,0:T(8,128)(2,1)}, u32[]{:S(2)}, u32[]{:S(2)}) %collective-permute-start.25) | collective-permute-done | bytes 294944 | tf_op jit(solution)/shard_map/ppermute | solution.py:493
  53.2 1.3 collective-permute-start.26
  54.5 0.0 copy-start.2
  54.5 0.8 reshape.166
  55.3 0.1 pad_add_fusion.place
  55.3 0.7 collective-permute-start.2
  56.0 3.5 %collective-permute-done.4.refs_5_ = bf16[96,1536]{1,0:T(8,128)(2,1)} collective-permute-done((bf16[96,1536]{1,0:T(8,128)(2,1)}, bf16[96,1536]{1,0:T(8,128)(2,1)}, u32[]{:S(2)}, u32[]{:S(2)}) %collective-permute-start.4) | collective-permute-done | bytes 294944 | tf_op jit(solution)/shard_map/ppermute | solution.py:493
  59.5 1.3 collective-permute-start.5
  60.8 5.0 %collective-permute-done.26.refs_6_ = bf16[96,1536]{1,0:T(8,128)(2,1)} collective-permute-done((bf16[96,1536]{1,0:T(8,128)(2,1)}, bf16[96,1536]{1,0:T(8,128)(2,1)}, u32[]{:S(2)}, u32[]{:S(2)}) %collective-permute-start.26) | collective-permute-done | bytes 294944 | tf_op jit(solution)/shard_map/ppermute | solution.py:493
  65.8 1.0 copy-done.3
  66.8 3.5 %norm.3 = (bf16[96,1536]{1,0:T(8,128)(2,1)S(1)}, bf16[96,1536]{1,0:T(8,128)(2,1)S(1)}, bf16[96,1536]{1,0:T(8,128)(2,1)S(1)}, bf16[96,1536]{1,0:T(8,128)(2,1)S(1)}) custom-call(s32[2]{0:T(128)S(1)} %pad_add_fusion.place, bf16[96,1536]{1,0:T(8,128)(2,1)S(1)} %bitcast.35, bf16[96,1536]{1,0:T(8,128)(2,1)} %collective-permute-done.21.refs_1_, ...), custom_call_target="tpu_custom_call" | custom-call | tf_op jit(solution)/shard_map/norm/pallas_call | solution.py:500
  70.3 1.3 collective-permute-start.28
  71.6 0.2 collective-permute-start.30
  71.8 1.2 collective-permute-start.32
  73.1 2.6 %collective-permute-start.27 = (bf16[96,1536]{1,0:T(8,128)(2,1)S(1)}, bf16[96,1536]{1,0:T(8,128)(2,1)S(1)}, u32[]{:S(2)}, u32[]{:S(2)}) collective-permute-start(bf16[96,1536]{1,0:T(8,128)(2,1)S(1)} %get-tuple-element.50), channel_id=1, source_target_pairs={{0,4},{4,0},{8,12},{12,8},{16,20},{20,16},{24,28},{28,24},{1,5},{5... | collective-permute-start | bytes 884744 | tf_op jit(solution)/shard_map/ppermute | solution.py:430
  75.7 3.8 %norm.2 = (bf16[96,1536]{1,0:T(8,128)(2,1)S(1)}, bf16[96,1536]{1,0:T(8,128)(2,1)S(1)}, bf16[96,1536]{1,0:T(8,128)(2,1)S(1)}, bf16[96,1536]{1,0:T(8,128)(2,1)S(1)}) custom-call(s32[2]{0:T(128)S(1)} %pad_add_fusion.place, bf16[96,1536]{1,0:T(8,128)(2,1)S(1)} %bitcast.28, bf16[96,1536]{1,0:T(8,128)(2,1)} %collective-permute-done.refs_1_, ...), custom_call_target="tpu_custom_call" | custom-call | tf_op jit(solution)/shard_map/norm/pallas_call | solution.py:500
  79.5 1.3 collective-permute-start.7
  80.8 0.2 collective-permute-start.9
  81.0 2.4 %collective-permute-done.32 = bf16[96,1536]{1,0:T(8,128)(2,1)S(1)} collective-permute-done((bf16[96,1536]{1,0:T(8,128)(2,1)S(1)}, bf16[96,1536]{1,0:T(8,128)(2,1)S(1)}, u32[]{:S(2)}, u32[]{:S(2)}) %collective-permute-start.32) | collective-permute-done | bytes 294944 | tf_op jit(solution)/shard_map/ppermute | solution.py:430
  83.4 2.2 %collective-permute-start.11 = (bf16[96,1536]{1,0:T(8,128)(2,1)S(1)}, bf16[96,1536]{1,0:T(8,128)(2,1)S(1)}, u32[]{:S(2)}, u32[]{:S(2)}) collective-permute-start(bf16[96,1536]{1,0:T(8,128)(2,1)S(1)} %get-tuple-element.40), channel_id=1, source_target_pairs={{0,24},{4,28},{8,16},{12,20},{16,8},{20,12},{24,0},{28,4},{1,25},{... | collective-permute-start | bytes 884744 | tf_op jit(solution)/shard_map/ppermute | solution.py:430
  85.6 5.3 %collective-permute-start.29 = (bf16[96,1536]{1,0:T(8,128)(2,1)S(1)}, bf16[96,1536]{1,0:T(8,128)(2,1)S(1)}, u32[]{:S(2)}, u32[]{:S(2)}) collective-permute-start(bf16[96,1536]{1,0:T(8,128)(2,1)S(1)} %collective-permute-done.28), channel_id=1, source_target_pairs={{0,4},{4,0},{8,12},{12,8},{16,20},{20,16},{24,28},{28,24},{1,5},{5... | collective-permute-start | bytes 884744 | tf_op jit(solution)/shard_map/ppermute | solution.py:430
  90.9 3.9 %collective-permute-start.31 = (bf16[96,1536]{1,0:T(8,128)(2,1)S(1)}, bf16[96,1536]{1,0:T(8,128)(2,1)S(1)}, u32[]{:S(2)}, u32[]{:S(2)}) collective-permute-start(bf16[96,1536]{1,0:T(8,128)(2,1)S(1)} %collective-permute-done.30), channel_id=1, source_target_pairs={{0,4},{4,0},{8,12},{12,8},{16,20},{20,16},{24,28},{28,24},{1,5},{5... | collective-permute-start | bytes 884744 | tf_op jit(solution)/shard_map/ppermute | solution.py:430
  94.8 5.7 %collective-permute-start.33 = (bf16[96,1536]{1,0:T(8,128)(2,1)S(1)}, bf16[96,1536]{1,0:T(8,128)(2,1)S(1)}, u32[]{:S(2)}, u32[]{:S(2)}) collective-permute-start(bf16[96,1536]{1,0:T(8,128)(2,1)S(1)} %collective-permute-done.32), channel_id=1, source_target_pairs={{0,4},{4,0},{8,12},{12,8},{16,20},{20,16},{24,28},{28,24},{1,5},{5... | collective-permute-start | bytes 884744 | tf_op jit(solution)/shard_map/ppermute | solution.py:430
  100.5 0.0 collective-permute-start.6
  100.6 0.5 collective-permute-start.8
  101.1 0.1 collective-permute-start.10
  101.1 0.6 collective-permute-done.33
  101.8 0.4 collective-permute-start.12
  102.1 5.1 %project.3 = (bf16[96,1152]{1,0:T(8,128)(2,1)S(1)}, bf16[96,1152]{1,0:T(8,128)(2,1)S(1)}, bf16[96,1152]{1,0:T(8,128)(2,1)S(1)}, bf16[96,1152]{1,0:T(8,128)(2,1)S...) custom-call(s32[1]{0:T(128)} %bitcast.place, ...), custom_call_target="tpu_custom_call" | custom-call | tf_op jit(solution)/shard_map/project/pallas_call | solution.py:518
  107.2 0.2 collective-permute-start.34
  107.5 2.0 %collective-permute-start.36 = (bf16[96,1152]{1,0:T(8,128)(2,1)S(1)}, bf16[96,1152]{1,0:T(8,128)(2,1)S(1)}, u32[]{:S(2)}, u32[]{:S(2)}) collective-permute-start(bf16[96,1152]{1,0:T(8,128)(2,1)S(1)} %get-tuple-element.57), channel_id=1, source_target_pairs={{0,12},{4,8},{8,4},{12,0},{16,28},{20,24},{24,20},{28,16},{1,13},{... | collective-permute-start | bytes 663560 | tf_op jit(solution)/shard_map/ppermute | solution.py:430
  109.5 0.5 collective-permute-start.37
  110.0 1.1 collective-permute-start.38
  111.1 0.0 copy-start.13
  111.1 5.1 %project.2 = (bf16[96,1152]{1,0:T(8,128)(2,1)S(1)}, bf16[96,1152]{1,0:T(8,128)(2,1)S(1)}, bf16[96,1152]{1,0:T(8,128)(2,1)S(1)}, bf16[96,1152]{1,0:T(8,128)(2,1)S...) custom-call(s32[1]{0:T(128)} %bitcast.place, ...), custom_call_target="tpu_custom_call" | custom-call | tf_op jit(solution)/shard_map/project/pallas_call | solution.py:518
  116.2 0.0 copy-start.4
  116.2 0.6 collective-permute-start.39
  116.8 2.4 %collective-permute-start.40 = (bf16[96,1152]{1,0:T(8,128)(2,1)S(1)}, bf16[96,1152]{1,0:T(8,128)(2,1)S(1)}, u32[]{:S(2)}, u32[]{:S(2)}) collective-permute-start(bf16[96,1152]{1,0:T(8,128)(2,1)S(1)} %get-tuple-element.61), channel_id=1, source_target_pairs={{0,28},{4,24},{8,20},{12,16},{16,12},{20,8},{24,4},{28,0},{1,29},{... | collective-permute-start | bytes 663560 | tf_op jit(solution)/shard_map/ppermute | solution.py:430
  119.2 0.9 collective-permute-done.36.refs_3_
  120.0 0.1 add_convert_fusion
  120.1 11.0 %collective-permute-done.38.refs_5_ = bf16[96,1152]{1,0:T(8,128)(2,1)S(1)} collective-permute-done((bf16[96,1152]{1,0:T(8,128)(2,1)S(1)}, bf16[96,1152]{1,0:T(8,128)(2,1)S(1)}, u32[]{:S(2)}, u32[]{:S(2)}) %collective-permute-start.38) | collective-permute-done | bytes 221216 | tf_op jit(solution)/shard_map/ppermute | solution.py:430
  131.1 0.5 collective-permute-start.17
  131.6 1.3 collective-permute-start.18
  133.0 1.9 %collective-permute-start.19 = (bf16[96,1152]{1,0:T(8,128)(2,1)S(1)}, bf16[96,1152]{1,0:T(8,128)(2,1)S(1)}, u32[]{:S(2)}, u32[]{:S(2)}) collective-permute-start(bf16[96,1152]{1,0:T(8,128)(2,1)S(1)} %get-tuple-element.47), channel_id=1, source_target_pairs={{0,24},{4,28},{8,16},{12,20},{16,8},{20,12},{24,0},{28,4},{1,25},{... | collective-permute-start | bytes 663560 | tf_op jit(solution)/shard_map/ppermute | solution.py:430
  134.9 0.7 collective-permute-start.20
  135.6 2.2 %fusion = (f32[4,48,768]{2,1,0:T(8,128)S(1)}, f32[4,48,768]{2,1,0:T(8,128)S(1)}, f32[4,48,768]{2,1,0:T(8,128)S(1)}) fusion(f32[768]{0:T(1024)S(1)} %copy-done.10, f32[4,48]{1,0:T(4,128)S(1)} %add_convert_fusion, pred[768]{0:T(1024)(128)(4,1)S(1)} %copy-done.13, pred[768]{0:T(1024)(128)(4,1)S(1)} %copy-done.12, pred[768]{0:T(1024)(128)(4,1)S(1)} %copy-done.11), kind=kLoop, calls=%fused_computation.2 | loop fusion | flops 737280 | bytes 1775616 | tf_op jit(solution)/shard_map/jit(_where)/select_n | solution.py:470
  137.8 3.2 %copy-done = bf16[40,128,768]{2,1,0:T(8,128)(2,1)S(1)} copy-done((bf16[40,128,768]{2,1,0:T(8,128)(2,1)S(1)}, bf16[40,128,768]{2,1,0:T(8,128)(2,1)}, u32[]{:S(2)}) %copy-start) | copy-done | bytes 7864344
  141.0 17.8 %attend.2 = (bf16[4,48,768]{2,1,0:T(8,128)(2,1)}, bf16[4,48,768]{2,1,0:T(8,128)(2,1)}, bf16[4,48,768]{2,1,0:T(8,128)(2,1)}) custom-call(s32[1]{0:T(128)} %bitcast.place, s32[4]{0:T(128)S(1)} %copy-done.6, s32[4]{0:T(128)S(1)} %copy-done.5, s32[4,16]{1,0:T(4,128)S(1)} %copy-done.4, bf16[96,1152]{1,0:T(8,128)(2,1)S(1)} %get-tuple-element.54.refs_0_, ...), custom_call_target="tpu_custom_call" | custom-call | tf_op jit(solution)/shard_map/attend/pallas_call | solution.py:547
  158.9 14.7 %attend.3 = (bf16[4,48,768]{2,1,0:T(8,128)(2,1)}, bf16[4,48,768]{2,1,0:T(8,128)(2,1)}, bf16[4,48,768]{2,1,0:T(8,128)(2,1)}) custom-call(s32[1]{0:T(128)} %bitcast.place, s32[4]{0:T(128)S(1)} %copy-done.6, s32[4]{0:T(128)S(1)} %copy-done.5, s32[4,16]{1,0:T(4,128)S(1)} %copy-done.4, ...), custom_call_target="tpu_custom_call", output_to_operand_aliasing={{0}: (18, {}), {1}: (19, {}), {2}: (20, {})} | custom-call | tf_op jit(solution)/shard_map/attend/pallas_call | solution.py:547
  (65 shorter events, 0.2 us)
Async XLA Ops:
  21.8 16.0 %collective-permute-start.21 = (bf16[96,1536]{1,0:T(8,128)(2,1)}, bf16[96,1536]{1,0:T(8,128)(2,1)}, u32[]{:S(2)}, u32[]{:S(2)}) collective-permute-start(bf16[96,1536]{1,0:T(8,128)(2,1)} %bitcast.33), channel_id=1, source_target_pairs={{0,1},{1,2},{2,3},{4,5},{5,6},{6,7},{8,9},{9,10},{10,11},{12,13},{... | collective-permute-start | bytes 884744 | tf_op jit(solution)/shard_map/ppermute | solution.py:492
  25.7 13.5 %collective-permute-start.24 = (bf16[96,1536]{1,0:T(8,128)(2,1)}, bf16[96,1536]{1,0:T(8,128)(2,1)}, u32[]{:S(2)}, u32[]{:S(2)}) collective-permute-start(bf16[96,1536]{1,0:T(8,128)(2,1)} %bitcast.34), channel_id=1, source_target_pairs={{1,0},{2,1},{3,2},{5,4},{6,5},{7,6},{9,8},{10,9},{11,10},{13,12},{... | collective-permute-start | bytes 884744 | tf_op jit(solution)/shard_map/ppermute | solution.py:493
  27.0 4.5 %copy-start.1 = (bf16[2,48,1536]{2,1,0:T(8,128)(2,1)S(1)}, bf16[2,48,1536]{2,1,0:T(8,128)(2,1)}, u32[]{:S(2)}) copy-start(bf16[2,48,1536]{2,1,0:T(8,128)(2,1)} %get-tuple-element.36) | copy-start | bytes 884740
  27.0 27.5 %copy-start.8 = (bf16[6144]{0:T(1024)(128)(2,1)S(1)}, bf16[6144]{0:T(1024)(128)(2,1)}, u32[]{:S(2)}) copy-start(bf16[6144]{0:T(1024)(128)(2,1)} %param.18) | copy-start | bytes 36868
  30.6 71.5 %collective-permute-start.13 = (bf16[768,1152]{1,0:T(8,128)(2,1)}, bf16[768,1152]{1,0:T(8,128)(2,1)S(1)}, u32[]{:S(2)}, u32[]{:S(2)}) collective-permute-start(bf16[768,1152]{1,0:T(8,128)(2,1)} %get-tuple-element.65), channel_id=1, source_target_pairs={{0,4},{4,0},{8,12},{12,8},{16,20},{20,16},{24,28},{28,24},{1,5},{5... | collective-permute-start | bytes 5308424 | tf_op jit(solution)/shard_map/ppermute | solution.py:430
  31.5 10.7 %collective-permute-start = (bf16[96,1536]{1,0:T(8,128)(2,1)S(1)}, bf16[96,1536]{1,0:T(8,128)(2,1)}, u32[]{:S(2)}, u32[]{:S(2)}) collective-permute-start(bf16[96,1536]{1,0:T(8,128)(2,1)S(1)} %bitcast.26), channel_id=1, source_target_pairs={{0,1},{1,2},{2,3},{4,5},{5,6},{6,7},{8,9},{9,10},{10,11},{12,13},{... | collective-permute-start | bytes 884744 | tf_op jit(solution)/shard_map/ppermute | solution.py:492
  36.5 10.3 %collective-permute-start.3 = (bf16[96,1536]{1,0:T(8,128)(2,1)S(1)}, bf16[96,1536]{1,0:T(8,128)(2,1)}, u32[]{:S(2)}, u32[]{:S(2)}) collective-permute-start(bf16[96,1536]{1,0:T(8,128)(2,1)S(1)} %bitcast.27), channel_id=1, source_target_pairs={{1,0},{2,1},{3,2},{5,4},{6,5},{7,6},{9,8},{10,9},{11,10},{13,12},{... | collective-permute-start | bytes 884744 | tf_op jit(solution)/shard_map/ppermute | solution.py:493
  37.8 10.3 %collective-permute-start.22 = (bf16[96,1536]{1,0:T(8,128)(2,1)}, bf16[96,1536]{1,0:T(8,128)(2,1)}, u32[]{:S(2)}, u32[]{:S(2)}) collective-permute-start(bf16[96,1536]{1,0:T(8,128)(2,1)} %collective-permute-done.21.refs_1_), channel_id=1, source_target_pairs={{1,2},{2,3},{5,6},{6,7},{9,10},{10,11},{13,14},{14,15},{17,18},{18... | collective-permute-start | bytes 884744 | tf_op jit(solution)/shard_map/ppermute | solution.py:492
  39.2 13.9 %collective-permute-start.25 = (bf16[96,1536]{1,0:T(8,128)(2,1)}, bf16[96,1536]{1,0:T(8,128)(2,1)}, u32[]{:S(2)}, u32[]{:S(2)}) collective-permute-start(bf16[96,1536]{1,0:T(8,128)(2,1)} %collective-permute-done.24.refs_4_), channel_id=1, source_target_pairs={{1,0},{2,1},{5,4},{6,5},{9,8},{10,9},{13,12},{14,13},{17,16},{18,1... | collective-permute-start | bytes 884744 | tf_op jit(solution)/shard_map/ppermute | solution.py:493
  42.2 13.1 %collective-permute-start.1 = (bf16[96,1536]{1,0:T(8,128)(2,1)}, bf16[96,1536]{1,0:T(8,128)(2,1)}, u32[]{:S(2)}, u32[]{:S(2)}) collective-permute-start(bf16[96,1536]{1,0:T(8,128)(2,1)} %collective-permute-done.refs_1_), channel_id=1, source_target_pairs={{1,2},{2,3},{5,6},{6,7},{9,10},{10,11},{13,14},{14,15},{17,18},{18... | collective-permute-start | bytes 884744 | tf_op jit(solution)/shard_map/ppermute | solution.py:492
  46.9 12.6 %collective-permute-start.4 = (bf16[96,1536]{1,0:T(8,128)(2,1)}, bf16[96,1536]{1,0:T(8,128)(2,1)}, u32[]{:S(2)}, u32[]{:S(2)}) collective-permute-start(bf16[96,1536]{1,0:T(8,128)(2,1)} %collective-permute-done.3.refs_4_), channel_id=1, source_target_pairs={{1,0},{2,1},{5,4},{6,5},{9,8},{10,9},{13,12},{14,13},{17,16},{18,1... | collective-permute-start | bytes 884744 | tf_op jit(solution)/shard_map/ppermute | solution.py:493
  48.2 12.6 %collective-permute-start.23 = (bf16[96,1536]{1,0:T(8,128)(2,1)}, bf16[96,1536]{1,0:T(8,128)(2,1)}, u32[]{:S(2)}, u32[]{:S(2)}) collective-permute-start(bf16[96,1536]{1,0:T(8,128)(2,1)} %collective-permute-done.22.refs_2_), channel_id=1, source_target_pairs={{2,3},{6,7},{10,11},{14,15},{18,19},{22,23},{26,27},{30,31}} | collective-permute-start | bytes 884744 | tf_op jit(solution)/shard_map/ppermute | solution.py:492
  53.2 12.6 %collective-permute-start.26 = (bf16[96,1536]{1,0:T(8,128)(2,1)}, bf16[96,1536]{1,0:T(8,128)(2,1)}, u32[]{:S(2)}, u32[]{:S(2)}) collective-permute-start(bf16[96,1536]{1,0:T(8,128)(2,1)} %collective-permute-done.25.refs_5_), channel_id=1, source_target_pairs={{1,0},{5,4},{9,8},{13,12},{17,16},{21,20},{25,24},{29,28}} | collective-permute-start | bytes 884744 | tf_op jit(solution)/shard_map/ppermute | solution.py:493
  54.5 21.2 %copy-start.2 = (bf16[2,48,1536]{2,1,0:T(8,128)(2,1)S(1)}, bf16[2,48,1536]{2,1,0:T(8,128)(2,1)}, u32[]{:S(2)}) copy-start(bf16[2,48,1536]{2,1,0:T(8,128)(2,1)} %get-tuple-element.36) | copy-start | bytes 884740
  55.3 16.5 %collective-permute-start.2 = (bf16[96,1536]{1,0:T(8,128)(2,1)}, bf16[96,1536]{1,0:T(8,128)(2,1)S(1)}, u32[]{:S(2)}, u32[]{:S(2)}) collective-permute-start(bf16[96,1536]{1,0:T(8,128)(2,1)} %collective-permute-done.1.refs_2_), channel_id=1, source_target_pairs={{2,3},{6,7},{10,11},{14,15},{18,19},{22,23},{26,27},{30,31}} | collective-permute-start | bytes 884744 | tf_op jit(solution)/shard_map/ppermute | solution.py:492
  59.5 13.6 %collective-permute-start.5 = (bf16[96,1536]{1,0:T(8,128)(2,1)}, bf16[96,1536]{1,0:T(8,128)(2,1)S(1)}, u32[]{:S(2)}, u32[]{:S(2)}) collective-permute-start(bf16[96,1536]{1,0:T(8,128)(2,1)} %collective-permute-done.4.refs_5_), channel_id=1, source_target_pairs={{1,0},{5,4},{9,8},{13,12},{17,16},{21,20},{25,24},{29,28}} | collective-permute-start | bytes 884744 | tf_op jit(solution)/shard_map/ppermute | solution.py:493
  65.8 1.0 copy-start.3
  66.8 35.4 %copy-start.7 = (s32[32]{0:T(128)S(1)}, s32[32]{0:T(128)}, u32[]{:S(2)}) copy-start(s32[32]{0:T(128)} %get-tuple-element.35.source) | copy-start | bytes 388
  70.3 9.2 %collective-permute-start.28 = (bf16[96,1536]{1,0:T(8,128)(2,1)S(1)}, bf16[96,1536]{1,0:T(8,128)(2,1)S(1)}, u32[]{:S(2)}, u32[]{:S(2)}) collective-permute-start(bf16[96,1536]{1,0:T(8,128)(2,1)S(1)} %get-tuple-element.51), channel_id=1, source_target_pairs={{0,8},{4,12},{8,0},{12,4},{16,24},{20,28},{24,16},{28,20},{1,9},{5... | collective-permute-start | bytes 884744 | tf_op jit(solution)/shard_map/ppermute | solution.py:430
  71.6 9.2 %collective-permute-start.30 = (bf16[96,1536]{1,0:T(8,128)(2,1)S(1)}, bf16[96,1536]{1,0:T(8,128)(2,1)S(1)}, u32[]{:S(2)}, u32[]{:S(2)}) collective-permute-start(bf16[96,1536]{1,0:T(8,128)(2,1)S(1)} %get-tuple-element.52), channel_id=1, source_target_pairs={{0,16},{4,20},{8,24},{12,28},{16,0},{20,4},{24,8},{28,12},{1,17},{... | collective-permute-start | bytes 884744 | tf_op jit(solution)/shard_map/ppermute | solution.py:430
  71.8 11.6 %collective-permute-start.32 = (bf16[96,1536]{1,0:T(8,128)(2,1)S(1)}, bf16[96,1536]{1,0:T(8,128)(2,1)S(1)}, u32[]{:S(2)}, u32[]{:S(2)}) collective-permute-start(bf16[96,1536]{1,0:T(8,128)(2,1)S(1)} %get-tuple-element.53), channel_id=1, source_target_pairs={{0,24},{4,28},{8,16},{12,20},{16,8},{20,12},{24,0},{28,4},{1,25},{... | collective-permute-start | bytes 884744 | tf_op jit(solution)/shard_map/ppermute | solution.py:430
  73.1 12.5 %collective-permute-start.27 = (bf16[96,1536]{1,0:T(8,128)(2,1)S(1)}, bf16[96,1536]{1,0:T(8,128)(2,1)S(1)}, u32[]{:S(2)}, u32[]{:S(2)}) collective-permute-start(bf16[96,1536]{1,0:T(8,128)(2,1)S(1)} %get-tuple-element.50), channel_id=1, source_target_pairs={{0,4},{4,0},{8,12},{12,8},{16,20},{20,16},{24,28},{28,24},{1,5},{5... | collective-permute-start | bytes 884744 | tf_op jit(solution)/shard_map/ppermute | solution.py:430
  75.7 62.1 %slice-start = ((s8[7864320]{0:T(1024)(128)(4,1)}), s8[4194304]{0:T(1024)(128)(4,1)S(1)}, s32[]{:S(2)}) async-start(s8[7864320]{0:T(1024)(128)(4,1)} %bitcast.24), calls=%async_computation | async-start | bytes 8388608
  79.5 11.4 %collective-permute-start.7 = (bf16[96,1536]{1,0:T(8,128)(2,1)S(1)}, bf16[96,1536]{1,0:T(8,128)(2,1)S(1)}, u32[]{:S(2)}, u32[]{:S(2)}) collective-permute-start(bf16[96,1536]{1,0:T(8,128)(2,1)S(1)} %get-tuple-element.38), channel_id=1, source_target_pairs={{0,8},{4,12},{8,0},{12,4},{16,24},{20,28},{24,16},{28,20},{1,9},{5... | collective-permute-start | bytes 884744 | tf_op jit(solution)/shard_map/ppermute | solution.py:430
  80.8 14.1 %collective-permute-start.9 = (bf16[96,1536]{1,0:T(8,128)(2,1)S(1)}, bf16[96,1536]{1,0:T(8,128)(2,1)S(1)}, u32[]{:S(2)}, u32[]{:S(2)}) collective-permute-start(bf16[96,1536]{1,0:T(8,128)(2,1)S(1)} %get-tuple-element.39), channel_id=1, source_target_pairs={{0,16},{4,20},{8,24},{12,28},{16,0},{20,4},{24,8},{28,12},{1,17},{... | collective-permute-start | bytes 884744 | tf_op jit(solution)/shard_map/ppermute | solution.py:430
  83.4 17.1 %collective-permute-start.11 = (bf16[96,1536]{1,0:T(8,128)(2,1)S(1)}, bf16[96,1536]{1,0:T(8,128)(2,1)S(1)}, u32[]{:S(2)}, u32[]{:S(2)}) collective-permute-start(bf16[96,1536]{1,0:T(8,128)(2,1)S(1)} %get-tuple-element.40), channel_id=1, source_target_pairs={{0,24},{4,28},{8,16},{12,20},{16,8},{20,12},{24,0},{28,4},{1,25},{... | collective-permute-start | bytes 884744 | tf_op jit(solution)/shard_map/ppermute | solution.py:430
  85.6 15.0 %collective-permute-start.29 = (bf16[96,1536]{1,0:T(8,128)(2,1)S(1)}, bf16[96,1536]{1,0:T(8,128)(2,1)S(1)}, u32[]{:S(2)}, u32[]{:S(2)}) collective-permute-start(bf16[96,1536]{1,0:T(8,128)(2,1)S(1)} %collective-permute-done.28), channel_id=1, source_target_pairs={{0,4},{4,0},{8,12},{12,8},{16,20},{20,16},{24,28},{28,24},{1,5},{5... | collective-permute-start | bytes 884744 | tf_op jit(solution)/shard_map/ppermute | solution.py:430
  90.9 10.2 %collective-permute-start.31 = (bf16[96,1536]{1,0:T(8,128)(2,1)S(1)}, bf16[96,1536]{1,0:T(8,128)(2,1)S(1)}, u32[]{:S(2)}, u32[]{:S(2)}) collective-permute-start(bf16[96,1536]{1,0:T(8,128)(2,1)S(1)} %collective-permute-done.30), channel_id=1, source_target_pairs={{0,4},{4,0},{8,12},{12,8},{16,20},{20,16},{24,28},{28,24},{1,5},{5... | collective-permute-start | bytes 884744 | tf_op jit(solution)/shard_map/ppermute | solution.py:430
  94.8 6.9 %collective-permute-start.33 = (bf16[96,1536]{1,0:T(8,128)(2,1)S(1)}, bf16[96,1536]{1,0:T(8,128)(2,1)S(1)}, u32[]{:S(2)}, u32[]{:S(2)}) collective-permute-start(bf16[96,1536]{1,0:T(8,128)(2,1)S(1)} %collective-permute-done.32), channel_id=1, source_target_pairs={{0,4},{4,0},{8,12},{12,8},{16,20},{20,16},{24,28},{28,24},{1,5},{5... | collective-permute-start | bytes 884744 | tf_op jit(solution)/shard_map/ppermute | solution.py:430
  100.5 6.9 %collective-permute-start.6 = (bf16[96,1536]{1,0:T(8,128)(2,1)S(1)}, bf16[96,1536]{1,0:T(8,128)(2,1)S(1)}, u32[]{:S(2)}, u32[]{:S(2)}) collective-permute-start(bf16[96,1536]{1,0:T(8,128)(2,1)S(1)} %get-tuple-element.37), channel_id=1, source_target_pairs={{0,4},{4,0},{8,12},{12,8},{16,20},{20,16},{24,28},{28,24},{1,5},{5... | collective-permute-start | bytes 884744 | tf_op jit(solution)/shard_map/ppermute | solution.py:430
  100.6 6.9 %collective-permute-start.8 = (bf16[96,1536]{1,0:T(8,128)(2,1)S(1)}, bf16[96,1536]{1,0:T(8,128)(2,1)S(1)}, u32[]{:S(2)}, u32[]{:S(2)}) collective-permute-start(bf16[96,1536]{1,0:T(8,128)(2,1)S(1)} %collective-permute-done.7), channel_id=1, source_target_pairs={{0,4},{4,0},{8,12},{12,8},{16,20},{20,16},{24,28},{28,24},{1,5},{5... | collective-permute-start | bytes 884744 | tf_op jit(solution)/shard_map/ppermute | solution.py:430
  101.1 8.4 %collective-permute-start.10 = (bf16[96,1536]{1,0:T(8,128)(2,1)S(1)}, bf16[96,1536]{1,0:T(8,128)(2,1)S(1)}, u32[]{:S(2)}, u32[]{:S(2)}) collective-permute-start(bf16[96,1536]{1,0:T(8,128)(2,1)S(1)} %collective-permute-done.9), channel_id=1, source_target_pairs={{0,4},{4,0},{8,12},{12,8},{16,20},{20,16},{24,28},{28,24},{1,5},{5... | collective-permute-start | bytes 884744 | tf_op jit(solution)/shard_map/ppermute | solution.py:430
  101.8 8.2 %collective-permute-start.12 = (bf16[96,1536]{1,0:T(8,128)(2,1)S(1)}, bf16[96,1536]{1,0:T(8,128)(2,1)S(1)}, u32[]{:S(2)}, u32[]{:S(2)}) collective-permute-start(bf16[96,1536]{1,0:T(8,128)(2,1)S(1)} %collective-permute-done.11), channel_id=1, source_target_pairs={{0,4},{4,0},{8,12},{12,8},{16,20},{20,16},{24,28},{28,24},{1,5},{5... | collective-permute-start | bytes 884744 | tf_op jit(solution)/shard_map/ppermute | solution.py:430
  102.1 7.8 %copy-start.9 = (bf16[2304]{0:T(1024)(128)(2,1)S(1)}, bf16[2304]{0:T(1024)(128)(2,1)}, u32[]{:S(2)}) copy-start(bf16[2304]{0:T(1024)(128)(2,1)} %param.21) | copy-start | bytes 13828
  102.1 35.6 %slice-start.1 = ((s8[7864320]{0:T(1024)(128)(4,1)}), s8[3670016]{0:T(1024)(128)(4,1)S(1)}, s32[]{:S(2)}) async-start(s8[7864320]{0:T(1024)(128)(4,1)} %bitcast.24), calls=%async_computation.1 | async-start | bytes 7340032
  107.2 9.0 %collective-permute-start.34 = (bf16[96,1152]{1,0:T(8,128)(2,1)S(1)}, bf16[96,1152]{1,0:T(8,128)(2,1)S(1)}, u32[]{:S(2)}, u32[]{:S(2)}) collective-permute-start(bf16[96,1152]{1,0:T(8,128)(2,1)S(1)} %get-tuple-element.55), channel_id=1, source_target_pairs={{0,4},{4,0},{8,12},{12,8},{16,20},{20,16},{24,28},{28,24},{1,5},{5... | collective-permute-start | bytes 663560 | tf_op jit(solution)/shard_map/ppermute | solution.py:430
  107.4 9.3 %collective-permute-start.35 = (bf16[96,1152]{1,0:T(8,128)(2,1)S(1)}, bf16[96,1152]{1,0:T(8,128)(2,1)S(1)}, u32[]{:S(2)}, u32[]{:S(2)}) collective-permute-start(bf16[96,1152]{1,0:T(8,128)(2,1)S(1)} %get-tuple-element.56), channel_id=1, source_target_pairs={{0,8},{4,12},{8,0},{12,4},{16,24},{20,28},{24,16},{28,20},{1,9},{5... | collective-permute-start | bytes 663560 | tf_op jit(solution)/shard_map/ppermute | solution.py:430
  107.5 12.6 %collective-permute-start.36 = (bf16[96,1152]{1,0:T(8,128)(2,1)S(1)}, bf16[96,1152]{1,0:T(8,128)(2,1)S(1)}, u32[]{:S(2)}, u32[]{:S(2)}) collective-permute-start(bf16[96,1152]{1,0:T(8,128)(2,1)S(1)} %get-tuple-element.57), channel_id=1, source_target_pairs={{0,12},{4,8},{8,4},{12,0},{16,28},{20,24},{24,20},{28,16},{1,13},{... | collective-permute-start | bytes 663560 | tf_op jit(solution)/shard_map/ppermute | solution.py:430
  109.5 10.6 %collective-permute-start.37 = (bf16[96,1152]{1,0:T(8,128)(2,1)S(1)}, bf16[96,1152]{1,0:T(8,128)(2,1)S(1)}, u32[]{:S(2)}, u32[]{:S(2)}) collective-permute-start(bf16[96,1152]{1,0:T(8,128)(2,1)S(1)} %get-tuple-element.58), channel_id=1, source_target_pairs={{0,16},{4,20},{8,24},{12,28},{16,0},{20,4},{24,8},{28,12},{1,17},{... | collective-permute-start | bytes 663560 | tf_op jit(solution)/shard_map/ppermute | solution.py:430
  110.0 21.2 %collective-permute-start.38 = (bf16[96,1152]{1,0:T(8,128)(2,1)S(1)}, bf16[96,1152]{1,0:T(8,128)(2,1)S(1)}, u32[]{:S(2)}, u32[]{:S(2)}) collective-permute-start(bf16[96,1152]{1,0:T(8,128)(2,1)S(1)} %get-tuple-element.59), channel_id=1, source_target_pairs={{0,20},{4,16},{8,28},{12,24},{16,4},{20,0},{24,12},{28,8},{1,21},{... | collective-permute-start | bytes 663560 | tf_op jit(solution)/shard_map/ppermute | solution.py:430
  111.0 9.0 %copy-start.5 = (s32[4]{0:T(128)S(1)}, s32[4]{0:T(128)}, u32[]{:S(2)}) copy-start(s32[4]{0:T(128)} %all_lengths.3) | copy-start | bytes 52
  111.1 24.5 %copy-start.10 = (f32[768]{0:T(1024)S(1)}, f32[768]{0:T(1024)}, u32[]{:S(2)}) copy-start(f32[768]{0:T(1024)} %constant.45) | copy-start | bytes 9220
  111.1 24.5 %copy-start.11 = (pred[768]{0:T(1024)(128)(4,1)S(1)}, pred[768]{0:T(1024)(128)(4,1)}, u32[]{:S(2)}) copy-start(pred[768]{0:T(1024)(128)(4,1)} %constant.37.clone) | copy-start | bytes 2308
  111.1 24.5 %copy-start.12 = (pred[768]{0:T(1024)(128)(4,1)S(1)}, pred[768]{0:T(1024)(128)(4,1)}, u32[]{:S(2)}) copy-start(pred[768]{0:T(1024)(128)(4,1)} %constant.38.clone) | copy-start | bytes 2308
  111.1 24.5 %copy-start.13 = (pred[768]{0:T(1024)(128)(4,1)S(1)}, pred[768]{0:T(1024)(128)(4,1)}, u32[]{:S(2)}) copy-start(pred[768]{0:T(1024)(128)(4,1)} %constant.46) | copy-start | bytes 2308
  116.2 21.6 %copy-start.4 = (s32[4,16]{1,0:T(4,128)S(1)}, s32[4,16]{1,0:T(4,128)}, u32[]{:S(2)}) copy-start(s32[4,16]{1,0:T(4,128)} %table.3) | copy-start | bytes 772
  116.2 21.6 %copy-start.6 = (s32[4]{0:T(128)S(1)}, s32[4]{0:T(128)}, u32[]{:S(2)}) copy-start(s32[4]{0:T(128)} %get-tuple-element.34.slots) | copy-start | bytes 52
  116.2 14.9 %collective-permute-start.39 = (bf16[96,1152]{1,0:T(8,128)(2,1)S(1)}, bf16[96,1152]{1,0:T(8,128)(2,1)S(1)}, u32[]{:S(2)}, u32[]{:S(2)}) collective-permute-start(bf16[96,1152]{1,0:T(8,128)(2,1)S(1)} %get-tuple-element.60), channel_id=1, source_target_pairs={{0,24},{4,28},{8,16},{12,20},{16,8},{20,12},{24,0},{28,4},{1,25},{... | collective-permute-start | bytes 663560 | tf_op jit(solution)/shard_map/ppermute | solution.py:430
  116.8 14.8 %collective-permute-start.40 = (bf16[96,1152]{1,0:T(8,128)(2,1)S(1)}, bf16[96,1152]{1,0:T(8,128)(2,1)S(1)}, u32[]{:S(2)}, u32[]{:S(2)}) collective-permute-start(bf16[96,1152]{1,0:T(8,128)(2,1)S(1)} %get-tuple-element.61), channel_id=1, source_target_pairs={{0,28},{4,24},{8,20},{12,16},{16,12},{20,8},{24,4},{28,0},{1,29},{... | collective-permute-start | bytes 663560 | tf_op jit(solution)/shard_map/ppermute | solution.py:430
  120.0 12.9 %collective-permute-start.14 = (bf16[96,1152]{1,0:T(8,128)(2,1)S(1)}, bf16[96,1152]{1,0:T(8,128)(2,1)S(1)}, u32[]{:S(2)}, u32[]{:S(2)}) collective-permute-start(bf16[96,1152]{1,0:T(8,128)(2,1)S(1)} %get-tuple-element.42), channel_id=1, source_target_pairs={{0,4},{4,0},{8,12},{12,8},{16,20},{20,16},{24,28},{28,24},{1,5},{5... | collective-permute-start | bytes 663560 | tf_op jit(solution)/shard_map/ppermute | solution.py:430
  120.0 14.8 %collective-permute-start.15 = (bf16[96,1152]{1,0:T(8,128)(2,1)S(1)}, bf16[96,1152]{1,0:T(8,128)(2,1)S(1)}, u32[]{:S(2)}, u32[]{:S(2)}) collective-permute-start(bf16[96,1152]{1,0:T(8,128)(2,1)S(1)} %get-tuple-element.43), channel_id=1, source_target_pairs={{0,8},{4,12},{8,0},{12,4},{16,24},{20,28},{24,16},{28,20},{1,9},{5... | collective-permute-start | bytes 663560 | tf_op jit(solution)/shard_map/ppermute | solution.py:430
  131.1 27.7 %collective-permute-start.16 = (bf16[96,1152]{1,0:T(8,128)(2,1)S(1)}, bf16[96,1152]{1,0:T(8,128)(2,1)S(1)}, u32[]{:S(2)}, u32[]{:S(2)}) collective-permute-start(bf16[96,1152]{1,0:T(8,128)(2,1)S(1)} %get-tuple-element.44), channel_id=1, source_target_pairs={{0,12},{4,8},{8,4},{12,0},{16,28},{20,24},{24,20},{28,16},{1,13},{... | collective-permute-start | bytes 663560 | tf_op jit(solution)/shard_map/ppermute | solution.py:430
  131.1 27.7 %collective-permute-start.17 = (bf16[96,1152]{1,0:T(8,128)(2,1)S(1)}, bf16[96,1152]{1,0:T(8,128)(2,1)S(1)}, u32[]{:S(2)}, u32[]{:S(2)}) collective-permute-start(bf16[96,1152]{1,0:T(8,128)(2,1)S(1)} %get-tuple-element.45), channel_id=1, source_target_pairs={{0,16},{4,20},{8,24},{12,28},{16,0},{20,4},{24,8},{28,12},{1,17},{... | collective-permute-start | bytes 663560 | tf_op jit(solution)/shard_map/ppermute | solution.py:430
  131.6 27.3 %collective-permute-start.18 = (bf16[96,1152]{1,0:T(8,128)(2,1)S(1)}, bf16[96,1152]{1,0:T(8,128)(2,1)S(1)}, u32[]{:S(2)}, u32[]{:S(2)}) collective-permute-start(bf16[96,1152]{1,0:T(8,128)(2,1)S(1)} %get-tuple-element.46), channel_id=1, source_target_pairs={{0,20},{4,16},{8,28},{12,24},{16,4},{20,0},{24,12},{28,8},{1,21},{... | collective-permute-start | bytes 663560 | tf_op jit(solution)/shard_map/ppermute | solution.py:430
  133.0 25.9 %collective-permute-start.19 = (bf16[96,1152]{1,0:T(8,128)(2,1)S(1)}, bf16[96,1152]{1,0:T(8,128)(2,1)S(1)}, u32[]{:S(2)}, u32[]{:S(2)}) collective-permute-start(bf16[96,1152]{1,0:T(8,128)(2,1)S(1)} %get-tuple-element.47), channel_id=1, source_target_pairs={{0,24},{4,28},{8,16},{12,20},{16,8},{20,12},{24,0},{28,4},{1,25},{... | collective-permute-start | bytes 663560 | tf_op jit(solution)/shard_map/ppermute | solution.py:430
  134.9 24.1 %collective-permute-start.20 = (bf16[96,1152]{1,0:T(8,128)(2,1)S(1)}, bf16[96,1152]{1,0:T(8,128)(2,1)S(1)}, u32[]{:S(2)}, u32[]{:S(2)}) collective-permute-start(bf16[96,1152]{1,0:T(8,128)(2,1)S(1)} %get-tuple-element.48), channel_id=1, source_target_pairs={{0,28},{4,24},{8,20},{12,16},{16,12},{20,8},{24,4},{28,0},{1,29},{... | collective-permute-start | bytes 663560 | tf_op jit(solution)/shard_map/ppermute | solution.py:430
  137.8 3.2 %copy-start = (bf16[40,128,768]{2,1,0:T(8,128)(2,1)S(1)}, bf16[40,128,768]{2,1,0:T(8,128)(2,1)}, u32[]{:S(2)}) copy-start(bf16[40,128,768]{2,1,0:T(8,128)(2,1)} %refs_13_.3) | copy-start | bytes 23592964

commit v3 on v2

--- a/solution.py
+++ b/solution.py
@@ -47,12 +47,19 @@
 
     lax.fori_loop(0, everyone, rank, 0)
 
+    shift = req_count.bit_length() - 1
+
+    def note(item, shade):
+        color[item] = shade
+        slot = slot_of[item]
+        to = (shade * groups + (slot >> shift)) * half + ((slot & (req_count - 1)) >> 1)
+        sources[to] = ((item >> shift) ^ me) * half + ((item & (req_count - 1)) >> 1)
+        return slot
+
     def walk(pair, carry):
         def body(state):
-            item = state[0]
-            color[item] = 0
-            color[item ^ 1] = 1
-            following = order[slot_of[item ^ 1] ^ 1]
+            note(state[0], 0)
+            following = order[note(state[0] ^ 1, 1) ^ 1]
             return following, color[following]
 
         lax.while_loop(lambda state: state[1] < 0, body, (2 * pair, color[2 * pair]))
@@ -73,26 +80,10 @@
             )
     for copy in copies:
         copy.start()
-
-    def pick(group, pair, part):
-        begin = group * req_count + 2 * pair
-        return 2 * pair + (color[order[begin]] ^ part)
-
     for pair in range(half):
+        first = color[order[me * req_count + 2 * pair]]
         for part in range(2):
-            slots[part * half + pair] = pick(me, pair, part)
-
-    def trace(distance, carry):
-        group = me ^ distance
-        for pair in range(half):
-            for part in range(2):
-                item = order[group * req_count + pick(group, pair, part)]
-                origin = lax.div(item, req_count) ^ me
-                within = lax.div(lax.rem(item, req_count), 2)
-                sources[(part * groups + distance) * half + pair] = origin * half + within
-        return carry
-
-    lax.fori_loop(0, groups, trace, 0)
+            slots[part * half + pair] = 2 * pair + (first ^ part)
     for copy in copies:
         copy.wait()
 
@@ -156,11 +147,10 @@
 
 
 def project_kernel(fresh_len, held_count, part, place, source, *refs):
-    groups = (len(refs) - 7) // 2
+    groups = len(refs) - 8
     tokens = refs[:groups]
     own_rows, other_rows = refs[groups : groups + 2]
-    outs = refs[groups + 2 : 2 * groups + 2]
-    held, weights, picked, sems, weight_sems = refs[2 * groups + 2 :]
+    out, held, weights, picked, sems, weight_sems = refs[groups + 2 :]
     core = place[0]
     depth = own_rows.shape[0]
     copies = [
@@ -196,46 +186,34 @@
             jnp.bfloat16
         )
         for index in range(together):
-            outs[first + index][...] = result[index * rows : (index + 1) * rows]
-
-
-def attend_kernel(shape, place, slots, all_lengths, table, *refs):
+            out[first + index] = result[index * rows : (index + 1) * rows]
+
+
+def attend_kernel(shape, slots, all_lengths, table, *refs):
     groups, held_count, fresh_len, page, heads, part = shape
-    parts = refs[:groups]
-    bias, cosine, sine_up, sine_down, key_pool, value_pool = refs[groups : groups + 6]
-    outs = refs[-9:-6]
-    keys, values, ready, sems, out_sems, new_sems = refs[-6:]
-    core = place[0]
+    parts, bias, cosine, sine_up, sine_down, key_pool, value_pool = refs[:7]
+    outs = refs[-6:-3]
+    ready, out_sems, new_sems = refs[-3:]
     chunk = CHUNK_PAGES * page
     pairs = heads // 2
 
     slot = [slots[part * held_count + index] for index in range(held_count)]
     lengths = [all_lengths[slot[index]] for index in range(held_count)]
     counts = [pl.cdiv(lengths[index], chunk) for index in range(held_count)]
-    bases = [jnp.int32(0)]
-    for count in counts[:-1]:
-        bases.append(bases[-1] + count * CHUNK_PAGES)
-
-    def copies(index, entry):
-        number = table[slot[index], entry]
-        to = bases[index] + entry
-        return (
-            pltpu.make_async_copy(key_pool.at[number], keys.at[to], sems.at[index]),
-            pltpu.make_async_copy(value_pool.at[number], values.at[to], sems.at[index]),
-        )
-
-    for index in range(held_count):
-
-        def start(entry, carry, index=index):
-            for copy in copies(index, entry):
-                copy.start()
-            return carry
-
-        lax.fori_loop(0, counts[index] * CHUNK_PAGES, start, 0)
-
-    even = sum(parts[index][...].astype(jnp.float32) for index in range(0, groups, 2))
-    odd = sum(parts[index][...].astype(jnp.float32) for index in range(1, groups, 2))
-    halves = (jnp.where(core == 0, even, odd), jnp.where(core == 0, odd, even))
+
+    def cached(pool, index, first, pair):
+        return jnp.concatenate(
+            [
+                pool[table[slot[index], first + entry], :, starts[pair] : starts[pair] + WINDOW]
+                for entry in range(CHUNK_PAGES)
+            ],
+            axis=0,
+        )
+
+    halves = [
+        sum(parts[index].astype(jnp.float32) for index in range(side, groups, 2))
+        for side in range(2)
+    ]
     halves = [
         half + bias[:, side * half.shape[1] : (side + 1) * half.shape[1]]
         for side, half in enumerate(halves)
@@ -337,20 +315,12 @@
             axis=0,
         )
 
-        def finish(entry, carry, index=index):
-            for copy in copies(index, entry):
-                copy.wait()
-            return carry
-
-        lax.fori_loop(0, counts[index] * CHUNK_PAGES, finish, 0)
-
         def step(part, carry, index=index, spread=spread):
             peak, denom, mixed = carry
-            first = bases[index] + part * CHUNK_PAGES
-            key_block = keys[pl.ds(first, CHUNK_PAGES)].reshape(chunk, width)
+            first = part * CHUNK_PAGES
             scores = jnp.concatenate(
                 [
-                    contract(spread[pair], key_block[:, starts[pair] : starts[pair] + WINDOW])
+                    contract(spread[pair], cached(key_pool, index, first, pair))
                     for pair in range(pairs)
                 ],
                 axis=0,
@@ -362,12 +332,11 @@
             weight = jnp.exp2((scores - higher) * factor)
             denom = denom * shrink + jnp.sum(weight, axis=1, keepdims=True)
             weight = weight.astype(jnp.bfloat16)
-            value_block = values[pl.ds(first, CHUNK_PAGES)].reshape(chunk, width)
             added = jnp.concatenate(
                 [
                     jnp.dot(
                         weight[pair * 2 * fresh_len : (pair + 1) * 2 * fresh_len],
-                        value_block[:, starts[pair] : starts[pair] + WINDOW],
+                        cached(value_pool, index, first, pair),
                         preferred_element_type=jnp.float32,
                     )
                     for pair in range(pairs)
@@ -479,24 +448,27 @@
     place = jnp.stack([core]).astype(jnp.int32)
     where = jnp.stack([layer, chip]).astype(jnp.int32)
     chunk_rows = half * fresh_len
-    span = page_table.shape[1]
-    pages = span + (half - 1) * (span // 2)
     out = jax.ShapeDtypeStruct((req_count, fresh_len, heads * HEAD), jnp.bfloat16)
 
     pieces = [[chunk.reshape(chunk_rows, width)] for chunk in chunks]
     ends = [(own[0], own[0]) for own in pieces]
     downs = [[], []]
-    for hop in range(1, wgt_size):
-        for part in range(2):
+    for part in range(2):
+        for hop in range(1, wgt_size):
             up, down = ends[part]
+            if part == 1 and hop == 1:
+                up, _ = lax.optimization_barrier((up, pieces[0][min(2, wgt_size - 1)]))
+                down = up
             up = lax.ppermute(up, "wgt", [(at, at + 1) for at in range(hop - 1, wgt_size - 1)])
             down = lax.ppermute(down, "wgt", [(at + 1, at) for at in range(wgt_size - hop)])
             ends[part] = (up, down)
             pieces[part].append(up)
             downs[part].append(down)
 
-    results = []
+    projected = []
     for part in range(2):
+        if part == 1:
+            pieces[1][-1], _ = lax.optimization_barrier((pieces[1][-1], projected[0]))
         normed = pl.pallas_call(
             functools.partial(norm_kernel, wgt_size, chips),
             out_shape=[jax.ShapeDtypeStruct((chunk_rows, block), jnp.bfloat16)] * chips,
@@ -517,9 +489,9 @@
 
         partial = pl.pallas_call(
             functools.partial(project_kernel, fresh_len, half, part),
-            out_shape=[jax.ShapeDtypeStruct((chunk_rows, half_cols), jnp.bfloat16)] * req_size,
+            out_shape=jax.ShapeDtypeStruct((req_size, chunk_rows, half_cols), jnp.bfloat16),
             in_specs=[SMEM] * 2 + [ANY] * (req_size + 2),
-            out_specs=[VMEM] * req_size,
+            out_specs=VMEM,
             scratch_shapes=[
                 pltpu.VMEM((req_size * half, fresh_len, block), jnp.bfloat16),
                 pltpu.VMEM((block, half_cols), jnp.bfloat16),
@@ -537,13 +509,16 @@
             other_rows,
         )
 
-        parts = [partial[0]]
-        parts += [swap(partial[distance], distance) for distance in range(1, req_size)]
+        projected.append(partial)
+
+    results = []
+    for part in range(2):
+        parts = lax.all_to_all(projected[part], "req", 0, 0, tiled=True)
 
         operands = [
-            place, slots, lengths, page_table, *parts, bias, *tables, key_pool, value_pool
+            slots, lengths, page_table, parts, bias, *tables, key_pool, value_pool
         ]
-        specs = [SMEM] * 4 + [VMEM] * (req_size + 4) + [ANY] * 2
+        specs = [SMEM] * 3 + [VMEM] * 7
         results = pl.pallas_call(
             functools.partial(
                 attend_kernel, (req_size, half, fresh_len, page, heads, part)
@@ -552,15 +527,12 @@
             in_specs=specs + [ANY] * len(results),
             out_specs=[ANY] * 3,
             scratch_shapes=[
-                pltpu.VMEM((pages, page, heads * HEAD), jnp.bfloat16),
-                pltpu.VMEM((pages, page, heads * HEAD), jnp.bfloat16),
                 pltpu.VMEM((3, half, fresh_len, heads * HEAD), jnp.bfloat16),
-                pltpu.SemaphoreType.DMA((half,)),
                 pltpu.SemaphoreType.DMA((half,)),
                 pltpu.SemaphoreType.DMA((2, half)),
             ],
             input_output_aliases={len(specs) + index: index for index in range(len(results))},
-            compiler_params=pltpu.CompilerParams(vmem_limit_bytes=24 * MIB),
+            compiler_params=pltpu.CompilerParams(vmem_limit_bytes=30 * MIB),
             name="attend",
         )(*operands, *results)
     return results

time: 176 us -> 201 us (1.14)
  the two profiles are of different devices: /device:TPU:5 before, /device:TPU:0 now
where the time goes in v3:
time: 201 us
  waiting for transfers between devices  77.6 us (39%)
  Pallas kernels  50.9 us (25%)
  starting transfers between devices  33.7 us (17%)
  local copies, waits for them, and re-layouts  33.2 us (17%)
  other arithmetic  4.44 us (2%)
    ppermute x6, waiting for transfers between devices, per_device(): lax.ppermute(down, 'wgt', [(at + 1, at) for at in range(wgt_size - hop)])  37.8 us
    unnamed x62, local copies, waits for them, and re-layouts  29 us
    ppermute x15, waiting for transfers between devices, swap(): lax.ppermute(value, 'req', [(device, device ^ distance) for device in ran...  23.8 us
    pallas_call x1, Pallas kernels, per_device(): pl.pallas_call(functools.partial(plan_kernel, req_count), out_shape=[jax....  21.2 us
    pallas_call x2, Pallas kernels, per_device(): pl.pallas_call(functools.partial(attend_kernel, (req_size, half, fresh_le...  13.4 us
    ppermute x6, waiting for transfers between devices, per_device(): lax.ppermute(up, 'wgt', [(at, at + 1) for at in range(hop - 1, wgt_size -...  11.9 us
    ppermute x6, starting transfers between devices, per_device(): lax.ppermute(up, 'wgt', [(at, at + 1) for at in range(hop - 1, wgt_size -...  10.2 us
    pallas_call x2, Pallas kernels, per_device(): pl.pallas_call(functools.partial(project_kernel, fresh_len, half, part),...  10.1 us
  transfers between devices with their start and end apart: 29, of which 17 were waited for; matrix products, arithmetic and copies ran while one was open for 3% of the time, Pallas kernels for 19%

profile of v3, /device:TPU:0, one launch (start us, length us, event | category | flops | bytes accessed | tf_op | source)
XLA Modules:
  0.0 201.0 jit_solution(10798393194670166578)
XLA Ops:
  0.6 3.5 %constant_dynamic-slice_fusion = (bf16[768,1152]{1,0:T(8,128)(2,1)}, bf16[768,1152]{1,0:T(8,128)(2,1)S(1)}) fusion(bf16[768,2304]{1,0:T(8,128)(2,1)} %param.20, s32[]{:T(128)S(6)} %select_n.20, s32[]{:T(128)S(6)} %select_n.19), kind=kLoop, calls=%fused_computation.8 | loop fusion | bytes 7077896 | tf_op jit(solution)/shard_map/dynamic_slice | solution.py:404
  4.6 21.2 %plan.1 = (s32[4]{0:T(128)}, s32[32]{0:T(128)}, bf16[2,48,1536]{2,1,0:T(8,128)(2,1)}, bf16[2,48,1536]{2,1,0:T(8,128)(2,1)}) custom-call(s32[1]{0:T(128)} %bitcast.place, s32[32]{0:T(128)} %group_of.1, bf16[4,48,1536]{2,1,0:T(8,128)(2,1)} %arrivals.1), custom_call_target="tpu_custom_call" | custom-call | tf_op jit(solution)/shard_map/plan/pallas_call | solution.py:408
  25.9 4.5 %collective-permute-start = (bf16[96,1536]{1,0:T(8,128)(2,1)}, bf16[96,1536]{1,0:T(8,128)(2,1)S(1)}, u32[]{:S(2)}, u32[]{:S(2)}) collective-permute-start(bf16[96,1536]{1,0:T(8,128)(2,1)} %bitcast.29), channel_id=1, source_target_pairs={{0,1},{1,2},{2,3},{4,5},{5,6},{6,7},{8,9},{9,10},{10,11},{12,13},{... | collective-permute-start | bytes 884744 | tf_op jit(solution)/shard_map/ppermute | solution.py:462
  30.4 1.3 collective-permute-start.6
  31.7 5.9 %collective-permute-done.refs_1_ = bf16[96,1536]{1,0:T(8,128)(2,1)S(1)} collective-permute-done((bf16[96,1536]{1,0:T(8,128)(2,1)}, bf16[96,1536]{1,0:T(8,128)(2,1)S(1)}, u32[]{:S(2)}, u32[]{:S(2)}) %collective-permute-start) | collective-permute-done | bytes 294944 | tf_op jit(solution)/shard_map/ppermute | solution.py:462
  37.6 1.4 collective-permute-start.1
  39.0 0.7 copy-done.16
  39.7 1.9 collective-permute-done.6.refs_4_
  41.6 1.3 collective-permute-start.7
  42.9 0.7 copy-done.18
  43.6 1.4 collective-permute-start.5
  45.0 8.5 %collective-permute-done.7.refs_5_ = bf16[96,1536]{1,0:T(8,128)(2,1)} collective-permute-done((bf16[96,1536]{1,0:T(8,128)(2,1)S(1)}, bf16[96,1536]{1,0:T(8,128)(2,1)}, u32[]{:S(2)}, u32[]{:S(2)}) %collective-permute-start.7) | collective-permute-done | bytes 294944 | tf_op jit(solution)/shard_map/ppermute | solution.py:463
  53.5 1.3 collective-permute-start.8
  54.8 0.7 reshape.166
  55.6 7.8 %collective-permute-done.8.refs_6_ = bf16[96,1536]{1,0:T(8,128)(2,1)} collective-permute-done((bf16[96,1536]{1,0:T(8,128)(2,1)}, bf16[96,1536]{1,0:T(8,128)(2,1)}, u32[]{:S(2)}, u32[]{:S(2)}) %collective-permute-start.8) | collective-permute-done | bytes 294944 | tf_op jit(solution)/shard_map/ppermute | solution.py:463
  63.5 1.0 copy-done.15
  64.4 1.0 copy-done.17
  65.4 1.0 copy-done.19
  66.3 3.5 %norm.2 = (bf16[96,1536]{1,0:T(8,128)(2,1)S(1)}, bf16[96,1536]{1,0:T(8,128)(2,1)S(1)}, bf16[96,1536]{1,0:T(8,128)(2,1)S(1)}, bf16[96,1536]{1,0:T(8,128)(2,1)S(1)}) custom-call(s32[2]{0:T(128)S(1)} %pad_add_fusion.place, bf16[96,1536]{1,0:T(8,128)(2,1)S(1)} %bitcast.31, bf16[96,1536]{1,0:T(8,128)(2,1)S(1)} %copy-done.17, ...), custom_call_target="tpu_custom_call" | custom-call | tf_op jit(solution)/shard_map/norm/pallas_call | solution.py:472
  69.9 1.6 collective-permute-start.10
  71.4 1.5 collective-permute-start.12
  73.4 6.5 %collective-permute-done.10 = bf16[96,1536]{1,0:T(8,128)(2,1)S(1)} collective-permute-done((bf16[96,1536]{1,0:T(8,128)(2,1)S(1)}, bf16[96,1536]{1,0:T(8,128)(2,1)S(1)}, u32[]{:S(2)}, u32[]{:S(2)}) %collective-permute-start.10) | collective-permute-done | bytes 294944 | tf_op jit(solution)/shard_map/ppermute | solution.py:399
  79.9 4.4 %collective-permute-done.12 = bf16[96,1536]{1,0:T(8,128)(2,1)S(1)} collective-permute-done((bf16[96,1536]{1,0:T(8,128)(2,1)S(1)}, bf16[96,1536]{1,0:T(8,128)(2,1)S(1)}, u32[]{:S(2)}, u32[]{:S(2)}) %collective-permute-start.12) | collective-permute-done | bytes 294944 | tf_op jit(solution)/shard_map/ppermute | solution.py:399
  84.8 1.1 collective-permute-done.13
  86.3 5.1 %project.2 = bf16[8,96,1152]{2,1,0:T(8,128)(2,1)S(1)} custom-call(s32[1]{0:T(128)} %bitcast.1.place, s32[32]{0:T(128)S(1)} %copy-done.29, bf16[2,48,1536]{2,1,0:T(8,128)(2,1)S(1)} %bitcast.28, bf16[2,48,1536]{2,1,0:T(8,128)(2,1)S(1)} %bitcast.38, bf16[2,48,1536]{2,1,0:T(8,128)(2,1)S(1)} %bitcast.32, bf16[2,48,1536]{2,1,0:T(8,128)(2,1)S(1)} %bitcast.40, ...), custom_call_target="tpu_custom_call" | custom-call | tf_op jit(solution)/shard_map/project/pallas_call | solution.py:490
  91.4 1.2 copy-done.4
  92.6 3.6 %all-to-all-start.1 = ((bf16[8,96,1152]{2,1,0:T(8,128)(2,1)}), bf16[8,96,1152]{2,1,0:T(8,128)(2,1)S(1)}, u32[]{:S(2)}, u32[]{:S(2)}) async-start(bf16[8,96,1152]{2,1,0:T(8,128)(2,1)} %copy-done.4), calls=%async_computation.1 | async-start | bytes 3538944 | tf_op jit(solution)/shard_map/all_to_all | solution.py:516
  96.3 1.6 collective-permute-start.2
  97.9 1.3 collective-permute-start.17
  99.2 5.9 %collective-permute-done.2.refs_1_ = bf16[96,1536]{1,0:T(8,128)(2,1)S(1)} collective-permute-done((bf16[96,1536]{1,0:T(8,128)(2,1)}, bf16[96,1536]{1,0:T(8,128)(2,1)S(1)}, u32[]{:S(2)}, u32[]{:S(2)}) %collective-permute-start.2) | collective-permute-done | bytes 294944 | tf_op jit(solution)/shard_map/ppermute | solution.py:462
  105.8 3.3 %collective-permute-done.17.refs_4_ = bf16[96,1536]{1,0:T(8,128)(2,1)S(1)} collective-permute-done((bf16[96,1536]{1,0:T(8,128)(2,1)}, bf16[96,1536]{1,0:T(8,128)(2,1)S(1)}, u32[]{:S(2)}, u32[]{:S(2)}) %collective-permute-start.17) | collective-permute-done | bytes 294944 | tf_op jit(solution)/shard_map/ppermute | solution.py:463
  109.1 1.3 collective-permute-start.18
  111.1 8.2 %collective-permute-done.18.refs_5_ = bf16[96,1536]{1,0:T(8,128)(2,1)S(1)} collective-permute-done((bf16[96,1536]{1,0:T(8,128)(2,1)S(1)}, bf16[96,1536]{1,0:T(8,128)(2,1)S(1)}, u32[]{:S(2)}, u32[]{:S(2)}) %collective-permute-start.18) | collective-permute-done | bytes 294944 | tf_op jit(solution)/shard_map/ppermute | solution.py:463
  119.3 1.3 collective-permute-start.19
  120.6 8.0 %collective-permute-done.19.refs_6_ = bf16[96,1536]{1,0:T(8,128)(2,1)S(1)} collective-permute-done((bf16[96,1536]{1,0:T(8,128)(2,1)S(1)}, bf16[96,1536]{1,0:T(8,128)(2,1)S(1)}, u32[]{:S(2)}, u32[]{:S(2)}) %collective-permute-start.19) | collective-permute-done | bytes 294944 | tf_op jit(solution)/shard_map/ppermute | solution.py:463
  128.6 1.0 copy-done.14
  129.6 0.7 copy-done.21
  130.3 0.7 copy-done.23
  131.0 2.6 %norm.3 = (bf16[96,1536]{1,0:T(8,128)(2,1)S(1)}, bf16[96,1536]{1,0:T(8,128)(2,1)S(1)}, bf16[96,1536]{1,0:T(8,128)(2,1)S(1)}, bf16[96,1536]{1,0:T(8,128)(2,1)S(1)}) custom-call(s32[2]{0:T(128)S(1)} %pad_add_fusion.place, bf16[96,1536]{1,0:T(8,128)(2,1)S(1)} %bitcast.26, bf16[96,1536]{1,0:T(8,128)(2,1)S(1)} %collective-permute-done.2.refs_1_, ...), custom_call_target="tpu_custom_call" | custom-call | tf_op jit(solution)/shard_map/norm/pallas_call | solution.py:472
  133.7 1.3 collective-permute-start.21
  134.9 1.5 collective-permute-start.23
  136.4 0.8 collective-permute-start.25
  137.2 6.2 %collective-permute-done.21 = bf16[96,1536]{1,0:T(8,128)(2,1)S(1)} collective-permute-done((bf16[96,1536]{1,0:T(8,128)(2,1)S(1)}, bf16[96,1536]{1,0:T(8,128)(2,1)S(1)}, u32[]{:S(2)}, u32[]{:S(2)}) %collective-permute-start.21) | collective-permute-done | bytes 294944 | tf_op jit(solution)/shard_map/ppermute | solution.py:399
  143.4 3.8 %collective-permute-done.23 = bf16[96,1536]{1,0:T(8,128)(2,1)S(1)} collective-permute-done((bf16[96,1536]{1,0:T(8,128)(2,1)S(1)}, bf16[96,1536]{1,0:T(8,128)(2,1)S(1)}, u32[]{:S(2)}, u32[]{:S(2)}) %collective-permute-start.23) | collective-permute-done | bytes 294944 | tf_op jit(solution)/shard_map/ppermute | solution.py:399
  147.7 1.1 collective-permute-done.24
  149.2 5.1 %project.3 = bf16[8,96,1152]{2,1,0:T(8,128)(2,1)S(1)} custom-call(s32[1]{0:T(128)} %bitcast.1.place, s32[32]{0:T(128)S(1)} %copy-done.29, bf16[2,48,1536]{2,1,0:T(8,128)(2,1)S(1)} %bitcast.27, bf16[2,48,1536]{2,1,0:T(8,128)(2,1)S(1)} %bitcast.39, bf16[2,48,1536]{2,1,0:T(8,128)(2,1)S(1)} %bitcast.33, bf16[2,48,1536]{2,1,0:T(8,128)(2,1)S(1)} %bitcast.41, ...), custom_call_target="tpu_custom_call" | custom-call | tf_op jit(solution)/shard_map/project/pallas_call | solution.py:490
  154.3 1.2 copy-done.5
  155.5 3.6 %all-to-all-start = ((bf16[8,96,1152]{2,1,0:T(8,128)(2,1)}), bf16[8,96,1152]{2,1,0:T(8,128)(2,1)S(1)}, u32[]{:S(2)}, u32[]{:S(2)}) async-start(bf16[8,96,1152]{2,1,0:T(8,128)(2,1)} %copy-done.5), calls=%async_computation | async-start | bytes 3538944 | tf_op jit(solution)/shard_map/all_to_all | solution.py:516
  159.1 0.7 reshape.169.refs_1_
  159.8 0.7 add_convert_fusion
  160.5 2.9 %fusion = (f32[4,48,768]{2,1,0:T(8,128)S(1)}, f32[4,48,768]{2,1,0:T(8,128)S(1)}, f32[4,48,768]{2,1,0:T(8,128)S(1)}) fusion(f32[768]{0:T(1024)} %constant.45, f32[4,48]{1,0:T(4,128)S(1)} %add_convert_fusion, pred[768]{0:T(1024)(128)(4,1)} %constant.46, pred[768]{0:T(1024)(128)(4,1)} %constant.38.clone, pred[768]{0:T(1024)(128)(4,1)} %constant.37.clone), kind=kLoop, calls=%fused_computation.2 | loop fusion | flops 737280 | bytes 1775616 | tf_op jit(solution)/shard_map/jit(_where)/select_n | solution.py:439
  163.5 3.2 %copy-done = bf16[40,128,768]{2,1,0:T(8,128)(2,1)S(1)} copy-done((bf16[40,128,768]{2,1,0:T(8,128)(2,1)S(1)}, bf16[40,128,768]{2,1,0:T(8,128)(2,1)}, u32[]{:S(2)}) %copy-start) | copy-done | bytes 7864344
  166.7 3.2 %copy-done.2 = bf16[40,128,768]{2,1,0:T(8,128)(2,1)S(1)} copy-done((bf16[40,128,768]{2,1,0:T(8,128)(2,1)S(1)}, bf16[40,128,768]{2,1,0:T(8,128)(2,1)}, u32[]{:S(2)}) %copy-start.2) | copy-done | bytes 7864344
  170.0 5.6 %attend.2 = (bf16[4,48,768]{2,1,0:T(8,128)(2,1)}, bf16[4,48,768]{2,1,0:T(8,128)(2,1)}, bf16[4,48,768]{2,1,0:T(8,128)(2,1)}) custom-call(s32[4]{0:T(128)S(1)} %copy-done.27, s32[4]{0:T(128)S(1)} %copy-done.25, s32[4,16]{1,0:T(4,128)S(1)} %copy-done.24, bf16[8,96,1152]{2,1,0:T(8,128)(2,1)S(1)} %all-to-all-done.1.refs_0_, f32[1,2304]{1,0:T(1,128)S(1)} %reshape.169.refs_1_, ...), custom_call_target="tpu_custom_call" | custom-call | tf_op jit(solution)/shard_map/attend/pallas_call | solution.py:522
  175.6 0.8 copy-done.8
  176.4 0.8 copy-done.10
  177.2 0.8 copy-done.12
  178.0 4.1 %all-to-all-done.refs_0_ = bf16[8,96,1152]{2,1,0:T(8,128)(2,1)S(1)} async-done(((bf16[8,96,1152]{2,1,0:T(8,128)(2,1)}), bf16[8,96,1152]{2,1,0:T(8,128)(2,1)S(1)}, u32[]{:S(2)}, u32[]{:S(2)}) %all-to-all-start) | async-done | bytes 1769504 | tf_op jit(solution)/shard_map/all_to_all | solution.py:516
  182.1 3.2 %copy-done.1 = bf16[40,128,768]{2,1,0:T(8,128)(2,1)S(1)} copy-done((bf16[40,128,768]{2,1,0:T(8,128)(2,1)S(1)}, bf16[40,128,768]{2,1,0:T(8,128)(2,1)}, u32[]{:S(2)}) %copy-start.1) | copy-done | bytes 7864344
  185.4 3.2 %copy-done.3 = bf16[40,128,768]{2,1,0:T(8,128)(2,1)S(1)} copy-done((bf16[40,128,768]{2,1,0:T(8,128)(2,1)S(1)}, bf16[40,128,768]{2,1,0:T(8,128)(2,1)}, u32[]{:S(2)}) %copy-start.3) | copy-done | bytes 7864344
  188.6 1.1 copy-done.9
  189.7 1.1 copy-done.11
  190.7 1.1 copy-done.13
  193.0 7.8 %attend.3 = (bf16[4,48,768]{2,1,0:T(8,128)(2,1)}, bf16[4,48,768]{2,1,0:T(8,128)(2,1)}, bf16[4,48,768]{2,1,0:T(8,128)(2,1)}) custom-call(s32[4]{0:T(128)S(1)} %copy-done.28, s32[4]{0:T(128)S(1)} %copy-done.26, s32[4,16]{1,0:T(4,128)S(1)} %copy-done.24, ...), custom_call_target="tpu_custom_call", output_to_operand_aliasing={{0}: (10, {}), {1}: (11, {}), {2}: (12, {})} | custom-call | tf_op jit(solution)/shard_map/attend/pallas_call | solution.py:522
  (70 shorter events, 5.6 us)
Async XLA Ops:
  0.6 54.2 %copy-start.30 = (bf16[6144]{0:T(1024)(128)(2,1)S(1)}, bf16[6144]{0:T(1024)(128)(2,1)}, u32[]{:S(2)}) copy-start(bf16[6144]{0:T(1024)(128)(2,1)} %param.18) | copy-start | bytes 36868
  4.2 82.1 %collective-permute-start.16 = (bf16[768,1152]{1,0:T(8,128)(2,1)}, bf16[768,1152]{1,0:T(8,128)(2,1)S(1)}, u32[]{:S(2)}, u32[]{:S(2)}) collective-permute-start(bf16[768,1152]{1,0:T(8,128)(2,1)} %get-tuple-element.37), channel_id=1, source_target_pairs={{0,4},{4,0},{8,12},{12,8},{16,20},{20,16},{24,28},{28,24},{1,5},{5... | collective-permute-start | bytes 5308424 | tf_op jit(solution)/shard_map/ppermute | solution.py:399
  25.9 60.5 %copy-start.29 = (s32[32]{0:T(128)S(1)}, s32[32]{0:T(128)}, u32[]{:S(2)}) copy-start(s32[32]{0:T(128)} %get-tuple-element.21.source) | copy-start | bytes 388
  25.9 11.7 %collective-permute-start = (bf16[96,1536]{1,0:T(8,128)(2,1)}, bf16[96,1536]{1,0:T(8,128)(2,1)S(1)}, u32[]{:S(2)}, u32[]{:S(2)}) collective-permute-start(bf16[96,1536]{1,0:T(8,128)(2,1)} %bitcast.29), channel_id=1, source_target_pairs={{0,1},{1,2},{2,3},{4,5},{5,6},{6,7},{8,9},{9,10},{10,11},{12,13},{... | collective-permute-start | bytes 884744 | tf_op jit(solution)/shard_map/ppermute | solution.py:462
  30.4 11.2 %collective-permute-start.6 = (bf16[96,1536]{1,0:T(8,128)(2,1)}, bf16[96,1536]{1,0:T(8,128)(2,1)S(1)}, u32[]{:S(2)}, u32[]{:S(2)}) collective-permute-start(bf16[96,1536]{1,0:T(8,128)(2,1)} %bitcast.30), channel_id=1, source_target_pairs={{1,0},{2,1},{3,2},{5,4},{6,5},{7,6},{9,8},{10,9},{11,10},{13,12},{... | collective-permute-start | bytes 884744 | tf_op jit(solution)/shard_map/ppermute | solution.py:463
  37.6 6.0 %collective-permute-start.1 = (bf16[96,1536]{1,0:T(8,128)(2,1)S(1)}, bf16[96,1536]{1,0:T(8,128)(2,1)}, u32[]{:S(2)}, u32[]{:S(2)}) collective-permute-start(bf16[96,1536]{1,0:T(8,128)(2,1)S(1)} %collective-permute-done.refs_1_), channel_id=1, source_target_pairs={{1,2},{2,3},{5,6},{6,7},{9,10},{10,11},{13,14},{14,15},{17,18},{18... | collective-permute-start | bytes 884744 | tf_op jit(solution)/shard_map/ppermute | solution.py:462
  39.0 0.7 copy-start.16
  41.6 11.9 %collective-permute-start.7 = (bf16[96,1536]{1,0:T(8,128)(2,1)S(1)}, bf16[96,1536]{1,0:T(8,128)(2,1)}, u32[]{:S(2)}, u32[]{:S(2)}) collective-permute-start(bf16[96,1536]{1,0:T(8,128)(2,1)S(1)} %collective-permute-done.6.refs_4_), channel_id=1, source_target_pairs={{1,0},{2,1},{5,4},{6,5},{9,8},{10,9},{13,12},{14,13},{17,16},{18,1... | collective-permute-start | bytes 884744 | tf_op jit(solution)/shard_map/ppermute | solution.py:463
  42.9 0.7 copy-start.18
  43.6 12.0 %collective-permute-start.5 = (bf16[96,1536]{1,0:T(8,128)(2,1)}, bf16[96,1536]{1,0:T(8,128)(2,1)}, u32[]{:S(2)}, u32[]{:S(2)}) collective-permute-start(bf16[96,1536]{1,0:T(8,128)(2,1)} %collective-permute-done.1.refs_2_), channel_id=1, source_target_pairs={{2,3},{6,7},{10,11},{14,15},{18,19},{22,23},{26,27},{30,31}} | collective-permute-start | bytes 884744 | tf_op jit(solution)/shard_map/ppermute | solution.py:462
  53.5 9.9 %collective-permute-start.8 = (bf16[96,1536]{1,0:T(8,128)(2,1)}, bf16[96,1536]{1,0:T(8,128)(2,1)}, u32[]{:S(2)}, u32[]{:S(2)}) collective-permute-start(bf16[96,1536]{1,0:T(8,128)(2,1)} %collective-permute-done.7.refs_5_), channel_id=1, source_target_pairs={{1,0},{5,4},{9,8},{13,12},{17,16},{21,20},{25,24},{29,28}} | collective-permute-start | bytes 884744 | tf_op jit(solution)/shard_map/ppermute | solution.py:463
  54.8 31.5 %copy-start.20 = (f32[6144]{0:T(1024)}, f32[6144]{0:T(1024)S(1)}, u32[]{:S(2)}) copy-start(f32[6144]{0:T(1024)S(1)} %reshape.164) | copy-start | bytes 73732
  55.5 30.8 %copy-start.22 = (f32[6144]{0:T(1024)}, f32[6144]{0:T(1024)S(1)}, u32[]{:S(2)}) copy-start(f32[6144]{0:T(1024)S(1)} %reshape.166) | copy-start | bytes 73732
  63.5 1.0 copy-start.15
  64.4 1.0 copy-start.17
  65.4 1.0 copy-start.19
  69.9 10.0 %collective-permute-start.10 = (bf16[96,1536]{1,0:T(8,128)(2,1)S(1)}, bf16[96,1536]{1,0:T(8,128)(2,1)S(1)}, u32[]{:S(2)}, u32[]{:S(2)}) collective-permute-start(bf16[96,1536]{1,0:T(8,128)(2,1)S(1)} %get-tuple-element.26), channel_id=1, source_target_pairs={{0,8},{4,12},{8,0},{12,4},{16,24},{20,28},{24,16},{28,20},{1,9},{5... | collective-permute-start | bytes 884744 | tf_op jit(solution)/shard_map/ppermute | solution.py:399
  71.4 12.9 %collective-permute-start.12 = (bf16[96,1536]{1,0:T(8,128)(2,1)S(1)}, bf16[96,1536]{1,0:T(8,128)(2,1)S(1)}, u32[]{:S(2)}, u32[]{:S(2)}) collective-permute-start(bf16[96,1536]{1,0:T(8,128)(2,1)S(1)} %get-tuple-element.27), channel_id=1, source_target_pairs={{0,16},{4,20},{8,24},{12,28},{16,0},{20,4},{24,8},{28,12},{1,17},{... | collective-permute-start | bytes 884744 | tf_op jit(solution)/shard_map/ppermute | solution.py:399
  72.9 11.4 %collective-permute-start.14 = (bf16[96,1536]{1,0:T(8,128)(2,1)S(1)}, bf16[96,1536]{1,0:T(8,128)(2,1)S(1)}, u32[]{:S(2)}, u32[]{:S(2)}) collective-permute-start(bf16[96,1536]{1,0:T(8,128)(2,1)S(1)} %get-tuple-element.28), channel_id=1, source_target_pairs={{0,24},{4,28},{8,16},{12,20},{16,8},{20,12},{24,0},{28,4},{1,25},{... | collective-permute-start | bytes 884744 | tf_op jit(solution)/shard_map/ppermute | solution.py:399
  73.4 11.4 %collective-permute-start.9 = (bf16[96,1536]{1,0:T(8,128)(2,1)S(1)}, bf16[96,1536]{1,0:T(8,128)(2,1)S(1)}, u32[]{:S(2)}, u32[]{:S(2)}) collective-permute-start(bf16[96,1536]{1,0:T(8,128)(2,1)S(1)} %get-tuple-element.25), channel_id=1, source_target_pairs={{0,4},{4,0},{8,12},{12,8},{16,20},{20,16},{24,28},{28,24},{1,5},{5... | collective-permute-start | bytes 884744 | tf_op jit(solution)/shard_map/ppermute | solution.py:399
  79.9 4.9 %collective-permute-start.11 = (bf16[96,1536]{1,0:T(8,128)(2,1)S(1)}, bf16[96,1536]{1,0:T(8,128)(2,1)S(1)}, u32[]{:S(2)}, u32[]{:S(2)}) collective-permute-start(bf16[96,1536]{1,0:T(8,128)(2,1)S(1)} %collective-permute-done.10), channel_id=1, source_target_pairs={{0,4},{4,0},{8,12},{12,8},{16,20},{20,16},{24,28},{28,24},{1,5},{5... | collective-permute-start | bytes 884744 | tf_op jit(solution)/shard_map/ppermute | solution.py:399
  84.3 1.6 collective-permute-start.13
  84.3 2.0 collective-permute-start.15
  86.3 5.1 %copy-start.6 = (bf16[768,1152]{1,0:T(8,128)(2,1)}, bf16[768,1152]{1,0:T(8,128)(2,1)S(1)}, u32[]{:S(2)}) copy-start(bf16[768,1152]{1,0:T(8,128)(2,1)S(1)} %collective-permute-done.16.refs_9_) | copy-start | bytes 5308420
  91.4 1.2 copy-start.4
  92.6 62.8 %all-to-all-start.1 = ((bf16[8,96,1152]{2,1,0:T(8,128)(2,1)}), bf16[8,96,1152]{2,1,0:T(8,128)(2,1)S(1)}, u32[]{:S(2)}, u32[]{:S(2)}) async-start(bf16[8,96,1152]{2,1,0:T(8,128)(2,1)} %copy-done.4), calls=%async_computation.1 | async-start | bytes 3538944 | tf_op jit(solution)/shard_map/all_to_all | solution.py:516
  96.2 53.0 %copy-start.7 = (bf16[768,1152]{1,0:T(8,128)(2,1)S(1)}, bf16[768,1152]{1,0:T(8,128)(2,1)}, u32[]{:S(2)}) copy-start(bf16[768,1152]{1,0:T(8,128)(2,1)} %copy-done.6) | copy-start | bytes 5308420
  96.3 8.8 %collective-permute-start.2 = (bf16[96,1536]{1,0:T(8,128)(2,1)}, bf16[96,1536]{1,0:T(8,128)(2,1)S(1)}, u32[]{:S(2)}, u32[]{:S(2)}) collective-permute-start(bf16[96,1536]{1,0:T(8,128)(2,1)} %bitcast.24), channel_id=1, source_target_pairs={{0,1},{1,2},{2,3},{4,5},{5,6},{6,7},{8,9},{9,10},{10,11},{12,13},{... | collective-permute-start | bytes 884744 | tf_op jit(solution)/shard_map/ppermute | solution.py:462
  97.9 11.2 %collective-permute-start.17 = (bf16[96,1536]{1,0:T(8,128)(2,1)}, bf16[96,1536]{1,0:T(8,128)(2,1)S(1)}, u32[]{:S(2)}, u32[]{:S(2)}) collective-permute-start(bf16[96,1536]{1,0:T(8,128)(2,1)} %bitcast.25), channel_id=1, source_target_pairs={{1,0},{2,1},{3,2},{5,4},{6,5},{7,6},{9,8},{10,9},{11,10},{13,12},{... | collective-permute-start | bytes 884744 | tf_op jit(solution)/shard_map/ppermute | solution.py:463
  105.1 5.3 %collective-permute-start.3 = (bf16[96,1536]{1,0:T(8,128)(2,1)S(1)}, bf16[96,1536]{1,0:T(8,128)(2,1)S(1)}, u32[]{:S(2)}, u32[]{:S(2)}) collective-permute-start(bf16[96,1536]{1,0:T(8,128)(2,1)S(1)} %collective-permute-done.2.refs_1_), channel_id=1, source_target_pairs={{1,2},{2,3},{5,6},{6,7},{9,10},{10,11},{13,14},{14,15},{17,18},{18... | collective-permute-start | bytes 884744 | tf_op jit(solution)/shard_map/ppermute | solution.py:462
  109.1 10.2 %collective-permute-start.18 = (bf16[96,1536]{1,0:T(8,128)(2,1)S(1)}, bf16[96,1536]{1,0:T(8,128)(2,1)S(1)}, u32[]{:S(2)}, u32[]{:S(2)}) collective-permute-start(bf16[96,1536]{1,0:T(8,128)(2,1)S(1)} %collective-permute-done.17.refs_4_), channel_id=1, source_target_pairs={{1,0},{2,1},{5,4},{6,5},{9,8},{10,9},{13,12},{14,13},{17,16},{18,1... | collective-permute-start | bytes 884744 | tf_op jit(solution)/shard_map/ppermute | solution.py:463
  110.4 10.2 %collective-permute-start.4 = (bf16[96,1536]{1,0:T(8,128)(2,1)S(1)}, bf16[96,1536]{1,0:T(8,128)(2,1)S(1)}, u32[]{:S(2)}, u32[]{:S(2)}) collective-permute-start(bf16[96,1536]{1,0:T(8,128)(2,1)S(1)} %collective-permute-done.3.refs_2_), channel_id=1, source_target_pairs={{2,3},{6,7},{10,11},{14,15},{18,19},{22,23},{26,27},{30,31}} | collective-permute-start | bytes 884744 | tf_op jit(solution)/shard_map/ppermute | solution.py:462
  119.3 9.3 %collective-permute-start.19 = (bf16[96,1536]{1,0:T(8,128)(2,1)S(1)}, bf16[96,1536]{1,0:T(8,128)(2,1)S(1)}, u32[]{:S(2)}, u32[]{:S(2)}) collective-permute-start(bf16[96,1536]{1,0:T(8,128)(2,1)S(1)} %collective-permute-done.18.refs_5_), channel_id=1, source_target_pairs={{1,0},{5,4},{9,8},{13,12},{17,16},{21,20},{25,24},{29,28}} | collective-permute-start | bytes 884744 | tf_op jit(solution)/shard_map/ppermute | solution.py:463
  128.6 1.0 copy-start.14
  129.6 0.7 copy-start.21
  130.3 0.7 copy-start.23
  133.7 9.7 %collective-permute-start.21 = (bf16[96,1536]{1,0:T(8,128)(2,1)S(1)}, bf16[96,1536]{1,0:T(8,128)(2,1)S(1)}, u32[]{:S(2)}, u32[]{:S(2)}) collective-permute-start(bf16[96,1536]{1,0:T(8,128)(2,1)S(1)} %get-tuple-element.31), channel_id=1, source_target_pairs={{0,8},{4,12},{8,0},{12,4},{16,24},{20,28},{24,16},{28,20},{1,9},{5... | collective-permute-start | bytes 884744 | tf_op jit(solution)/shard_map/ppermute | solution.py:399
  134.9 12.3 %collective-permute-start.23 = (bf16[96,1536]{1,0:T(8,128)(2,1)S(1)}, bf16[96,1536]{1,0:T(8,128)(2,1)S(1)}, u32[]{:S(2)}, u32[]{:S(2)}) collective-permute-start(bf16[96,1536]{1,0:T(8,128)(2,1)S(1)} %get-tuple-element.32), channel_id=1, source_target_pairs={{0,16},{4,20},{8,24},{12,28},{16,0},{20,4},{24,8},{28,12},{1,17},{... | collective-permute-start | bytes 884744 | tf_op jit(solution)/shard_map/ppermute | solution.py:399
  136.4 10.8 %collective-permute-start.25 = (bf16[96,1536]{1,0:T(8,128)(2,1)S(1)}, bf16[96,1536]{1,0:T(8,128)(2,1)S(1)}, u32[]{:S(2)}, u32[]{:S(2)}) collective-permute-start(bf16[96,1536]{1,0:T(8,128)(2,1)S(1)} %get-tuple-element.33), channel_id=1, source_target_pairs={{0,24},{4,28},{8,16},{12,20},{16,8},{20,12},{24,0},{28,4},{1,25},{... | collective-permute-start | bytes 884744 | tf_op jit(solution)/shard_map/ppermute | solution.py:399
  137.2 10.5 %collective-permute-start.20 = (bf16[96,1536]{1,0:T(8,128)(2,1)S(1)}, bf16[96,1536]{1,0:T(8,128)(2,1)S(1)}, u32[]{:S(2)}, u32[]{:S(2)}) collective-permute-start(bf16[96,1536]{1,0:T(8,128)(2,1)S(1)} %get-tuple-element.30), channel_id=1, source_target_pairs={{0,4},{4,0},{8,12},{12,8},{16,20},{20,16},{24,28},{28,24},{1,5},{5... | collective-permute-start | bytes 884744 | tf_op jit(solution)/shard_map/ppermute | solution.py:399
  143.4 4.3 %collective-permute-start.22 = (bf16[96,1536]{1,0:T(8,128)(2,1)S(1)}, bf16[96,1536]{1,0:T(8,128)(2,1)S(1)}, u32[]{:S(2)}, u32[]{:S(2)}) collective-permute-start(bf16[96,1536]{1,0:T(8,128)(2,1)S(1)} %collective-permute-done.21), channel_id=1, source_target_pairs={{0,4},{4,0},{8,12},{12,8},{16,20},{20,16},{24,28},{28,24},{1,5},{5... | collective-permute-start | bytes 884744 | tf_op jit(solution)/shard_map/ppermute | solution.py:399
  147.2 1.6 collective-permute-start.24
  147.2 2.0 collective-permute-start.26
  154.3 1.2 copy-start.5
  155.5 26.7 %all-to-all-start = ((bf16[8,96,1152]{2,1,0:T(8,128)(2,1)}), bf16[8,96,1152]{2,1,0:T(8,128)(2,1)S(1)}, u32[]{:S(2)}, u32[]{:S(2)}) async-start(bf16[8,96,1152]{2,1,0:T(8,128)(2,1)} %copy-done.5), calls=%async_computation | async-start | bytes 3538944 | tf_op jit(solution)/shard_map/all_to_all | solution.py:516
  159.1 4.4 %copy-start.24 = (s32[4,16]{1,0:T(4,128)S(1)}, s32[4,16]{1,0:T(4,128)}, u32[]{:S(2)}) copy-start(s32[4,16]{1,0:T(4,128)} %table.3) | copy-start | bytes 772
  159.1 4.4 %copy-start.25 = (s32[4]{0:T(128)S(1)}, s32[4]{0:T(128)}, u32[]{:S(2)}) copy-start(s32[4]{0:T(128)} %all_lengths.3) | copy-start | bytes 52
  159.1 4.4 %copy-start.27 = (s32[4]{0:T(128)S(1)}, s32[4]{0:T(128)}, u32[]{:S(2)}) copy-start(s32[4]{0:T(128)} %get-tuple-element.20.slots) | copy-start | bytes 52
  163.5 3.2 %copy-start = (bf16[40,128,768]{2,1,0:T(8,128)(2,1)S(1)}, bf16[40,128,768]{2,1,0:T(8,128)(2,1)}, u32[]{:S(2)}) copy-start(bf16[40,128,768]{2,1,0:T(8,128)(2,1)} %refs_5_.3) | copy-start | bytes 23592964
  166.7 3.2 %copy-start.2 = (bf16[40,128,768]{2,1,0:T(8,128)(2,1)S(1)}, bf16[40,128,768]{2,1,0:T(8,128)(2,1)}, u32[]{:S(2)}) copy-start(bf16[40,128,768]{2,1,0:T(8,128)(2,1)} %refs_6_.3) | copy-start | bytes 23592964
  175.5 0.8 copy-start.8
  176.4 0.8 copy-start.10
  177.2 0.8 copy-start.12
  182.1 3.2 %copy-start.1 = (bf16[40,128,768]{2,1,0:T(8,128)(2,1)S(1)}, bf16[40,128,768]{2,1,0:T(8,128)(2,1)}, u32[]{:S(2)}) copy-start(bf16[40,128,768]{2,1,0:T(8,128)(2,1)} %refs_5_.3) | copy-start | bytes 23592964
  185.4 3.2 %copy-start.3 = (bf16[40,128,768]{2,1,0:T(8,128)(2,1)S(1)}, bf16[40,128,768]{2,1,0:T(8,128)(2,1)}, u32[]{:S(2)}) copy-start(bf16[40,128,768]{2,1,0:T(8,128)(2,1)} %refs_6_.3) | copy-start | bytes 23592964
  188.6 1.1 copy-start.9
  189.7 1.1 copy-start.11
  190.7 1.1 copy-start.13
  191.8 0.7 copy-start.26
  192.5 0.6 copy-start.28

commit v4 on v3

--- a/solution.py
+++ b/solution.py
@@ -17,9 +17,9 @@
 CHUNK_PAGES = 4
 MIB = 1024 * 1024
 
-ANY = pl.BlockSpec(memory_space=pl.ANY)
 SMEM = pl.BlockSpec(memory_space=pltpu.SMEM)
 VMEM = pl.BlockSpec(memory_space=pltpu.VMEM)
+HBM = pl.BlockSpec(memory_space=pltpu.HBM)
 
 
 def plan_kernel(req_count, place, group_of, arrivals, slots, sources, *refs):
@@ -143,14 +143,14 @@
             outs[offset][at, :] = value.astype(jnp.bfloat16)
         return carry
 
-    lax.fori_loop(0, rows // step, body, 0)
+    lax.fori_loop(0, rows // step, body, 0, unroll=2)
 
 
 def project_kernel(fresh_len, held_count, part, place, source, *refs):
-    groups = len(refs) - 8
+    groups = len(refs) - 10
     tokens = refs[:groups]
     own_rows, other_rows = refs[groups : groups + 2]
-    out, held, weights, picked, sems, weight_sems = refs[groups + 2 :]
+    out, held, weights, picked, ready, sems, weight_sems, out_sems = refs[groups + 2 :]
     core = place[0]
     depth = own_rows.shape[0]
     copies = [
@@ -186,29 +186,58 @@
             jnp.bfloat16
         )
         for index in range(together):
-            out[first + index] = result[index * rows : (index + 1) * rows]
+            ready[first + index] = result[index * rows : (index + 1) * rows]
+        targets = pl.ds(first, together)
+        copies.append(
+            pltpu.make_async_copy(
+                ready.at[targets], out.at[targets], out_sems.at[first // together]
+            )
+        )
+        copies[-1].start()
+    for copy in copies[groups + 2 :]:
+        copy.wait()
 
 
 def attend_kernel(shape, slots, all_lengths, table, *refs):
     groups, held_count, fresh_len, page, heads, part = shape
     parts, bias, cosine, sine_up, sine_down, key_pool, value_pool = refs[:7]
+    before = refs[7:-6]
     outs = refs[-6:-3]
-    ready, out_sems, new_sems = refs[-3:]
+    keys, values, sems = refs[-3:]
     chunk = CHUNK_PAGES * page
     pairs = heads // 2
 
     slot = [slots[part * held_count + index] for index in range(held_count)]
     lengths = [all_lengths[slot[index]] for index in range(held_count)]
     counts = [pl.cdiv(lengths[index], chunk) for index in range(held_count)]
-
-    def cached(pool, index, first, pair):
-        return jnp.concatenate(
-            [
-                pool[table[slot[index], first + entry], :, starts[pair] : starts[pair] + WINDOW]
-                for entry in range(CHUNK_PAGES)
-            ],
-            axis=0,
-        )
+    bases = [jnp.int32(0)]
+    for count in counts[:-1]:
+        bases.append(bases[-1] + count * CHUNK_PAGES)
+
+    def copies(index, entry):
+        number = table[slot[index], entry]
+        to = bases[index] + entry
+        return (
+            pltpu.make_async_copy(key_pool.at[number], keys.at[to], sems.at[index]),
+            pltpu.make_async_copy(value_pool.at[number], values.at[to], sems.at[index]),
+        )
+
+    for index in range(held_count):
+
+        def start(entry, carry, index=index):
+            for copy in copies(index, entry):
+                copy.start()
+            return carry
+
+        lax.fori_loop(0, counts[index] * CHUNK_PAGES, start, 0)
+
+    def cached(pages, index, part, pair):
+        held = pages[
+            pl.ds(bases[index] + part * CHUNK_PAGES, CHUNK_PAGES),
+            :,
+            starts[pair] : starts[pair] + WINDOW,
+        ]
+        return held.reshape(chunk, WINDOW)
 
     halves = [
         sum(parts[index].astype(jnp.float32) for index in range(side, groups, 2))
@@ -245,19 +274,17 @@
     queries = turn(kind(0)).astype(jnp.bfloat16)
     turned = turn(kind(1)).astype(jnp.bfloat16)
     plain = kind(2).astype(jnp.bfloat16)
+
+    def put(which, index, value):
+        outs[which][slot[index] if before else index] = value
+
+    for which, held in enumerate(before):
+        for index in range(held_count):
+            outs[which][slots[index]] = held[index]
     for index in range(held_count):
         rows = slice(index * fresh_len, (index + 1) * fresh_len)
-        ready[1, index] = turned[rows]
-        ready[2, index] = plain[rows]
-    new_copies = [
-        pltpu.make_async_copy(
-            ready.at[which, index], outs[which].at[slot[index]], new_sems.at[which - 1, index]
-        )
-        for which in (1, 2)
-        for index in range(held_count)
-    ]
-    for copy in new_copies:
-        copy.start()
+        put(1, index, turned[rows])
+        put(2, index, plain[rows])
 
     factor = 1.0 / math.sqrt(HEAD) / math.log(2.0)
     starts = [(2 * HEAD * pair) // LANES * LANES for pair in range(pairs)]
@@ -315,12 +342,18 @@
             axis=0,
         )
 
+        def finish(entry, carry, index=index):
+            for copy in copies(index, entry):
+                copy.wait()
+            return carry
+
+        lax.fori_loop(0, counts[index] * CHUNK_PAGES, finish, 0)
+
         def step(part, carry, index=index, spread=spread):
             peak, denom, mixed = carry
-            first = part * CHUNK_PAGES
             scores = jnp.concatenate(
                 [
-                    contract(spread[pair], cached(key_pool, index, first, pair))
+                    contract(spread[pair], cached(keys, index, part, pair))
                     for pair in range(pairs)
                 ],
                 axis=0,
@@ -336,7 +369,7 @@
                 [
                     jnp.dot(
                         weight[pair * 2 * fresh_len : (pair + 1) * 2 * fresh_len],
-                        cached(value_pool, index, first, pair),
+                        cached(values, index, part, pair),
                         preferred_element_type=jnp.float32,
                     )
                     for pair in range(pairs)
@@ -356,15 +389,7 @@
                     place_at = starts[pair] // LANES + side
                     tile = part[:, side * LANES : (side + 1) * LANES]
                     tiles[place_at] = tile if tiles[place_at] is None else tiles[place_at] + tile
-        ready[0, index] = jnp.concatenate(tiles, axis=1).astype(jnp.bfloat16)
-        new_copies.append(
-            pltpu.make_async_copy(
-                ready.at[0, index], outs[0].at[slot[index]], out_sems.at[index]
-            )
-        )
-        new_copies[-1].start()
-    for copy in new_copies:
-        copy.wait()
+        put(0, index, jnp.concatenate(tiles, axis=1).astype(jnp.bfloat16))
 
 
 def per_device(
@@ -400,8 +425,8 @@
             value, "req", [(device, device ^ distance) for device in range(req_size)]
         )
 
-    own_rows = lax.dynamic_slice_in_dim(w_qkv, core * half_cols, half_cols, 1)
-    other_rows = swap(lax.dynamic_slice_in_dim(w_qkv, (1 - core) * half_cols, half_cols, 1), 1)
+    def after(value, others):
+        return lax.optimization_barrier((value, others))[0]
 
     half = req_count // 2
     piece = jax.ShapeDtypeStruct((half, fresh_len, width), jnp.bfloat16)
@@ -413,8 +438,8 @@
             piece,
             piece,
         ],
-        in_specs=[SMEM, SMEM, ANY],
-        out_specs=[SMEM, SMEM, ANY, ANY],
+        in_specs=[SMEM, SMEM, HBM],
+        out_specs=[SMEM, SMEM, VMEM, VMEM],
         scratch_shapes=[
             pltpu.SMEM((everyone,), jnp.int32),
             pltpu.SMEM((everyone,), jnp.int32),
@@ -448,7 +473,8 @@
     place = jnp.stack([core]).astype(jnp.int32)
     where = jnp.stack([layer, chip]).astype(jnp.int32)
     chunk_rows = half * fresh_len
-    out = jax.ShapeDtypeStruct((req_count, fresh_len, heads * HEAD), jnp.bfloat16)
+    span = page_table.shape[1]
+    pages = span + (half - 1) * (span // 2)
 
     pieces = [[chunk.reshape(chunk_rows, width)] for chunk in chunks]
     ends = [(own[0], own[0]) for own in pieces]
@@ -457,22 +483,27 @@
         for hop in range(1, wgt_size):
             up, down = ends[part]
             if part == 1 and hop == 1:
-                up, _ = lax.optimization_barrier((up, pieces[0][min(2, wgt_size - 1)]))
-                down = up
+                up = down = after(up, (pieces[0][min(2, wgt_size - 1)], downs[0][min(1, wgt_size - 2)]))
             up = lax.ppermute(up, "wgt", [(at, at + 1) for at in range(hop - 1, wgt_size - 1)])
             down = lax.ppermute(down, "wgt", [(at + 1, at) for at in range(wgt_size - hop)])
             ends[part] = (up, down)
             pieces[part].append(up)
             downs[part].append(down)
 
+    rows_held = after(w_qkv, pieces[0][1])
+    own_rows = lax.dynamic_slice_in_dim(rows_held, core * half_cols, half_cols, 1)
+    other_rows = swap(
+        lax.dynamic_slice_in_dim(rows_held, (1 - core) * half_cols, half_cols, 1), 1
+    )
+
     projected = []
     for part in range(2):
         if part == 1:
-            pieces[1][-1], _ = lax.optimization_barrier((pieces[1][-1], projected[0]))
+            pieces[1][-1] = after(pieces[1][-1], projected[0])
         normed = pl.pallas_call(
             functools.partial(norm_kernel, wgt_size, chips),
             out_shape=[jax.ShapeDtypeStruct((chunk_rows, block), jnp.bfloat16)] * chips,
-            in_specs=[SMEM] + [ANY] * (2 * wgt_size - 1) + [VMEM] * 2,
+            in_specs=[SMEM] + [HBM] * (2 * wgt_size - 1) + [VMEM] * 2,
             out_specs=[VMEM] * chips,
             scratch_shapes=[
                 pltpu.VMEM((wgt_size, chunk_rows, width), jnp.bfloat16),
@@ -485,19 +516,26 @@
         tokens = []
         for distance in range(chips):
             mine = normed[distance] if distance == 0 else swap(normed[distance], 2 * distance)
+            if part == 0:
+                mine = after(mine, (pieces[1][1], downs[1][0]))
             tokens += [mine, swap(mine, 1)]
+        if part == 0:
+            hop = min(2, wgt_size - 1)
+            tokens[-1] = after(tokens[-1], (pieces[1][hop], downs[1][hop - 1]))
 
         partial = pl.pallas_call(
             functools.partial(project_kernel, fresh_len, half, part),
             out_shape=jax.ShapeDtypeStruct((req_size, chunk_rows, half_cols), jnp.bfloat16),
-            in_specs=[SMEM] * 2 + [ANY] * (req_size + 2),
-            out_specs=VMEM,
+            in_specs=[SMEM] * 2 + [HBM] * (req_size + 2),
+            out_specs=HBM,
             scratch_shapes=[
                 pltpu.VMEM((req_size * half, fresh_len, block), jnp.bfloat16),
                 pltpu.VMEM((block, half_cols), jnp.bfloat16),
                 pltpu.VMEM((min(req_size, 4) * chunk_rows, block), jnp.bfloat16),
+                pltpu.VMEM((req_size, chunk_rows, half_cols), jnp.bfloat16),
                 pltpu.SemaphoreType.DMA((req_size,)),
                 pltpu.SemaphoreType.DMA((2,)),
+                pltpu.SemaphoreType.DMA((req_size // min(req_size, 4),)),
             ],
             compiler_params=pltpu.CompilerParams(vmem_limit_bytes=20 * MIB),
             name="project",
@@ -514,25 +552,28 @@
     results = []
     for part in range(2):
         parts = lax.all_to_all(projected[part], "req", 0, 0, tiled=True)
+        if part == 0:
+            parts = after(parts, projected[1])
 
         operands = [
             slots, lengths, page_table, parts, bias, *tables, key_pool, value_pool
         ]
-        specs = [SMEM] * 3 + [VMEM] * 7
+        specs = [SMEM] * 3 + [VMEM] * 5 + [HBM] * 2
+        count = half if part == 0 else req_count
+        out = jax.ShapeDtypeStruct((count, fresh_len, heads * HEAD), jnp.bfloat16)
         results = pl.pallas_call(
             functools.partial(
                 attend_kernel, (req_size, half, fresh_len, page, heads, part)
             ),
             out_shape=[out] * 3,
-            in_specs=specs + [ANY] * len(results),
-            out_specs=[ANY] * 3,
+            in_specs=specs + [VMEM] * len(results),
+            out_specs=[VMEM] * 3,
             scratch_shapes=[
-                pltpu.VMEM((3, half, fresh_len, heads * HEAD), jnp.bfloat16),
+                pltpu.VMEM((pages, page, heads * HEAD), jnp.bfloat16),
+                pltpu.VMEM((pages, page, heads * HEAD), jnp.bfloat16),
                 pltpu.SemaphoreType.DMA((half,)),
-                pltpu.SemaphoreType.DMA((2, half)),
             ],
-            input_output_aliases={len(specs) + index: index for index in range(len(results))},
-            compiler_params=pltpu.CompilerParams(vmem_limit_bytes=30 * MIB),
+            compiler_params=pltpu.CompilerParams(vmem_limit_bytes=24 * MIB),
             name="attend",
         )(*operands, *results)
     return results

time: 201 us -> 190 us (0.945); the launches traced: 201 us -> 187 us
  waiting for transfers between devices: 77.6 us -> 52.9 us
  local copies, waits for them, and re-layouts: 33.2 us -> 40 us
  starting transfers between devices: 33.7 us -> 38.8 us
    pallas_call x1, Pallas kernels: 21.2 us -> 3.68 us  [per_device(): pl.pallas_call(functools.partial(plan_kernel, req_count), out_shape=[jax....]
    pallas_call x2, Pallas kernels: 13.4 us -> 28.7 us  [per_device(): pl.pallas_call(functools.partial(attend_kernel, (req_size, half, fresh_le...]
    ppermute x6, waiting for transfers between devices: 37.8 us -> 24.5 us  [per_device(): lax.ppermute(down, 'wgt', [(at + 1, at) for at in range(wgt_size - hop)])]
    ppermute x6, waiting for transfers between devices: 11.9 us -> 4.54 us  [per_device(): lax.ppermute(up, 'wgt', [(at, at + 1) for at in range(hop - 1, wgt_size -...]
    unnamed x62 -> x82, local copies, waits for them, and re-layouts: 29 us -> 35.8 us
    ppermute x6, starting transfers between devices: 10.2 us -> 15.2 us  [per_device(): lax.ppermute(up, 'wgt', [(at, at + 1) for at in range(hop - 1, wgt_size -...]
    all_to_all x2, waiting for transfers between devices: 4.12 us -> 0.01 us  [per_device(): parts = lax.all_to_all(projected[part], 'req', 0, 0, tiled=True)]
    pallas_call x2, Pallas kernels: 10.1 us -> 12.4 us  [per_device(): pl.pallas_call(functools.partial(project_kernel, fresh_len, half, part),...]
  transfers between devices with their start and end apart: 29 -> 29, of which waited for: 17 -> 14; matrix products, arithmetic and copies ran while one was open for 3% -> 5% of each run, Pallas kernels for 19% -> 12%
where the time goes in v4:
time: 190 us; the launch traced here: 187 us
  waiting for transfers between devices  52.9 us (28%)
  Pallas kernels  49.8 us (26%)
  local copies, waits for them, and re-layouts  40 us (21%)
  starting transfers between devices  38.8 us (20%)
  other arithmetic  4.44 us (2%)
    unnamed x82, local copies, waits for them, and re-layouts  35.8 us
    pallas_call x2, Pallas kernels, per_device(): pl.pallas_call(functools.partial(attend_kernel, (req_size, half, fresh_le...  28.7 us
    ppermute x6, waiting for transfers between devices, per_device(): lax.ppermute(down, 'wgt', [(at + 1, at) for at in range(wgt_size - hop)])  24.5 us
    ppermute x15, waiting for transfers between devices, swap(): lax.ppermute(value, 'req', [(device, device ^ distance) for device in ran...  23.9 us
    ppermute x6, starting transfers between devices, per_device(): lax.ppermute(up, 'wgt', [(at, at + 1) for at in range(hop - 1, wgt_size -...  15.2 us
    pallas_call x2, Pallas kernels, per_device(): pl.pallas_call(functools.partial(project_kernel, fresh_len, half, part),...  12.4 us
    ppermute x15, starting transfers between devices, swap(): lax.ppermute(value, 'req', [(device, device ^ distance) for device in ran...  8.57 us
    ppermute x6, starting transfers between devices, per_device(): lax.ppermute(down, 'wgt', [(at + 1, at) for at in range(wgt_size - hop)])  7.69 us
  transfers between devices with their start and end apart: 29, of which 14 were waited for; matrix products, arithmetic and copies ran while one was open for 5% of the time, Pallas kernels for 12%

profile of v4, /device:TPU:0, one launch (start us, length us, event | category | flops | bytes accessed | tf_op | source)
XLA Modules:
  0.0 187.2 jit_solution(5093301650407972165)
XLA Ops:
  0.6 3.7 %plan.1 = (s32[4]{0:T(128)}, s32[32]{0:T(128)}, bf16[2,48,1536]{2,1,0:T(8,128)(2,1)}, bf16[2,48,1536]{2,1,0:T(8,128)(2,1)}) custom-call(s32[1]{0:T(128)} %bitcast.place, s32[32]{0:T(128)} %group_of.1, bf16[4,48,1536]{2,1,0:T(8,128)(2,1)} %arrivals.1), custom_call_target="tpu_custom_call" | custom-call | tf_op jit(solution)/shard_map/plan/pallas_call | solution.py:433
  4.3 5.7 %collective-permute-start = (bf16[96,1536]{1,0:T(8,128)(2,1)}, bf16[96,1536]{1,0:T(8,128)(2,1)}, u32[]{:S(2)}, u32[]{:S(2)}) collective-permute-start(bf16[96,1536]{1,0:T(8,128)(2,1)} %bitcast.27), channel_id=1, source_target_pairs={{0,1},{1,2},{2,3},{4,5},{5,6},{6,7},{8,9},{9,10},{10,11},{12,13},{... | collective-permute-start | bytes 884744 | tf_op jit(solution)/shard_map/ppermute | solution.py:487
  10.0 1.3 collective-permute-start.2
  11.3 4.5 %collective-permute-done.refs_1_ = bf16[96,1536]{1,0:T(8,128)(2,1)} collective-permute-done((bf16[96,1536]{1,0:T(8,128)(2,1)}, bf16[96,1536]{1,0:T(8,128)(2,1)}, u32[]{:S(2)}, u32[]{:S(2)}) %collective-permute-start) | collective-permute-done | bytes 294944 | tf_op jit(solution)/shard_map/ppermute | solution.py:487
  15.8 3.5 %constant_dynamic-slice_fusion = (bf16[768,1152]{1,0:T(8,128)(2,1)}, bf16[768,1152]{1,0:T(8,128)(2,1)S(1)}) fusion(bf16[768,2304]{1,0:T(8,128)(2,1)} %param.20, s32[]{:T(128)S(6)} %select_n.20, s32[]{:T(128)S(6)} %select_n.19), kind=kLoop, calls=%fused_computation.8 | loop fusion | bytes 7077896 | tf_op jit(solution)/shard_map/dynamic_slice | solution.py:496
  19.3 1.4 collective-permute-start.1
  20.7 1.3 collective-permute-start.3
  22.0 1.4 collective-permute-start.7
  23.4 12.2 %collective-permute-done.3.refs_5_ = bf16[96,1536]{1,0:T(8,128)(2,1)} collective-permute-done((bf16[96,1536]{1,0:T(8,128)(2,1)}, bf16[96,1536]{1,0:T(8,128)(2,1)}, u32[]{:S(2)}, u32[]{:S(2)}) %collective-permute-start.3) | collective-permute-done | bytes 294944 | tf_op jit(solution)/shard_map/ppermute | solution.py:488
  35.6 1.3 collective-permute-start.8
  37.0 5.3 %collective-permute-start.4 = (bf16[96,1536]{1,0:T(8,128)(2,1)}, bf16[96,1536]{1,0:T(8,128)(2,1)S(1)}, u32[]{:S(2)}, u32[]{:S(2)}) collective-permute-start(bf16[96,1536]{1,0:T(8,128)(2,1)} %bitcast.24), channel_id=1, source_target_pairs={{0,1},{1,2},{2,3},{4,5},{5,6},{6,7},{8,9},{9,10},{10,11},{12,13},{... | collective-permute-start | bytes 884744 | tf_op jit(solution)/shard_map/ppermute | solution.py:487
  42.3 0.7 reshape.166
  43.0 1.3 collective-permute-start.9
  44.3 2.2 %collective-permute-done.8.refs_6_ = bf16[96,1536]{1,0:T(8,128)(2,1)} collective-permute-done((bf16[96,1536]{1,0:T(8,128)(2,1)}, bf16[96,1536]{1,0:T(8,128)(2,1)}, u32[]{:S(2)}, u32[]{:S(2)}) %collective-permute-start.8) | collective-permute-done | bytes 294944 | tf_op jit(solution)/shard_map/ppermute | solution.py:488
  46.5 1.0 copy-done.19
  47.4 3.0 %norm.2 = (bf16[96,1536]{1,0:T(8,128)(2,1)S(1)}, bf16[96,1536]{1,0:T(8,128)(2,1)S(1)}, bf16[96,1536]{1,0:T(8,128)(2,1)S(1)}, bf16[96,1536]{1,0:T(8,128)(2,1)S(1)}) custom-call(s32[2]{0:T(128)S(1)} %pad_add_fusion.place, bf16[96,1536]{1,0:T(8,128)(2,1)S(1)} %bitcast.29, bf16[96,1536]{1,0:T(8,128)(2,1)} %collective-permute-done.refs_1_, ...), custom_call_target="tpu_custom_call" | custom-call | tf_op jit(solution)/shard_map/norm/pallas_call | solution.py:503
  50.4 2.5 %collective-permute-start.15 = (bf16[96,1536]{1,0:T(8,128)(2,1)S(1)}, bf16[96,1536]{1,0:T(8,128)(2,1)S(1)}, u32[]{:S(2)}, u32[]{:S(2)}) collective-permute-start(bf16[96,1536]{1,0:T(8,128)(2,1)S(1)} %get-tuple-element.38), channel_id=1, source_target_pairs={{0,24},{4,28},{8,16},{12,20},{16,8},{20,12},{24,0},{28,4},{1,25},{... | collective-permute-start | bytes 884744 | tf_op jit(solution)/shard_map/ppermute | solution.py:424
  54.0 1.3 collective-permute-start.17
  55.3 0.7 copy-done.17
  56.0 5.4 %collective-permute-done.15 = bf16[96,1536]{1,0:T(8,128)(2,1)S(1)} collective-permute-done((bf16[96,1536]{1,0:T(8,128)(2,1)S(1)}, bf16[96,1536]{1,0:T(8,128)(2,1)S(1)}, u32[]{:S(2)}, u32[]{:S(2)}) %collective-permute-start.15) | collective-permute-done | bytes 294944 | tf_op jit(solution)/shard_map/ppermute | solution.py:424
  61.4 0.7 collective-permute-start.5
  62.1 0.7 copy-done.15
  62.8 2.7 %collective-permute-done.13 = bf16[96,1536]{1,0:T(8,128)(2,1)S(1)} collective-permute-done((bf16[96,1536]{1,0:T(8,128)(2,1)S(1)}, bf16[96,1536]{1,0:T(8,128)(2,1)S(1)}, u32[]{:S(2)}, u32[]{:S(2)}) %collective-permute-start.13) | collective-permute-done | bytes 294944 | tf_op jit(solution)/shard_map/ppermute | solution.py:424
  66.5 1.0 collective-permute-done.16
  68.4 6.2 %project.2 = bf16[8,96,1152]{2,1,0:T(8,128)(2,1)S(1)} custom-call(s32[1]{0:T(128)} %bitcast.1.place, s32[32]{0:T(128)S(1)} %copy-done.39, bf16[2,48,1536]{2,1,0:T(8,128)(2,1)S(1)} %bitcast.30, bf16[2,48,1536]{2,1,0:T(8,128)(2,1)S(1)} %bitcast.39, bf16[2,48,1536]{2,1,0:T(8,128)(2,1)S(1)} %bitcast.34, bf16[2,48,1536]{2,1,0:T(8,128)(2,1)S(1)} %bitcast.44, ...), custom_call_target="tpu_custom_call" | custom-call | tf_op jit(solution)/shard_map/project/pallas_call | solution.py:526
  74.6 1.2 copy-done.4
  75.8 3.6 %all-to-all-start.1 = ((bf16[8,96,1152]{2,1,0:T(8,128)(2,1)}), bf16[8,96,1152]{2,1,0:T(8,128)(2,1)S(1)}, u32[]{:S(2)}, u32[]{:S(2)}) async-start(bf16[8,96,1152]{2,1,0:T(8,128)(2,1)} %copy-done.4), calls=%async_computation.1 | async-start | bytes 3538944 | tf_op jit(solution)/shard_map/all_to_all | solution.py:554
  79.4 0.8 collective-permute-start.6
  80.2 1.3 collective-permute-start.19
  81.6 10.1 %collective-permute-done.19.refs_6_ = bf16[96,1536]{1,0:T(8,128)(2,1)S(1)} collective-permute-done((bf16[96,1536]{1,0:T(8,128)(2,1)}, bf16[96,1536]{1,0:T(8,128)(2,1)S(1)}, u32[]{:S(2)}, u32[]{:S(2)}) %collective-permute-start.19) | collective-permute-done | bytes 294944 | tf_op jit(solution)/shard_map/ppermute | solution.py:488
  91.6 1.0 copy-done.14
  92.6 1.0 copy-done.16
  93.6 1.0 copy-done.18
  94.5 1.0 copy-done.21
  95.5 1.0 copy-done.23
  96.5 0.7 copy-done.25
  97.2 0.7 copy-done.27
  97.9 2.1 %norm.3 = (bf16[96,1536]{1,0:T(8,128)(2,1)S(1)}, bf16[96,1536]{1,0:T(8,128)(2,1)S(1)}, bf16[96,1536]{1,0:T(8,128)(2,1)S(1)}, bf16[96,1536]{1,0:T(8,128)(2,1)S(1)}) custom-call(s32[2]{0:T(128)S(1)} %pad_add_fusion.place, bf16[96,1536]{1,0:T(8,128)(2,1)S(1)} %bitcast.26, bf16[96,1536]{1,0:T(8,128)(2,1)S(1)} %copy-done.16, bf16[96,1536]{1,0:T(8,128)(2,1)S(1)} %copy-done.23, ...), custom_call_target="tpu_custom_call" | custom-call | tf_op jit(solution)/shard_map/norm/pallas_call | solution.py:503
  100.0 1.7 collective-permute-start.21
  101.7 1.5 collective-permute-start.23
  103.6 6.4 %collective-permute-done.21 = bf16[96,1536]{1,0:T(8,128)(2,1)S(1)} collective-permute-done((bf16[96,1536]{1,0:T(8,128)(2,1)S(1)}, bf16[96,1536]{1,0:T(8,128)(2,1)S(1)}, u32[]{:S(2)}, u32[]{:S(2)}) %collective-permute-start.21) | collective-permute-done | bytes 294944 | tf_op jit(solution)/shard_map/ppermute | solution.py:424
  110.0 6.0 %collective-permute-done.23 = bf16[96,1536]{1,0:T(8,128)(2,1)S(1)} collective-permute-done((bf16[96,1536]{1,0:T(8,128)(2,1)S(1)}, bf16[96,1536]{1,0:T(8,128)(2,1)S(1)}, u32[]{:S(2)}, u32[]{:S(2)}) %collective-permute-start.23) | collective-permute-done | bytes 294944 | tf_op jit(solution)/shard_map/ppermute | solution.py:424
  116.5 1.1 collective-permute-done.24
  118.0 6.2 %project.3 = bf16[8,96,1152]{2,1,0:T(8,128)(2,1)S(1)} custom-call(s32[1]{0:T(128)} %bitcast.1.place, s32[32]{0:T(128)S(1)} %copy-done.39, bf16[2,48,1536]{2,1,0:T(8,128)(2,1)S(1)} %bitcast.33, bf16[2,48,1536]{2,1,0:T(8,128)(2,1)S(1)} %bitcast.38, bf16[2,48,1536]{2,1,0:T(8,128)(2,1)S(1)} %bitcast.35, bf16[2,48,1536]{2,1,0:T(8,128)(2,1)S(1)} %bitcast.40, ...), custom_call_target="tpu_custom_call" | custom-call | tf_op jit(solution)/shard_map/project/pallas_call | solution.py:526
  124.2 1.2 copy-done.5
  125.5 3.8 %all-to-all-start = ((bf16[8,96,1152]{2,1,0:T(8,128)(2,1)}), bf16[8,96,1152]{2,1,0:T(8,128)(2,1)S(1)}, u32[]{:S(2)}, u32[]{:S(2)}) async-start(bf16[8,96,1152]{2,1,0:T(8,128)(2,1)} %copy-done.5), calls=%async_computation | async-start | bytes 3538944 | tf_op jit(solution)/shard_map/all_to_all | solution.py:554
  129.3 0.7 reshape.169.refs_1_
  130.0 0.7 add_convert_fusion
  130.7 2.9 %fusion = (f32[4,48,768]{2,1,0:T(8,128)S(1)}, f32[4,48,768]{2,1,0:T(8,128)S(1)}, f32[4,48,768]{2,1,0:T(8,128)S(1)}) fusion(f32[768]{0:T(1024)} %constant.45, f32[4,48]{1,0:T(4,128)S(1)} %add_convert_fusion, pred[768]{0:T(1024)(128)(4,1)} %constant.46, pred[768]{0:T(1024)(128)(4,1)} %constant.38.clone, pred[768]{0:T(1024)(128)(4,1)} %constant.37.clone), kind=kLoop, calls=%fused_computation.2 | loop fusion | flops 737280 | bytes 1775616 | tf_op jit(solution)/shard_map/jit(_where)/select_n | solution.py:464
  133.7 3.2 %copy-done = bf16[40,128,768]{2,1,0:T(8,128)(2,1)S(1)} copy-done((bf16[40,128,768]{2,1,0:T(8,128)(2,1)S(1)}, bf16[40,128,768]{2,1,0:T(8,128)(2,1)}, u32[]{:S(2)}) %copy-start) | copy-done | bytes 7864344
  136.9 3.2 %copy-done.2 = bf16[40,128,768]{2,1,0:T(8,128)(2,1)S(1)} copy-done((bf16[40,128,768]{2,1,0:T(8,128)(2,1)S(1)}, bf16[40,128,768]{2,1,0:T(8,128)(2,1)}, u32[]{:S(2)}) %copy-start.2) | copy-done | bytes 7864344
  140.1 11.0 %attend.2 = (bf16[2,48,768]{2,1,0:T(8,128)(2,1)S(1)}, bf16[2,48,768]{2,1,0:T(8,128)(2,1)S(1)}, bf16[2,48,768]{2,1,0:T(8,128)(2,1)S(1)}) custom-call(s32[4]{0:T(128)S(1)} %copy-done.37, s32[4]{0:T(128)S(1)} %copy-done.35, s32[4,16]{1,0:T(4,128)S(1)} %copy-done.34, bf16[8,96,1152]{2,1,0:T(8,128)(2,1)S(1)} %all-to-all-done.1.refs_0_, ...), custom_call_target="tpu_custom_call" | custom-call | tf_op jit(solution)/shard_map/attend/pallas_call | solution.py:564
  151.2 0.8 copy-done.8
  152.0 0.8 copy-done.10
  152.8 0.8 copy-done.12
  155.7 3.2 %copy-done.1 = bf16[40,128,768]{2,1,0:T(8,128)(2,1)S(1)} copy-done((bf16[40,128,768]{2,1,0:T(8,128)(2,1)S(1)}, bf16[40,128,768]{2,1,0:T(8,128)(2,1)}, u32[]{:S(2)}) %copy-start.1) | copy-done | bytes 7864344
  158.9 3.2 %copy-done.3 = bf16[40,128,768]{2,1,0:T(8,128)(2,1)S(1)} copy-done((bf16[40,128,768]{2,1,0:T(8,128)(2,1)S(1)}, bf16[40,128,768]{2,1,0:T(8,128)(2,1)}, u32[]{:S(2)}) %copy-start.3) | copy-done | bytes 7864344
  162.1 1.1 copy-done.9
  163.2 1.1 copy-done.11
  164.3 1.1 copy-done.13
  165.3 0.9 copy-done.29
  166.2 0.9 copy-done.31
  167.1 0.9 copy-done.33
  169.3 17.7 %attend.3 = (bf16[4,48,768]{2,1,0:T(8,128)(2,1)}, bf16[4,48,768]{2,1,0:T(8,128)(2,1)}, bf16[4,48,768]{2,1,0:T(8,128)(2,1)}) custom-call(s32[4]{0:T(128)S(1)} %copy-done.38, s32[4]{0:T(128)S(1)} %copy-done.36, s32[4,16]{1,0:T(4,128)S(1)} %copy-done.34, bf16[8,96,1152]{2,1,0:T(8,128)(2,1)S(1)} %all-to-all-done.refs_0_, f32[1,2304]{1,0:T(1,128)S(1)} %reshape.169.refs_1_, ...), custom_call_target="tpu_custom_call" | custom-call | tf_op jit(solution)/shard_map/attend/pallas_call | solution.py:564
  (90 shorter events, 7.7 us)
Async XLA Ops:
  4.3 11.5 %collective-permute-start = (bf16[96,1536]{1,0:T(8,128)(2,1)}, bf16[96,1536]{1,0:T(8,128)(2,1)}, u32[]{:S(2)}, u32[]{:S(2)}) collective-permute-start(bf16[96,1536]{1,0:T(8,128)(2,1)} %bitcast.27), channel_id=1, source_target_pairs={{0,1},{1,2},{2,3},{4,5},{5,6},{6,7},{8,9},{9,10},{10,11},{12,13},{... | collective-permute-start | bytes 884744 | tf_op jit(solution)/shard_map/ppermute | solution.py:487
  10.0 10.7 %collective-permute-start.2 = (bf16[96,1536]{1,0:T(8,128)(2,1)}, bf16[96,1536]{1,0:T(8,128)(2,1)}, u32[]{:S(2)}, u32[]{:S(2)}) collective-permute-start(bf16[96,1536]{1,0:T(8,128)(2,1)} %bitcast.28), channel_id=1, source_target_pairs={{1,0},{2,1},{3,2},{5,4},{6,5},{7,6},{9,8},{10,9},{11,10},{13,12},{... | collective-permute-start | bytes 884744 | tf_op jit(solution)/shard_map/ppermute | solution.py:488
  11.3 25.6 %copy-start.40 = (bf16[6144]{0:T(1024)(128)(2,1)S(1)}, bf16[6144]{0:T(1024)(128)(2,1)}, u32[]{:S(2)}) copy-start(bf16[6144]{0:T(1024)(128)(2,1)} %param.18) | copy-start | bytes 36868
  19.3 49.0 %copy-start.39 = (s32[32]{0:T(128)S(1)}, s32[32]{0:T(128)}, u32[]{:S(2)}) copy-start(s32[32]{0:T(128)} %get-tuple-element.28.source) | copy-start | bytes 388
  19.3 49.0 %collective-permute-start.18 = (bf16[768,1152]{1,0:T(8,128)(2,1)}, bf16[768,1152]{1,0:T(8,128)(2,1)S(1)}, u32[]{:S(2)}, u32[]{:S(2)}) collective-permute-start(bf16[768,1152]{1,0:T(8,128)(2,1)} %get-tuple-element.51), channel_id=1, source_target_pairs={{0,4},{4,0},{8,12},{12,8},{16,20},{20,16},{24,28},{28,24},{1,5},{5... | collective-permute-start | bytes 5308424 | tf_op jit(solution)/shard_map/ppermute | solution.py:424
  19.3 2.7 %collective-permute-start.1 = (bf16[96,1536]{1,0:T(8,128)(2,1)}, bf16[96,1536]{1,0:T(8,128)(2,1)}, u32[]{:S(2)}, u32[]{:S(2)}) collective-permute-start(bf16[96,1536]{1,0:T(8,128)(2,1)} %collective-permute-done.refs_1_), channel_id=1, source_target_pairs={{1,2},{2,3},{5,6},{6,7},{9,10},{10,11},{13,14},{14,15},{17,18},{18... | collective-permute-start | bytes 884744 | tf_op jit(solution)/shard_map/ppermute | solution.py:487
  20.7 14.9 %collective-permute-start.3 = (bf16[96,1536]{1,0:T(8,128)(2,1)}, bf16[96,1536]{1,0:T(8,128)(2,1)}, u32[]{:S(2)}, u32[]{:S(2)}) collective-permute-start(bf16[96,1536]{1,0:T(8,128)(2,1)} %collective-permute-done.2.refs_4_), channel_id=1, source_target_pairs={{1,0},{2,1},{5,4},{6,5},{9,8},{10,9},{13,12},{14,13},{17,16},{18,1... | collective-permute-start | bytes 884744 | tf_op jit(solution)/shard_map/ppermute | solution.py:488
  22.0 22.3 %collective-permute-start.7 = (bf16[96,1536]{1,0:T(8,128)(2,1)}, bf16[96,1536]{1,0:T(8,128)(2,1)}, u32[]{:S(2)}, u32[]{:S(2)}) collective-permute-start(bf16[96,1536]{1,0:T(8,128)(2,1)} %collective-permute-done.1.refs_2_), channel_id=1, source_target_pairs={{2,3},{6,7},{10,11},{14,15},{18,19},{22,23},{26,27},{30,31}} | collective-permute-start | bytes 884744 | tf_op jit(solution)/shard_map/ppermute | solution.py:487
  35.6 10.8 %collective-permute-start.8 = (bf16[96,1536]{1,0:T(8,128)(2,1)}, bf16[96,1536]{1,0:T(8,128)(2,1)}, u32[]{:S(2)}, u32[]{:S(2)}) collective-permute-start(bf16[96,1536]{1,0:T(8,128)(2,1)} %collective-permute-done.3.refs_5_), channel_id=1, source_target_pairs={{1,0},{5,4},{9,8},{13,12},{17,16},{21,20},{25,24},{29,28}} | collective-permute-start | bytes 884744 | tf_op jit(solution)/shard_map/ppermute | solution.py:488
  36.9 31.4 %copy-start.24 = (f32[6144]{0:T(1024)}, f32[6144]{0:T(1024)S(1)}, u32[]{:S(2)}) copy-start(f32[6144]{0:T(1024)S(1)} %reshape.164) | copy-start | bytes 73732
  37.0 16.4 %collective-permute-start.4 = (bf16[96,1536]{1,0:T(8,128)(2,1)}, bf16[96,1536]{1,0:T(8,128)(2,1)S(1)}, u32[]{:S(2)}, u32[]{:S(2)}) collective-permute-start(bf16[96,1536]{1,0:T(8,128)(2,1)} %bitcast.24), channel_id=1, source_target_pairs={{0,1},{1,2},{2,3},{4,5},{5,6},{6,7},{8,9},{9,10},{10,11},{12,13},{... | collective-permute-start | bytes 884744 | tf_op jit(solution)/shard_map/ppermute | solution.py:487
  43.0 25.3 %copy-start.26 = (f32[6144]{0:T(1024)}, f32[6144]{0:T(1024)S(1)}, u32[]{:S(2)}) copy-start(f32[6144]{0:T(1024)S(1)} %reshape.166) | copy-start | bytes 73732
  43.0 11.0 %collective-permute-start.9 = (bf16[96,1536]{1,0:T(8,128)(2,1)}, bf16[96,1536]{1,0:T(8,128)(2,1)S(1)}, u32[]{:S(2)}, u32[]{:S(2)}) collective-permute-start(bf16[96,1536]{1,0:T(8,128)(2,1)} %bitcast.25), channel_id=1, source_target_pairs={{1,0},{2,1},{3,2},{5,4},{6,5},{7,6},{9,8},{10,9},{11,10},{13,12},{... | collective-permute-start | bytes 884744 | tf_op jit(solution)/shard_map/ppermute | solution.py:488
  46.5 1.0 copy-start.19
  50.4 11.0 %collective-permute-start.15 = (bf16[96,1536]{1,0:T(8,128)(2,1)S(1)}, bf16[96,1536]{1,0:T(8,128)(2,1)S(1)}, u32[]{:S(2)}, u32[]{:S(2)}) collective-permute-start(bf16[96,1536]{1,0:T(8,128)(2,1)S(1)} %get-tuple-element.38), channel_id=1, source_target_pairs={{0,24},{4,28},{8,16},{12,20},{16,8},{20,12},{24,0},{28,4},{1,25},{... | collective-permute-start | bytes 884744 | tf_op jit(solution)/shard_map/ppermute | solution.py:424
  52.9 12.5 %collective-permute-start.13 = (bf16[96,1536]{1,0:T(8,128)(2,1)S(1)}, bf16[96,1536]{1,0:T(8,128)(2,1)S(1)}, u32[]{:S(2)}, u32[]{:S(2)}) collective-permute-start(bf16[96,1536]{1,0:T(8,128)(2,1)S(1)} %get-tuple-element.36), channel_id=1, source_target_pairs={{0,16},{4,20},{8,24},{12,28},{16,0},{20,4},{24,8},{28,12},{1,17},{... | collective-permute-start | bytes 884744 | tf_op jit(solution)/shard_map/ppermute | solution.py:424
  53.4 12.1 %collective-permute-start.11 = (bf16[96,1536]{1,0:T(8,128)(2,1)S(1)}, bf16[96,1536]{1,0:T(8,128)(2,1)S(1)}, u32[]{:S(2)}, u32[]{:S(2)}) collective-permute-start(bf16[96,1536]{1,0:T(8,128)(2,1)S(1)} %get-tuple-element.34), channel_id=1, source_target_pairs={{0,8},{4,12},{8,0},{12,4},{16,24},{20,28},{24,16},{28,20},{1,9},{5... | collective-permute-start | bytes 884744 | tf_op jit(solution)/shard_map/ppermute | solution.py:424
  54.0 12.0 %collective-permute-start.17 = (bf16[96,1536]{1,0:T(8,128)(2,1)S(1)}, bf16[96,1536]{1,0:T(8,128)(2,1)S(1)}, u32[]{:S(2)}, u32[]{:S(2)}) collective-permute-start(bf16[96,1536]{1,0:T(8,128)(2,1)S(1)} %collective-permute-done.9.refs_4_), channel_id=1, source_target_pairs={{1,0},{2,1},{5,4},{6,5},{9,8},{10,9},{13,12},{14,13},{17,16},{18,1... | collective-permute-start | bytes 884744 | tf_op jit(solution)/shard_map/ppermute | solution.py:488
  55.3 0.7 copy-start.17
  61.4 4.7 %collective-permute-start.5 = (bf16[96,1536]{1,0:T(8,128)(2,1)S(1)}, bf16[96,1536]{1,0:T(8,128)(2,1)S(1)}, u32[]{:S(2)}, u32[]{:S(2)}) collective-permute-start(bf16[96,1536]{1,0:T(8,128)(2,1)S(1)} %collective-permute-done.4.refs_1_), channel_id=1, source_target_pairs={{1,2},{2,3},{5,6},{6,7},{9,10},{10,11},{13,14},{14,15},{17,18},{18... | collective-permute-start | bytes 884744 | tf_op jit(solution)/shard_map/ppermute | solution.py:487
  65.5 2.0 %collective-permute-start.10 = (bf16[96,1536]{1,0:T(8,128)(2,1)S(1)}, bf16[96,1536]{1,0:T(8,128)(2,1)S(1)}, u32[]{:S(2)}, u32[]{:S(2)}) collective-permute-start(bf16[96,1536]{1,0:T(8,128)(2,1)S(1)} %get-tuple-element.33), channel_id=1, source_target_pairs={{0,4},{4,0},{8,12},{12,8},{16,20},{20,16},{24,28},{28,24},{1,5},{5... | collective-permute-start | bytes 884744 | tf_op jit(solution)/shard_map/ppermute | solution.py:424
  65.6 1.9 %collective-permute-start.16 = (bf16[96,1536]{1,0:T(8,128)(2,1)S(1)}, bf16[96,1536]{1,0:T(8,128)(2,1)S(1)}, u32[]{:S(2)}, u32[]{:S(2)}) collective-permute-start(bf16[96,1536]{1,0:T(8,128)(2,1)S(1)} %collective-permute-done.15), channel_id=1, source_target_pairs={{0,4},{4,0},{8,12},{12,8},{16,20},{20,16},{24,28},{28,24},{1,5},{5... | collective-permute-start | bytes 884744 | tf_op jit(solution)/shard_map/ppermute | solution.py:424
  66.0 2.4 %copy-start.20 = (bf16[96,1536]{1,0:T(8,128)(2,1)}, bf16[96,1536]{1,0:T(8,128)(2,1)S(1)}, u32[]{:S(2)}) copy-start(bf16[96,1536]{1,0:T(8,128)(2,1)S(1)} %collective-permute-done.17.refs_5_) | copy-start | bytes 884740
  66.0 1.9 %collective-permute-start.14 = (bf16[96,1536]{1,0:T(8,128)(2,1)S(1)}, bf16[96,1536]{1,0:T(8,128)(2,1)S(1)}, u32[]{:S(2)}, u32[]{:S(2)}) collective-permute-start(bf16[96,1536]{1,0:T(8,128)(2,1)S(1)} %collective-permute-done.13), channel_id=1, source_target_pairs={{0,4},{4,0},{8,12},{12,8},{16,20},{20,16},{24,28},{28,24},{1,5},{5... | collective-permute-start | bytes 884744 | tf_op jit(solution)/shard_map/ppermute | solution.py:424
  66.1 2.3 %copy-start.22 = (bf16[96,1536]{1,0:T(8,128)(2,1)}, bf16[96,1536]{1,0:T(8,128)(2,1)S(1)}, u32[]{:S(2)}) copy-start(bf16[96,1536]{1,0:T(8,128)(2,1)S(1)} %collective-permute-done.5.refs_2_) | copy-start | bytes 884740
  66.1 2.2 %collective-permute-start.12 = (bf16[96,1536]{1,0:T(8,128)(2,1)S(1)}, bf16[96,1536]{1,0:T(8,128)(2,1)S(1)}, u32[]{:S(2)}, u32[]{:S(2)}) collective-permute-start(bf16[96,1536]{1,0:T(8,128)(2,1)S(1)} %collective-permute-done.11), channel_id=1, source_target_pairs={{0,4},{4,0},{8,12},{12,8},{16,20},{20,16},{24,28},{28,24},{1,5},{5... | collective-permute-start | bytes 884744 | tf_op jit(solution)/shard_map/ppermute | solution.py:424
  68.3 6.3 %copy-start.6 = (bf16[768,1152]{1,0:T(8,128)(2,1)}, bf16[768,1152]{1,0:T(8,128)(2,1)S(1)}, u32[]{:S(2)}) copy-start(bf16[768,1152]{1,0:T(8,128)(2,1)S(1)} %collective-permute-done.18.refs_9_) | copy-start | bytes 5308420
  74.6 1.2 copy-start.4
  75.8 49.7 %all-to-all-start.1 = ((bf16[8,96,1152]{2,1,0:T(8,128)(2,1)}), bf16[8,96,1152]{2,1,0:T(8,128)(2,1)S(1)}, u32[]{:S(2)}, u32[]{:S(2)}) async-start(bf16[8,96,1152]{2,1,0:T(8,128)(2,1)} %copy-done.4), calls=%async_computation.1 | async-start | bytes 3538944 | tf_op jit(solution)/shard_map/all_to_all | solution.py:554
  79.4 38.6 %copy-start.7 = (bf16[768,1152]{1,0:T(8,128)(2,1)S(1)}, bf16[768,1152]{1,0:T(8,128)(2,1)}, u32[]{:S(2)}) copy-start(bf16[768,1152]{1,0:T(8,128)(2,1)} %copy-done.6) | copy-start | bytes 5308420
  79.4 2.1 %collective-permute-start.6 = (bf16[96,1536]{1,0:T(8,128)(2,1)}, bf16[96,1536]{1,0:T(8,128)(2,1)S(1)}, u32[]{:S(2)}, u32[]{:S(2)}) collective-permute-start(bf16[96,1536]{1,0:T(8,128)(2,1)} %copy-done.22), channel_id=1, source_target_pairs={{2,3},{6,7},{10,11},{14,15},{18,19},{22,23},{26,27},{30,31}} | collective-permute-start | bytes 884744 | tf_op jit(solution)/shard_map/ppermute | solution.py:487
  80.2 11.4 %collective-permute-start.19 = (bf16[96,1536]{1,0:T(8,128)(2,1)}, bf16[96,1536]{1,0:T(8,128)(2,1)S(1)}, u32[]{:S(2)}, u32[]{:S(2)}) collective-permute-start(bf16[96,1536]{1,0:T(8,128)(2,1)} %copy-done.20), channel_id=1, source_target_pairs={{1,0},{5,4},{9,8},{13,12},{17,16},{21,20},{25,24},{29,28}} | collective-permute-start | bytes 884744 | tf_op jit(solution)/shard_map/ppermute | solution.py:488
  91.6 1.0 copy-start.14
  92.6 1.0 copy-start.16
  93.6 1.0 copy-start.18
  94.5 1.0 copy-start.21
  95.5 1.0 copy-start.23
  96.5 0.7 copy-start.25
  97.2 0.7 copy-start.27
  100.0 10.0 %collective-permute-start.21 = (bf16[96,1536]{1,0:T(8,128)(2,1)S(1)}, bf16[96,1536]{1,0:T(8,128)(2,1)S(1)}, u32[]{:S(2)}, u32[]{:S(2)}) collective-permute-start(bf16[96,1536]{1,0:T(8,128)(2,1)S(1)} %get-tuple-element.44), channel_id=1, source_target_pairs={{0,8},{4,12},{8,0},{12,4},{16,24},{20,28},{24,16},{28,20},{1,9},{5... | collective-permute-start | bytes 884744 | tf_op jit(solution)/shard_map/ppermute | solution.py:424
  101.7 14.3 %collective-permute-start.23 = (bf16[96,1536]{1,0:T(8,128)(2,1)S(1)}, bf16[96,1536]{1,0:T(8,128)(2,1)S(1)}, u32[]{:S(2)}, u32[]{:S(2)}) collective-permute-start(bf16[96,1536]{1,0:T(8,128)(2,1)S(1)} %get-tuple-element.45), channel_id=1, source_target_pairs={{0,16},{4,20},{8,24},{12,28},{16,0},{20,4},{24,8},{28,12},{1,17},{... | collective-permute-start | bytes 884744 | tf_op jit(solution)/shard_map/ppermute | solution.py:424
  103.2 12.8 %collective-permute-start.25 = (bf16[96,1536]{1,0:T(8,128)(2,1)S(1)}, bf16[96,1536]{1,0:T(8,128)(2,1)S(1)}, u32[]{:S(2)}, u32[]{:S(2)}) collective-permute-start(bf16[96,1536]{1,0:T(8,128)(2,1)S(1)} %get-tuple-element.46), channel_id=1, source_target_pairs={{0,24},{4,28},{8,16},{12,20},{16,8},{20,12},{24,0},{28,4},{1,25},{... | collective-permute-start | bytes 884744 | tf_op jit(solution)/shard_map/ppermute | solution.py:424
  103.6 13.0 %collective-permute-start.20 = (bf16[96,1536]{1,0:T(8,128)(2,1)S(1)}, bf16[96,1536]{1,0:T(8,128)(2,1)S(1)}, u32[]{:S(2)}, u32[]{:S(2)}) collective-permute-start(bf16[96,1536]{1,0:T(8,128)(2,1)S(1)} %get-tuple-element.43), channel_id=1, source_target_pairs={{0,4},{4,0},{8,12},{12,8},{16,20},{20,16},{24,28},{28,24},{1,5},{5... | collective-permute-start | bytes 884744 | tf_op jit(solution)/shard_map/ppermute | solution.py:424
  110.0 6.5 %collective-permute-start.22 = (bf16[96,1536]{1,0:T(8,128)(2,1)S(1)}, bf16[96,1536]{1,0:T(8,128)(2,1)S(1)}, u32[]{:S(2)}, u32[]{:S(2)}) collective-permute-start(bf16[96,1536]{1,0:T(8,128)(2,1)S(1)} %collective-permute-done.21), channel_id=1, source_target_pairs={{0,4},{4,0},{8,12},{12,8},{16,20},{20,16},{24,28},{28,24},{1,5},{5... | collective-permute-start | bytes 884744 | tf_op jit(solution)/shard_map/ppermute | solution.py:424
  116.0 1.6 collective-permute-start.24
  116.0 2.0 %collective-permute-start.26 = (bf16[96,1536]{1,0:T(8,128)(2,1)S(1)}, bf16[96,1536]{1,0:T(8,128)(2,1)S(1)}, u32[]{:S(2)}, u32[]{:S(2)}) collective-permute-start(bf16[96,1536]{1,0:T(8,128)(2,1)S(1)} %collective-permute-done.25), channel_id=1, source_target_pairs={{0,4},{4,0},{8,12},{12,8},{16,20},{20,16},{24,28},{28,24},{1,5},{5... | collective-permute-start | bytes 884744 | tf_op jit(solution)/shard_map/ppermute | solution.py:424
  124.2 1.2 copy-start.5
  125.5 30.2 %all-to-all-start = ((bf16[8,96,1152]{2,1,0:T(8,128)(2,1)}), bf16[8,96,1152]{2,1,0:T(8,128)(2,1)S(1)}, u32[]{:S(2)}, u32[]{:S(2)}) async-start(bf16[8,96,1152]{2,1,0:T(8,128)(2,1)} %copy-done.5), calls=%async_computation | async-start | bytes 3538944 | tf_op jit(solution)/shard_map/all_to_all | solution.py:554
  129.2 4.4 %copy-start.34 = (s32[4,16]{1,0:T(4,128)S(1)}, s32[4,16]{1,0:T(4,128)}, u32[]{:S(2)}) copy-start(s32[4,16]{1,0:T(4,128)} %table.3) | copy-start | bytes 772
  129.3 4.4 %copy-start.35 = (s32[4]{0:T(128)S(1)}, s32[4]{0:T(128)}, u32[]{:S(2)}) copy-start(s32[4]{0:T(128)} %all_lengths.3) | copy-start | bytes 52
  129.3 4.4 %copy-start.37 = (s32[4]{0:T(128)S(1)}, s32[4]{0:T(128)}, u32[]{:S(2)}) copy-start(s32[4]{0:T(128)} %get-tuple-element.27.slots) | copy-start | bytes 52
  133.7 3.2 %copy-start = (bf16[40,128,768]{2,1,0:T(8,128)(2,1)S(1)}, bf16[40,128,768]{2,1,0:T(8,128)(2,1)}, u32[]{:S(2)}) copy-start(bf16[40,128,768]{2,1,0:T(8,128)(2,1)} %refs_5_.3) | copy-start | bytes 23592964
  136.9 3.2 %copy-start.2 = (bf16[40,128,768]{2,1,0:T(8,128)(2,1)S(1)}, bf16[40,128,768]{2,1,0:T(8,128)(2,1)}, u32[]{:S(2)}) copy-start(bf16[40,128,768]{2,1,0:T(8,128)(2,1)} %refs_6_.3) | copy-start | bytes 23592964
  151.2 0.8 copy-start.8
  152.0 0.8 copy-start.10
  152.8 0.8 copy-start.12
  155.7 3.2 %copy-start.1 = (bf16[40,128,768]{2,1,0:T(8,128)(2,1)S(1)}, bf16[40,128,768]{2,1,0:T(8,128)(2,1)}, u32[]{:S(2)}) copy-start(bf16[40,128,768]{2,1,0:T(8,128)(2,1)} %refs_5_.3) | copy-start | bytes 23592964
  158.9 3.2 %copy-start.3 = (bf16[40,128,768]{2,1,0:T(8,128)(2,1)S(1)}, bf16[40,128,768]{2,1,0:T(8,128)(2,1)}, u32[]{:S(2)}) copy-start(bf16[40,128,768]{2,1,0:T(8,128)(2,1)} %refs_6_.3) | copy-start | bytes 23592964
  162.1 1.1 copy-start.9
  163.2 1.1 copy-start.11
  164.3 1.1 copy-start.13
  165.3 0.9 copy-start.29
  166.2 0.9 copy-start.31
  167.1 0.9 copy-start.33
  (6 other events, 4.0 us)

commit v5 on v4

--- a/solution.py
+++ b/solution.py
@@ -15,7 +15,7 @@
 LANES = 128
 WINDOW = 2 * LANES
 CHUNK_PAGES = 4
-MIB = 1024 * 1024
+VMEM_LIMIT = 58 * 1024 * 1024
 
 SMEM = pl.BlockSpec(memory_space=pltpu.SMEM)
 VMEM = pl.BlockSpec(memory_space=pltpu.VMEM)
@@ -89,35 +89,19 @@
 
 
 def norm_kernel(depth, chips, place, *refs):
-    pieces = refs[: 2 * depth - 1]
-    gain, bias = refs[2 * depth - 1 : 2 * depth + 1]
-    outs = refs[2 * depth + 1 : 2 * depth + 1 + chips]
-    held, sems = refs[2 * depth + 1 + chips :]
+    pieces = refs[:depth]
+    gain, bias = refs[depth : depth + 2]
+    outs = refs[depth + 2 : depth + 2 + chips]
+    held, sems = refs[depth + 2 + chips :]
     me, chip = place[0], place[1]
-    copies = []
-    for index, piece in enumerate(pieces):
-        if index == 0:
-            offset = 0
-        elif index < depth:
-            offset = -index
-        else:
-            offset = index - depth + 1
-        copies.append((offset, pltpu.make_async_copy(piece, held.at[me + offset], sems.at[index])))
-
-    def inside(offset):
-        return (me + offset >= 0) & (me + offset < depth)
-
-    for offset, copy in copies:
-
-        @pl.when(inside(offset))
-        def _():
-            copy.start()
-
-    for offset, copy in copies:
-
-        @pl.when(inside(offset))
-        def _():
-            copy.wait()
+    copies = [
+        pltpu.make_async_copy(piece, held.at[me ^ distance], sems.at[distance])
+        for distance, piece in enumerate(pieces)
+    ]
+    for copy in copies:
+        copy.start()
+    for copy in copies:
+        copy.wait()
 
     rows, width = held.shape[1], held.shape[2]
     step = 16
@@ -476,21 +460,17 @@
     span = page_table.shape[1]
     pages = span + (half - 1) * (span // 2)
 
-    pieces = [[chunk.reshape(chunk_rows, width)] for chunk in chunks]
-    ends = [(own[0], own[0]) for own in pieces]
-    downs = [[], []]
-    for part in range(2):
-        for hop in range(1, wgt_size):
-            up, down = ends[part]
-            if part == 1 and hop == 1:
-                up = down = after(up, (pieces[0][min(2, wgt_size - 1)], downs[0][min(1, wgt_size - 2)]))
-            up = lax.ppermute(up, "wgt", [(at, at + 1) for at in range(hop - 1, wgt_size - 1)])
-            down = lax.ppermute(down, "wgt", [(at + 1, at) for at in range(wgt_size - hop)])
-            ends[part] = (up, down)
-            pieces[part].append(up)
-            downs[part].append(down)
-
-    rows_held = after(w_qkv, pieces[0][1])
+    pieces = []
+    for chunk in chunks:
+        own = chunk.reshape(chunk_rows, width)
+        if pieces:
+            own = after(own, pieces[0][1])
+        pieces.append([own])
+        for distance in range(1, wgt_size):
+            pairs = [(at, at ^ distance) for at in range(wgt_size)]
+            pieces[-1].append(lax.ppermute(own, "wgt", pairs))
+
+    rows_held = after(w_qkv, chunks[0])
     own_rows = lax.dynamic_slice_in_dim(rows_held, core * half_cols, half_cols, 1)
     other_rows = swap(
         lax.dynamic_slice_in_dim(rows_held, (1 - core) * half_cols, half_cols, 1), 1
@@ -503,25 +483,24 @@
         normed = pl.pallas_call(
             functools.partial(norm_kernel, wgt_size, chips),
             out_shape=[jax.ShapeDtypeStruct((chunk_rows, block), jnp.bfloat16)] * chips,
-            in_specs=[SMEM] + [HBM] * (2 * wgt_size - 1) + [VMEM] * 2,
+            in_specs=[SMEM] + [HBM] * wgt_size + [VMEM] * 2,
             out_specs=[VMEM] * chips,
             scratch_shapes=[
                 pltpu.VMEM((wgt_size, chunk_rows, width), jnp.bfloat16),
-                pltpu.SemaphoreType.DMA((2 * wgt_size - 1,)),
+                pltpu.SemaphoreType.DMA((wgt_size,)),
             ],
-            compiler_params=pltpu.CompilerParams(vmem_limit_bytes=12 * MIB),
+            compiler_params=pltpu.CompilerParams(vmem_limit_bytes=VMEM_LIMIT),
             name="norm",
-        )(where, *pieces[part], *downs[part], gain, shift)
+        )(where, *pieces[part], gain, shift)
 
         tokens = []
         for distance in range(chips):
             mine = normed[distance] if distance == 0 else swap(normed[distance], 2 * distance)
             if part == 0:
-                mine = after(mine, (pieces[1][1], downs[1][0]))
+                mine = after(mine, pieces[1][1])
             tokens += [mine, swap(mine, 1)]
         if part == 0:
-            hop = min(2, wgt_size - 1)
-            tokens[-1] = after(tokens[-1], (pieces[1][hop], downs[1][hop - 1]))
+            tokens[-1] = after(tokens[-1], pieces[1][wgt_size // 2])
 
         partial = pl.pallas_call(
             functools.partial(project_kernel, fresh_len, half, part),
@@ -537,7 +516,7 @@
                 pltpu.SemaphoreType.DMA((2,)),
                 pltpu.SemaphoreType.DMA((req_size // min(req_size, 4),)),
             ],
-            compiler_params=pltpu.CompilerParams(vmem_limit_bytes=20 * MIB),
+            compiler_params=pltpu.CompilerParams(vmem_limit_bytes=VMEM_LIMIT),
             name="project",
         )(
             place,
@@ -573,7 +552,7 @@
                 pltpu.VMEM((pages, page, heads * HEAD), jnp.bfloat16),
                 pltpu.SemaphoreType.DMA((half,)),
             ],
-            compiler_params=pltpu.CompilerParams(vmem_limit_bytes=24 * MIB),
+            compiler_params=pltpu.CompilerParams(vmem_limit_bytes=VMEM_LIMIT),
             name="attend",
         )(*operands, *results)
     return results

time: 190 us -> 161 us (0.85); the launches traced: 187 us -> 160 us
  local copies, waits for them, and re-layouts: 40 us -> 9.43 us
  waiting for transfers between devices: 52.9 us -> 69.2 us
  starting transfers between devices: 38.8 us -> 28.6 us
  Pallas kernels: 49.8 us -> 45.4 us
  other arithmetic: 4.44 us -> 6.74 us
    unnamed x82 -> x44, local copies, waits for them, and re-layouts: 35.8 us -> 5.28 us
    pallas_call x2, Pallas kernels: 28.7 us -> 17.9 us  [per_device(): pl.pallas_call(functools.partial(attend_kernel, (req_size, half, fresh_le...]
    all_to_all x2, waiting for transfers between devices: 0.01 us -> 9.19 us  [per_device(): parts = lax.all_to_all(projected[part], 'req', 0, 0, tiled=True)]
    ppermute x12 -> x6, starting transfers between devices: 22.8 us -> 13.7 us  [per_device(): pieces[-1].append(lax.ppermute(own, 'wgt', pairs))]
    ppermute x12 -> x6, waiting for transfers between devices: 29 us -> 35.1 us  [per_device(): pieces[-1].append(lax.ppermute(own, 'wgt', pairs))]
    pallas_call x2, Pallas kernels: 5.05 us -> 8.42 us  [per_device(): pl.pallas_call(functools.partial(norm_kernel, wgt_size, chips), out_shape...]
    pallas_call x2, Pallas kernels: 12.4 us -> 15.3 us  [per_device(): pl.pallas_call(functools.partial(project_kernel, fresh_len, half, part),...]
  transfers between devices with their start and end apart: 29 -> 23, of which waited for: 14 -> 12; matrix products, arithmetic and copies ran while one was open for 5% -> 5% of each run, Pallas kernels for 12% -> 16%
where the time goes in v5:
time: 161 us; the launch traced here: 160 us
  waiting for transfers between devices  69.2 us (43%)
  Pallas kernels  45.4 us (28%)
  starting transfers between devices  28.6 us (18%)
  local copies, waits for them, and re-layouts  9.43 us (6%)
  other arithmetic  6.74 us (4%)
    ppermute x6, waiting for transfers between devices, per_device(): pieces[-1].append(lax.ppermute(own, 'wgt', pairs))  35.1 us
    ppermute x15, waiting for transfers between devices, swap(): lax.ppermute(value, 'req', [(device, device ^ distance) for device in ran...  24.9 us
    pallas_call x2, Pallas kernels, per_device(): pl.pallas_call(functools.partial(attend_kernel, (req_size, half, fresh_le...  17.9 us
    pallas_call x2, Pallas kernels, per_device(): pl.pallas_call(functools.partial(project_kernel, fresh_len, half, part),...  15.3 us
    ppermute x6, starting transfers between devices, per_device(): pieces[-1].append(lax.ppermute(own, 'wgt', pairs))  13.7 us
    all_to_all x2, waiting for transfers between devices, per_device(): parts = lax.all_to_all(projected[part], 'req', 0, 0, tiled=True)  9.19 us
    pallas_call x2, Pallas kernels, per_device(): pl.pallas_call(functools.partial(norm_kernel, wgt_size, chips), out_shape...  8.42 us
    ppermute x15, starting transfers between devices, swap(): lax.ppermute(value, 'req', [(device, device ^ distance) for device in ran...  7.58 us
  transfers between devices with their start and end apart: 23, of which 12 were waited for; matrix products, arithmetic and copies ran while one was open for 5% of the time, Pallas kernels for 16%

profile of v5, /device:TPU:0, one launch (start us, length us, event | category | flops | bytes accessed | tf_op | source)
XLA Modules:
  0.0 160.3 jit_solution(3167578888115168915)
XLA Ops:
  0.6 3.7 %plan.1 = (s32[4]{0:T(128)}, s32[32]{0:T(128)}, bf16[2,48,1536]{2,1,0:T(8,128)(2,1)}, bf16[2,48,1536]{2,1,0:T(8,128)(2,1)}) custom-call(s32[1]{0:T(128)} %bitcast.place, s32[32]{0:T(128)} %group_of.1, bf16[4,48,1536]{2,1,0:T(8,128)(2,1)} %arrivals.1), custom_call_target="tpu_custom_call" | custom-call | tf_op jit(solution)/shard_map/plan/pallas_call | solution.py:417
  4.3 0.0 copy-start.18
  4.3 3.6 %constant_dynamic-slice_fusion = (bf16[768,1152]{1,0:T(8,128)(2,1)S(1)}, bf16[768,1152]{1,0:T(8,128)(2,1)}) fusion(bf16[768,2304]{1,0:T(8,128)(2,1)} %param.20, s32[]{:T(128)S(6)} %select_n.20, s32[]{:T(128)S(6)} %select_n.19), kind=kLoop, calls=%fused_computation.8 | loop fusion | bytes 7077896 | tf_op jit(solution)/shard_map/dynamic_slice | solution.py:476
  7.9 0.5 collective-permute-start.13
  8.3 2.6 %collective-permute-start = (bf16[96,1536]{1,0:T(8,128)(2,1)}, bf16[96,1536]{1,0:T(8,128)(2,1)}, u32[]{:S(2)}, u32[]{:S(2)}) collective-permute-start(bf16[96,1536]{1,0:T(8,128)(2,1)} %bitcast.5.refs_0_), channel_id=1, source_target_pairs={{0,1},{1,0},{2,3},{3,2},{4,5},{5,4},{6,7},{7,6},{8,9},{9,8},{10,11... | collective-permute-start | bytes 884744 | tf_op jit(solution)/shard_map/ppermute | solution.py:471
  10.9 2.6 %collective-permute-start.4 = (bf16[96,1536]{1,0:T(8,128)(2,1)}, bf16[96,1536]{1,0:T(8,128)(2,1)}, u32[]{:S(2)}, u32[]{:S(2)}) collective-permute-start(bf16[96,1536]{1,0:T(8,128)(2,1)} %bitcast.5.refs_0_), channel_id=1, source_target_pairs={{0,2},{1,3},{2,0},{3,1},{4,6},{5,7},{6,4},{7,5},{8,10},{9,11},{10,... | collective-permute-start | bytes 884744 | tf_op jit(solution)/shard_map/ppermute | solution.py:471
  13.5 0.0 collective-permute-start.5
  13.5 11.3 %collective-permute-done.refs_1_ = bf16[96,1536]{1,0:T(8,128)(2,1)} collective-permute-done((bf16[96,1536]{1,0:T(8,128)(2,1)}, bf16[96,1536]{1,0:T(8,128)(2,1)}, u32[]{:S(2)}, u32[]{:S(2)}) %collective-permute-start) | collective-permute-done | bytes 294944 | tf_op jit(solution)/shard_map/ppermute | solution.py:471
  24.8 0.0 collective-permute-start.1
  24.8 0.6 reshape.164
  25.4 1.3 reshape.166
  26.7 0.7 pad_add_fusion.place
  27.4 7.3 %collective-permute-done.4.refs_2_ = bf16[96,1536]{1,0:T(8,128)(2,1)} collective-permute-done((bf16[96,1536]{1,0:T(8,128)(2,1)}, bf16[96,1536]{1,0:T(8,128)(2,1)}, u32[]{:S(2)}, u32[]{:S(2)}) %collective-permute-start.4) | collective-permute-done | bytes 294944 | tf_op jit(solution)/shard_map/ppermute | solution.py:471
  34.7 0.0 collective-permute-done.5.refs_3_
  34.7 4.2 %norm.2 = (bf16[96,1536]{1,0:T(8,128)(2,1)}, bf16[96,1536]{1,0:T(8,128)(2,1)}, bf16[96,1536]{1,0:T(8,128)(2,1)}, bf16[96,1536]{1,0:T(8,128)(2,1)}) custom-call(s32[2]{0:T(128)} %pad_add_fusion.place, bf16[96,1536]{1,0:T(8,128)(2,1)} %bitcast.5.refs_0_, bf16[96,1536]{1,0:T(8,128)(2,1)} %collective-permute-done.refs_1_, ...), custom_call_target="tpu_custom_call" | custom-call | tf_op jit(solution)/shard_map/norm/pallas_call | solution.py:483
  38.9 1.6 collective-permute-start.7
  40.5 1.5 collective-permute-start.11
  42.0 0.5 collective-permute-start.9
  42.5 0.0 collective-permute-done.1.refs_1_
  42.5 7.2 %collective-permute-start.2 = (bf16[96,1536]{1,0:T(8,128)(2,1)}, bf16[96,1536]{1,0:T(8,128)(2,1)}, u32[]{:S(2)}, u32[]{:S(2)}) collective-permute-start(bf16[96,1536]{1,0:T(8,128)(2,1)} %bitcast.4.refs_0_), channel_id=1, source_target_pairs={{0,2},{1,3},{2,0},{3,1},{4,6},{5,7},{6,4},{7,5},{8,10},{9,11},{10,... | collective-permute-start | bytes 884744 | tf_op jit(solution)/shard_map/ppermute | solution.py:471
  49.7 0.0 collective-permute-done.7
  49.7 0.0 collective-permute-start.6
  49.7 4.7 %collective-permute-done.11 = bf16[96,1536]{1,0:T(8,128)(2,1)S(1)} collective-permute-done((bf16[96,1536]{1,0:T(8,128)(2,1)}, bf16[96,1536]{1,0:T(8,128)(2,1)S(1)}, u32[]{:S(2)}, u32[]{:S(2)}) %collective-permute-start.11) | collective-permute-done | bytes 294944 | tf_op jit(solution)/shard_map/ppermute | solution.py:408
  54.4 1.4 collective-permute-done.9
  55.7 0.0 collective-permute-start.12
  55.7 6.3 %collective-permute-done.2.refs_2_ = bf16[96,1536]{1,0:T(8,128)(2,1)} collective-permute-done((bf16[96,1536]{1,0:T(8,128)(2,1)}, bf16[96,1536]{1,0:T(8,128)(2,1)}, u32[]{:S(2)}, u32[]{:S(2)}) %collective-permute-start.2) | collective-permute-done | bytes 294944 | tf_op jit(solution)/shard_map/ppermute | solution.py:471
  62.1 0.0 collective-permute-done.6
  62.1 0.0 copy-start.9
  62.1 1.5 collective-permute-done.10
  63.7 0.6 copy-done.15
  64.4 0.6 copy-done.2
  65.0 7.7 %project.2 = bf16[8,96,1152]{2,1,0:T(8,128)(2,1)} custom-call(s32[1]{0:T(128)} %bitcast.1.place, s32[32]{0:T(128)} %get-tuple-element.28.source, bf16[2,48,1536]{2,1,0:T(8,128)(2,1)} %bitcast.24, bf16[2,48,1536]{2,1,0:T(8,128)(2,1)} %bitcast.32, bf16[2,48,1536]{2,1,0:T(8,128)(2,1)} %bitcast.25, bf16[2,48,1536]{2,1,0:T(8,128)(2,1)} %bitcast.34, ...), custom_call_target="tpu_custom_call" | custom-call | tf_op jit(solution)/shard_map/project/pallas_call | solution.py:505
  72.7 3.7 %all-to-all-start.1 = ((bf16[8,96,1152]{2,1,0:T(8,128)(2,1)}), bf16[8,96,1152]{2,1,0:T(8,128)(2,1)S(1)}, u32[]{:S(2)}, u32[]{:S(2)}) async-start(bf16[8,96,1152]{2,1,0:T(8,128)(2,1)} %project.2), calls=%async_computation.1 | async-start | bytes 3538944 | tf_op jit(solution)/shard_map/all_to_all | solution.py:533
  76.4 1.4 collective-permute-start.3
  77.8 10.1 %collective-permute-done.3.refs_3_ = bf16[96,1536]{1,0:T(8,128)(2,1)S(1)} collective-permute-done((bf16[96,1536]{1,0:T(8,128)(2,1)}, bf16[96,1536]{1,0:T(8,128)(2,1)S(1)}, u32[]{:S(2)}, u32[]{:S(2)}) %collective-permute-start.3) | collective-permute-done | bytes 294944 | tf_op jit(solution)/shard_map/ppermute | solution.py:471
  87.9 0.7 copy-done.17
  88.6 4.2 %norm.3 = (bf16[96,1536]{1,0:T(8,128)(2,1)}, bf16[96,1536]{1,0:T(8,128)(2,1)}, bf16[96,1536]{1,0:T(8,128)(2,1)}, bf16[96,1536]{1,0:T(8,128)(2,1)}) custom-call(s32[2]{0:T(128)} %pad_add_fusion.place, bf16[96,1536]{1,0:T(8,128)(2,1)} %bitcast.4.refs_0_, bf16[96,1536]{1,0:T(8,128)(2,1)} %collective-permute-done.1.refs_1_, ...), custom_call_target="tpu_custom_call" | custom-call | tf_op jit(solution)/shard_map/norm/pallas_call | solution.py:483
  92.8 1.7 %collective-permute-start.15 = (bf16[96,1536]{1,0:T(8,128)(2,1)}, bf16[96,1536]{1,0:T(8,128)(2,1)S(1)}, u32[]{:S(2)}, u32[]{:S(2)}) collective-permute-start(bf16[96,1536]{1,0:T(8,128)(2,1)} %get-tuple-element.44), channel_id=1, source_target_pairs={{0,8},{4,12},{8,0},{12,4},{16,24},{20,28},{24,16},{28,20},{1,9},{5... | collective-permute-start | bytes 884744 | tf_op jit(solution)/shard_map/ppermute | solution.py:408
  94.6 1.5 collective-permute-start.17
  96.0 0.4 collective-permute-start.19
  96.4 0.0 collective-permute-start.14
  96.4 9.0 %collective-permute-done.15 = bf16[96,1536]{1,0:T(8,128)(2,1)S(1)} collective-permute-done((bf16[96,1536]{1,0:T(8,128)(2,1)}, bf16[96,1536]{1,0:T(8,128)(2,1)S(1)}, u32[]{:S(2)}, u32[]{:S(2)}) %collective-permute-start.15) | collective-permute-done | bytes 294944 | tf_op jit(solution)/shard_map/ppermute | solution.py:408
  105.5 0.8 collective-permute-done.17
  106.3 0.0 collective-permute-start.18
  106.3 5.9 %collective-permute-done.19 = bf16[96,1536]{1,0:T(8,128)(2,1)S(1)} collective-permute-done((bf16[96,1536]{1,0:T(8,128)(2,1)}, bf16[96,1536]{1,0:T(8,128)(2,1)S(1)}, u32[]{:S(2)}, u32[]{:S(2)}) %collective-permute-start.19) | collective-permute-done | bytes 294944 | tf_op jit(solution)/shard_map/ppermute | solution.py:408
  112.2 0.0 collective-permute-start.20
  112.2 0.0 collective-permute-done.14
  112.2 0.0 copy-start.10
  112.3 0.0 collective-permute-done.18
  112.3 1.5 collective-permute-done.20
  113.8 0.7 copy-done.16
  114.5 7.7 %project.3 = bf16[8,96,1152]{2,1,0:T(8,128)(2,1)} custom-call(s32[1]{0:T(128)} %bitcast.1.place, s32[32]{0:T(128)} %get-tuple-element.28.source, bf16[2,48,1536]{2,1,0:T(8,128)(2,1)} %bitcast.26, bf16[2,48,1536]{2,1,0:T(8,128)(2,1)} %bitcast.33, bf16[2,48,1536]{2,1,0:T(8,128)(2,1)} %bitcast.29, bf16[2,48,1536]{2,1,0:T(8,128)(2,1)} %bitcast.35, ...), custom_call_target="tpu_custom_call" | custom-call | tf_op jit(solution)/shard_map/project/pallas_call | solution.py:505
  122.2 0.0 copy-start.19
  122.2 0.0 copy-start.20
  122.2 0.0 copy-start.21
  122.3 1.3 copy-done
  123.5 3.6 %all-to-all-start = ((bf16[8,96,1152]{2,1,0:T(8,128)(2,1)}), bf16[8,96,1152]{2,1,0:T(8,128)(2,1)S(1)}, u32[]{:S(2)}, u32[]{:S(2)}) async-start(bf16[8,96,1152]{2,1,0:T(8,128)(2,1)} %project.3), calls=%async_computation | async-start | bytes 3538944 | tf_op jit(solution)/shard_map/all_to_all | solution.py:533
  127.1 0.6 reshape.169.refs_1_
  127.7 0.1 add_convert_fusion
  127.8 4.1 %fusion = (f32[4,48,768]{2,1,0:T(8,128)}, f32[4,48,768]{2,1,0:T(8,128)}, f32[4,48,768]{2,1,0:T(8,128)}) fusion(f32[768]{0:T(1024)S(1)} %copy-done.21, f32[4,48]{1,0:T(4,128)S(1)} %add_convert_fusion, pred[768]{0:T(1024)(128)(4,1)} %constant.46, pred[768]{0:T(1024)(128)(4,1)} %constant.38.clone, pred[768]{0:T(1024)(128)(4,1)} %constant.37.clone), kind=kLoop, calls=%fused_computation.2 | loop fusion | flops 737280 | bytes 1775616 | tf_op jit(solution)/shard_map/jit(_where)/select_n | solution.py:448
  131.9 9.1 %attend.2 = (bf16[2,48,768]{2,1,0:T(8,128)(2,1)}, bf16[2,48,768]{2,1,0:T(8,128)(2,1)}, bf16[2,48,768]{2,1,0:T(8,128)(2,1)}) custom-call(s32[4]{0:T(128)} %get-tuple-element.27.slots, s32[4]{0:T(128)} %all_lengths.3, s32[4,16]{1,0:T(4,128)} %table.3, bf16[8,96,1152]{2,1,0:T(8,128)(2,1)} %copy-done, f32[1,2304]{1,0:T(1,128)} %reshape.169.refs_1_, ...), custom_call_target="tpu_custom_call" | custom-call | tf_op jit(solution)/shard_map/attend/pallas_call | solution.py:543
  141.0 9.2 %all-to-all-done.refs_0_ = bf16[8,96,1152]{2,1,0:T(8,128)(2,1)S(1)} async-done(((bf16[8,96,1152]{2,1,0:T(8,128)(2,1)}), bf16[8,96,1152]{2,1,0:T(8,128)(2,1)S(1)}, u32[]{:S(2)}, u32[]{:S(2)}) %all-to-all-start) | async-done | bytes 1769504 | tf_op jit(solution)/shard_map/all_to_all | solution.py:533
  150.2 1.3 copy-done.1
  151.4 8.8 %attend.3 = (bf16[4,48,768]{2,1,0:T(8,128)(2,1)}, bf16[4,48,768]{2,1,0:T(8,128)(2,1)}, bf16[4,48,768]{2,1,0:T(8,128)(2,1)}) custom-call(s32[4]{0:T(128)} %get-tuple-element.27.slots, s32[4]{0:T(128)} %all_lengths.3, s32[4,16]{1,0:T(4,128)} %table.3, bf16[8,96,1152]{2,1,0:T(8,128)(2,1)} %copy-done.1, f32[1,2304]{1,0:T(1,128)} %reshape.169.refs_1_, ...), custom_call_target="tpu_custom_call" | custom-call | tf_op jit(solution)/shard_map/attend/pallas_call | solution.py:543
  (40 shorter events, 0.1 us)
Async XLA Ops:
  4.3 20.5 %copy-start.18 = (bf16[6144]{0:T(1024)(128)(2,1)S(1)}, bf16[6144]{0:T(1024)(128)(2,1)}, u32[]{:S(2)}) copy-start(bf16[6144]{0:T(1024)(128)(2,1)} %param.18) | copy-start | bytes 36868
  7.9 55.8 %collective-permute-start.13 = (bf16[768,1152]{1,0:T(8,128)(2,1)S(1)}, bf16[768,1152]{1,0:T(8,128)(2,1)S(1)}, u32[]{:S(2)}, u32[]{:S(2)}) collective-permute-start(bf16[768,1152]{1,0:T(8,128)(2,1)S(1)} %get-tuple-element.51), channel_id=1, source_target_pairs={{0,4},{4,0},{8,12},{12,8},{16,20},{20,16},{24,28},{28,24},{1,5},{5... | collective-permute-start | bytes 5308424 | tf_op jit(solution)/shard_map/ppermute | solution.py:408
  8.3 16.5 %collective-permute-start = (bf16[96,1536]{1,0:T(8,128)(2,1)}, bf16[96,1536]{1,0:T(8,128)(2,1)}, u32[]{:S(2)}, u32[]{:S(2)}) collective-permute-start(bf16[96,1536]{1,0:T(8,128)(2,1)} %bitcast.5.refs_0_), channel_id=1, source_target_pairs={{0,1},{1,0},{2,3},{3,2},{4,5},{5,4},{6,7},{7,6},{8,9},{9,8},{10,11... | collective-permute-start | bytes 884744 | tf_op jit(solution)/shard_map/ppermute | solution.py:471
  10.9 23.8 %collective-permute-start.4 = (bf16[96,1536]{1,0:T(8,128)(2,1)}, bf16[96,1536]{1,0:T(8,128)(2,1)}, u32[]{:S(2)}, u32[]{:S(2)}) collective-permute-start(bf16[96,1536]{1,0:T(8,128)(2,1)} %bitcast.5.refs_0_), channel_id=1, source_target_pairs={{0,2},{1,3},{2,0},{3,1},{4,6},{5,7},{6,4},{7,5},{8,10},{9,11},{10,... | collective-permute-start | bytes 884744 | tf_op jit(solution)/shard_map/ppermute | solution.py:471
  13.5 21.2 %collective-permute-start.5 = (bf16[96,1536]{1,0:T(8,128)(2,1)}, bf16[96,1536]{1,0:T(8,128)(2,1)}, u32[]{:S(2)}, u32[]{:S(2)}) collective-permute-start(bf16[96,1536]{1,0:T(8,128)(2,1)} %bitcast.5.refs_0_), channel_id=1, source_target_pairs={{0,3},{1,2},{2,1},{3,0},{4,7},{5,6},{6,5},{7,4},{8,11},{9,10},{10,... | collective-permute-start | bytes 884744 | tf_op jit(solution)/shard_map/ppermute | solution.py:471
  24.8 17.7 %collective-permute-start.1 = (bf16[96,1536]{1,0:T(8,128)(2,1)}, bf16[96,1536]{1,0:T(8,128)(2,1)}, u32[]{:S(2)}, u32[]{:S(2)}) collective-permute-start(bf16[96,1536]{1,0:T(8,128)(2,1)} %bitcast.4.refs_0_), channel_id=1, source_target_pairs={{0,1},{1,0},{2,3},{3,2},{4,5},{5,4},{6,7},{7,6},{8,9},{9,8},{10,11... | collective-permute-start | bytes 884744 | tf_op jit(solution)/shard_map/ppermute | solution.py:471
  38.9 10.7 %collective-permute-start.7 = (bf16[96,1536]{1,0:T(8,128)(2,1)}, bf16[96,1536]{1,0:T(8,128)(2,1)S(1)}, u32[]{:S(2)}, u32[]{:S(2)}) collective-permute-start(bf16[96,1536]{1,0:T(8,128)(2,1)} %get-tuple-element.34), channel_id=1, source_target_pairs={{0,8},{4,12},{8,0},{12,4},{16,24},{20,28},{24,16},{28,20},{1,9},{5... | collective-permute-start | bytes 884744 | tf_op jit(solution)/shard_map/ppermute | solution.py:408
  40.5 13.9 %collective-permute-start.11 = (bf16[96,1536]{1,0:T(8,128)(2,1)}, bf16[96,1536]{1,0:T(8,128)(2,1)S(1)}, u32[]{:S(2)}, u32[]{:S(2)}) collective-permute-start(bf16[96,1536]{1,0:T(8,128)(2,1)} %get-tuple-element.38), channel_id=1, source_target_pairs={{0,24},{4,28},{8,16},{12,20},{16,8},{20,12},{24,0},{28,4},{1,25},{... | collective-permute-start | bytes 884744 | tf_op jit(solution)/shard_map/ppermute | solution.py:408
  42.0 13.7 %collective-permute-start.9 = (bf16[96,1536]{1,0:T(8,128)(2,1)}, bf16[96,1536]{1,0:T(8,128)(2,1)S(1)}, u32[]{:S(2)}, u32[]{:S(2)}) collective-permute-start(bf16[96,1536]{1,0:T(8,128)(2,1)} %get-tuple-element.36), channel_id=1, source_target_pairs={{0,16},{4,20},{8,24},{12,28},{16,0},{20,4},{24,8},{28,12},{1,17},{... | collective-permute-start | bytes 884744 | tf_op jit(solution)/shard_map/ppermute | solution.py:408
  42.5 19.6 %collective-permute-start.2 = (bf16[96,1536]{1,0:T(8,128)(2,1)}, bf16[96,1536]{1,0:T(8,128)(2,1)}, u32[]{:S(2)}, u32[]{:S(2)}) collective-permute-start(bf16[96,1536]{1,0:T(8,128)(2,1)} %bitcast.4.refs_0_), channel_id=1, source_target_pairs={{0,2},{1,3},{2,0},{3,1},{4,6},{5,7},{6,4},{7,5},{8,10},{9,11},{10,... | collective-permute-start | bytes 884744 | tf_op jit(solution)/shard_map/ppermute | solution.py:471
  49.7 14.0 %copy-start.3 = (bf16[96,1536]{1,0:T(8,128)(2,1)}, bf16[96,1536]{1,0:T(8,128)(2,1)S(1)}, u32[]{:S(2)}) copy-start(bf16[96,1536]{1,0:T(8,128)(2,1)S(1)} %collective-permute-done.7) | copy-start | bytes 884740
  49.7 12.4 %collective-permute-start.6 = (bf16[96,1536]{1,0:T(8,128)(2,1)}, bf16[96,1536]{1,0:T(8,128)(2,1)S(1)}, u32[]{:S(2)}, u32[]{:S(2)}) collective-permute-start(bf16[96,1536]{1,0:T(8,128)(2,1)} %get-tuple-element.33), channel_id=1, source_target_pairs={{0,4},{4,0},{8,12},{12,8},{16,20},{20,16},{24,28},{28,24},{1,5},{5... | collective-permute-start | bytes 884744 | tf_op jit(solution)/shard_map/ppermute | solution.py:408
  54.4 9.3 %copy-start.4 = (bf16[96,1536]{1,0:T(8,128)(2,1)}, bf16[96,1536]{1,0:T(8,128)(2,1)S(1)}, u32[]{:S(2)}) copy-start(bf16[96,1536]{1,0:T(8,128)(2,1)S(1)} %collective-permute-done.11) | copy-start | bytes 884740
  54.4 7.7 %collective-permute-start.8 = (bf16[96,1536]{1,0:T(8,128)(2,1)S(1)}, bf16[96,1536]{1,0:T(8,128)(2,1)S(1)}, u32[]{:S(2)}, u32[]{:S(2)}) collective-permute-start(bf16[96,1536]{1,0:T(8,128)(2,1)S(1)} %collective-permute-done.7), channel_id=1, source_target_pairs={{0,4},{4,0},{8,12},{12,8},{16,20},{20,16},{24,28},{28,24},{1,5},{5... | collective-permute-start | bytes 884744 | tf_op jit(solution)/shard_map/ppermute | solution.py:408
  55.7 7.9 %copy-start.5 = (bf16[96,1536]{1,0:T(8,128)(2,1)}, bf16[96,1536]{1,0:T(8,128)(2,1)S(1)}, u32[]{:S(2)}) copy-start(bf16[96,1536]{1,0:T(8,128)(2,1)S(1)} %collective-permute-done.9) | copy-start | bytes 884740
  55.7 6.3 %collective-permute-start.12 = (bf16[96,1536]{1,0:T(8,128)(2,1)S(1)}, bf16[96,1536]{1,0:T(8,128)(2,1)S(1)}, u32[]{:S(2)}, u32[]{:S(2)}) collective-permute-start(bf16[96,1536]{1,0:T(8,128)(2,1)S(1)} %collective-permute-done.11), channel_id=1, source_target_pairs={{0,4},{4,0},{8,12},{12,8},{16,20},{20,16},{24,28},{28,24},{1,5},{5... | collective-permute-start | bytes 884744 | tf_op jit(solution)/shard_map/ppermute | solution.py:408
  62.1 1.6 collective-permute-start.10
  62.1 1.6 %copy-start.13 = (bf16[96,1536]{1,0:T(8,128)(2,1)}, bf16[96,1536]{1,0:T(8,128)(2,1)S(1)}, u32[]{:S(2)}) copy-start(bf16[96,1536]{1,0:T(8,128)(2,1)S(1)} %collective-permute-done.12) | copy-start | bytes 884740
  62.1 1.6 %copy-start.9 = (bf16[96,1536]{1,0:T(8,128)(2,1)}, bf16[96,1536]{1,0:T(8,128)(2,1)S(1)}, u32[]{:S(2)}) copy-start(bf16[96,1536]{1,0:T(8,128)(2,1)S(1)} %collective-permute-done.6) | copy-start | bytes 884740
  62.1 1.6 copy-start.11
  63.6 0.7 copy-start.15
  63.6 1.3 copy-start.2
  72.7 49.6 %all-to-all-start.1 = ((bf16[8,96,1152]{2,1,0:T(8,128)(2,1)}), bf16[8,96,1152]{2,1,0:T(8,128)(2,1)S(1)}, u32[]{:S(2)}, u32[]{:S(2)}) async-start(bf16[8,96,1152]{2,1,0:T(8,128)(2,1)} %project.2), calls=%async_computation.1 | async-start | bytes 3538944 | tf_op jit(solution)/shard_map/all_to_all | solution.py:533
  76.4 11.5 %collective-permute-start.3 = (bf16[96,1536]{1,0:T(8,128)(2,1)}, bf16[96,1536]{1,0:T(8,128)(2,1)S(1)}, u32[]{:S(2)}, u32[]{:S(2)}) collective-permute-start(bf16[96,1536]{1,0:T(8,128)(2,1)} %bitcast.4.refs_0_), channel_id=1, source_target_pairs={{0,3},{1,2},{2,1},{3,0},{4,7},{5,6},{6,5},{7,4},{8,11},{9,10},{10,... | collective-permute-start | bytes 884744 | tf_op jit(solution)/shard_map/ppermute | solution.py:471
  87.9 0.7 copy-start.17
  92.8 12.6 %collective-permute-start.15 = (bf16[96,1536]{1,0:T(8,128)(2,1)}, bf16[96,1536]{1,0:T(8,128)(2,1)S(1)}, u32[]{:S(2)}, u32[]{:S(2)}) collective-permute-start(bf16[96,1536]{1,0:T(8,128)(2,1)} %get-tuple-element.44), channel_id=1, source_target_pairs={{0,8},{4,12},{8,0},{12,4},{16,24},{20,28},{24,16},{28,20},{1,9},{5... | collective-permute-start | bytes 884744 | tf_op jit(solution)/shard_map/ppermute | solution.py:408
  94.6 11.7 %collective-permute-start.17 = (bf16[96,1536]{1,0:T(8,128)(2,1)}, bf16[96,1536]{1,0:T(8,128)(2,1)S(1)}, u32[]{:S(2)}, u32[]{:S(2)}) collective-permute-start(bf16[96,1536]{1,0:T(8,128)(2,1)} %get-tuple-element.45), channel_id=1, source_target_pairs={{0,16},{4,20},{8,24},{12,28},{16,0},{20,4},{24,8},{28,12},{1,17},{... | collective-permute-start | bytes 884744 | tf_op jit(solution)/shard_map/ppermute | solution.py:408
  96.0 16.2 %collective-permute-start.19 = (bf16[96,1536]{1,0:T(8,128)(2,1)}, bf16[96,1536]{1,0:T(8,128)(2,1)S(1)}, u32[]{:S(2)}, u32[]{:S(2)}) collective-permute-start(bf16[96,1536]{1,0:T(8,128)(2,1)} %get-tuple-element.46), channel_id=1, source_target_pairs={{0,24},{4,28},{8,16},{12,20},{16,8},{20,12},{24,0},{28,4},{1,25},{... | collective-permute-start | bytes 884744 | tf_op jit(solution)/shard_map/ppermute | solution.py:408
  96.4 15.8 %collective-permute-start.14 = (bf16[96,1536]{1,0:T(8,128)(2,1)}, bf16[96,1536]{1,0:T(8,128)(2,1)S(1)}, u32[]{:S(2)}, u32[]{:S(2)}) collective-permute-start(bf16[96,1536]{1,0:T(8,128)(2,1)} %get-tuple-element.43), channel_id=1, source_target_pairs={{0,4},{4,0},{8,12},{12,8},{16,20},{20,16},{24,28},{28,24},{1,5},{5... | collective-permute-start | bytes 884744 | tf_op jit(solution)/shard_map/ppermute | solution.py:408
  105.4 8.4 %copy-start.6 = (bf16[96,1536]{1,0:T(8,128)(2,1)}, bf16[96,1536]{1,0:T(8,128)(2,1)S(1)}, u32[]{:S(2)}) copy-start(bf16[96,1536]{1,0:T(8,128)(2,1)S(1)} %collective-permute-done.15) | copy-start | bytes 884740
  105.4 6.8 %collective-permute-start.16 = (bf16[96,1536]{1,0:T(8,128)(2,1)S(1)}, bf16[96,1536]{1,0:T(8,128)(2,1)S(1)}, u32[]{:S(2)}, u32[]{:S(2)}) collective-permute-start(bf16[96,1536]{1,0:T(8,128)(2,1)S(1)} %collective-permute-done.15), channel_id=1, source_target_pairs={{0,4},{4,0},{8,12},{12,8},{16,20},{20,16},{24,28},{28,24},{1,5},{5... | collective-permute-start | bytes 884744 | tf_op jit(solution)/shard_map/ppermute | solution.py:408
  106.3 7.5 %copy-start.7 = (bf16[96,1536]{1,0:T(8,128)(2,1)}, bf16[96,1536]{1,0:T(8,128)(2,1)S(1)}, u32[]{:S(2)}) copy-start(bf16[96,1536]{1,0:T(8,128)(2,1)S(1)} %collective-permute-done.17) | copy-start | bytes 884740
  106.3 6.0 %collective-permute-start.18 = (bf16[96,1536]{1,0:T(8,128)(2,1)S(1)}, bf16[96,1536]{1,0:T(8,128)(2,1)S(1)}, u32[]{:S(2)}, u32[]{:S(2)}) collective-permute-start(bf16[96,1536]{1,0:T(8,128)(2,1)S(1)} %collective-permute-done.17), channel_id=1, source_target_pairs={{0,4},{4,0},{8,12},{12,8},{16,20},{20,16},{24,28},{28,24},{1,5},{5... | collective-permute-start | bytes 884744 | tf_op jit(solution)/shard_map/ppermute | solution.py:408
  112.2 1.6 copy-start.8
  112.2 1.6 collective-permute-start.20
  112.2 1.6 copy-start.10
  112.2 1.6 copy-start.12
  112.3 1.6 copy-start.14
  113.8 0.7 copy-start.16
  122.2 4.9 %copy-start.19 = (bf16[2304]{0:T(1024)(128)(2,1)S(1)}, bf16[2304]{0:T(1024)(128)(2,1)}, u32[]{:S(2)}) copy-start(bf16[2304]{0:T(1024)(128)(2,1)} %param.21) | copy-start | bytes 13828
  122.2 5.5 %copy-start.20 = (s32[4]{0:T(128)S(1)}, s32[4]{0:T(128)}, u32[]{:S(2)}) copy-start(s32[4]{0:T(128)} %all_lengths.3) | copy-start | bytes 52
  122.2 5.6 %copy-start.21 = (f32[768]{0:T(1024)S(1)}, f32[768]{0:T(1024)}, u32[]{:S(2)}) copy-start(f32[768]{0:T(1024)} %constant.45) | copy-start | bytes 9220
  122.2 1.3 copy-start
  123.5 26.7 %all-to-all-start = ((bf16[8,96,1152]{2,1,0:T(8,128)(2,1)}), bf16[8,96,1152]{2,1,0:T(8,128)(2,1)S(1)}, u32[]{:S(2)}, u32[]{:S(2)}) async-start(bf16[8,96,1152]{2,1,0:T(8,128)(2,1)} %project.3), calls=%async_computation | async-start | bytes 3538944 | tf_op jit(solution)/shard_map/all_to_all | solution.py:533
  150.2 1.3 copy-start.1
